TPU v7x, 512 devices: a whole 4x4x16 slice. The times are simulated.
512 devices in a mesh: band: 64 (over z, x_lo, core), ga: 8 (over x_hi, y).
Axes of the slice: x: 4 (x_hi: 2, x_lo: 2; x = x_hi * 2 + x_lo), y: 4, z: 16, core: 2. Of those that a mesh axis runs over, the one named last changes fastest.
Arguments:
- orbitals: bfloat16 [128, 128, 128, 128], P('band', 'ga'), may hold values from -6 to 6
- owners: int32 [2], replicated, may hold values from 0 to 127
- cutoff: int32 [128, 128], replicated, may hold values from 16 to 64
Outputs:
- exchange_terms: float32 [128, 128, 128, 128], P('band', 'ga')
- owner_terms: bfloat16 [2, 128, 128, 128], P(None, 'ga')
All inputs are finite; a program needn't handle non-finite values.
Results may differ from a plain program's by a relative error of at most 0.012.
Values may be sent and summed in bfloat16 or wider, within the bound.
No kernel may reach another device: no remote copies, remote signals or barrier semaphores. Data moves between devices by JAX's collectives and lax.ppermute only.
A program may use at most 64 MiB of HBM per device.

v0:
```python
import math

import jax
import jax.numpy as jnp
from jax import lax
from jax.sharding import PartitionSpec as P

COULOMB = math.pi / 8
HIGHEST = lax.Precision.HIGHEST


def broadcast(array, axis, root):
    mine = lax.axis_index(axis) == root
    return lax.psum(jnp.where(mine, array, jnp.zeros_like(array)), axis)


def signed_freq(indices, length):
    return jnp.where(indices < length // 2, indices, indices - length)


def symmetric_cutoff(cutoff):
    length = cutoff.shape[0]
    mirror = (length - jnp.arange(length, dtype=jnp.int32)) % length
    mirrored = jnp.take(jnp.take(cutoff, mirror, axis=0), mirror, axis=1)
    return jnp.minimum(cutoff, mirrored)


def coulomb_kernel(limits, first_row):
    length = limits.shape[0]
    rows = limits.shape[1]
    full_range = jnp.arange(length, dtype=jnp.int32)
    freq_full = signed_freq(full_range, length)
    freq_rows = signed_freq(first_row + jnp.arange(rows, dtype=jnp.int32), length)
    squared = (
        freq_full[:, None, None] ** 2
        + freq_rows[None, :, None] ** 2
        + freq_full[None, None, :] ** 2
    ).astype(jnp.float32)
    inside = (jnp.abs(freq_full)[None, None, :] <= limits[:, :, None]) & (squared > 0)
    scale = COULOMB * float(length) ** 1.5
    return jnp.where(inside, scale / jnp.maximum(squared, 1.0), 0.0)


def dft_tables(length):
    indices = jnp.arange(length, dtype=jnp.int32)
    product = indices[:, None] * indices[None, :] % length
    angles = product.astype(jnp.float32) * (2.0 * math.pi / length)
    return (jnp.cos(angles), jnp.sin(angles))


def along_axis(real_part, imag_part, pattern, cosine, sine_table, direction):
    real_cos = jnp.einsum(pattern, real_part, cosine, precision=HIGHEST)
    real_sin = jnp.einsum(pattern, real_part, sine_table, precision=HIGHEST)
    imag_cos = jnp.einsum(pattern, imag_part, cosine, precision=HIGHEST)
    imag_sin = jnp.einsum(pattern, imag_part, sine_table, precision=HIGHEST)
    return (real_cos + direction * imag_sin, imag_cos - direction * real_sin)


def shards(orbitals, owners, cutoff):
    bands = orbitals.shape[0]
    length = orbitals.shape[2]
    steps_count = owners.shape[0]
    rows = length // lax.axis_size("ga")
    first_row = lax.axis_index("ga") * rows
    limits = lax.dynamic_slice_in_dim(symmetric_cutoff(cutoff), first_row, rows, 1)
    kernel = coulomb_kernel(limits, first_row) / float(length) ** 3
    cosine, sine_table = dft_tables(length)
    values = orbitals.astype(jnp.float32)
    roots = owners // bands
    slots = owners % bands
    owner_fields = []
    for step_index in range(steps_count):
        picked = lax.dynamic_index_in_dim(orbitals, slots[step_index], 0, keepdims=False)
        received = broadcast(picked, "band", roots[step_index])
        owner_fields.append(received.astype(jnp.float32))
    exchange_terms = jnp.zeros(values.shape, jnp.float32)
    part_list = []
    for step_index in range(steps_count):
        owner_field = owner_fields[step_index]
        density = values * owner_field[None]
        leading = density.shape[0]
        paired = density.reshape((leading // 2, 2) + density.shape[1:])
        real_part = paired[:, 0]
        imag_part = paired[:, 1]
        real_part, imag_part = along_axis(
            real_part, imag_part, "qxyz,zk->qxyk", cosine, sine_table, 1.0
        )
        real_part, imag_part = along_axis(
            real_part, imag_part, "qxyz,yk->qxkz", cosine, sine_table, 1.0
        )
        first = lax.all_to_all(real_part, "ga", split_axis=2, concat_axis=1, tiled=True)
        second = lax.all_to_all(imag_part, "ga", split_axis=2, concat_axis=1, tiled=True)
        first, second = along_axis(first, second, "qxyz,xk->qkyz", cosine, sine_table, 1.0)
        first = first * kernel
        second = second * kernel
        real_part, imag_part = along_axis(first, second, "qxyz,xk->qkyz", cosine, sine_table, -1.0)
        real_part, imag_part = (
            lax.all_to_all(
                real_part.astype(jnp.bfloat16), "ga", split_axis=1, concat_axis=2, tiled=True
            ).astype(real_part.dtype),
            lax.all_to_all(
                imag_part.astype(jnp.bfloat16), "ga", split_axis=1, concat_axis=2, tiled=True
            ).astype(imag_part.dtype),
        )
        real_part, imag_part = along_axis(
            real_part, imag_part, "qxyz,yk->qxkz", cosine, sine_table, -1.0
        )
        real_part, imag_part = along_axis(
            real_part, imag_part, "qxyz,zk->qxyk", cosine, sine_table, -1.0
        )
        potential = jnp.stack([real_part, imag_part], 1).reshape(density.shape)
        exchange_terms = exchange_terms + potential * owner_field[None]
        part_list.append(jnp.sum(potential * values, axis=0))
    owner_parts = jnp.stack(part_list)
    owner_terms = lax.psum(owner_parts, "band").astype(jnp.bfloat16)
    return (exchange_terms, owner_terms)


def solution(mesh):
    in_specs = (P("band", "ga", None, None), P(), P())
    out_specs = (P("band", "ga", None, None), P(None, "ga", None, None))
    return jax.shard_map(shards, mesh=mesh, in_specs=in_specs, out_specs=out_specs, check_vma=False)
```

profile of v0, /device:TPU:1, one launch (start us, length us, event | category | flops | bytes accessed | tf_op | source)
XLA Modules:
  0.0 865.4 jit_solution(9518066890620308244)
XLA Ops:
  13.9 2.3 select_bitcast_fusion.1
  18.2 443.3 %all-reduce.4.cloned.1.call-done = (bf16[16,128,128]{2,1,0:T(8,128)(2,1)}, bf16[16,128,128]{2,1,0:T(8,128)(2,1)}) async-done(((bf16[16,128,128]{2,1,0:T(8,128)(2,1)}, bf16[16,128,128]{2,1,0:T(8,128)(2,1)}), (bf16[16,128,128]{2,1,0:T(8,128)(2,1)}, bf16[16,128,128]{2,1,0:T(8,128)(2,1)})) %all-reduce.4.cloned.1.call-update) | async-done | bytes 1048592 | tf_op jit(solution)/shard_map/psum | solution.py:14
  471.3 2.3 fusion.108
  476.4 6.4 all-to-all-start.1
  489.4 2.2 convolution_add_fusion.2
  491.6 5.8 all-to-all-done.1
  497.4 5.5 all-to-all-start
  512.6 4.8 all-to-all-done
  517.4 6.2 all-to-all-start.5
  529.0 2.5 fusion.20
  531.5 6.4 all-to-all-done.5
  537.9 5.7 all-to-all-start.4
  551.3 6.8 all-to-all-done.4
  558.0 6.0 all-to-all-start.3
  573.5 6.6 all-to-all-start.2
  584.9 3.9 all-to-all-done.2
  588.8 5.4 all-to-all-start.7
  596.1 2.2 fusion.102
  600.0 3.0 all-to-all-done.7
  603.0 5.5 all-to-all-start.6
  608.6 3.4 fusion.15
  614.4 2.8 all-to-all-done.6
  627.4 2.3 fusion.2
  629.9 228.3 %all-reduce.5 = bf16[2,16,128,128]{3,2,1,0:T(8,128)(2,1)} all-reduce(f32[2,16,128,128]{3,2,1,0:T(8,128)S(1)} %pad_maximum_fusion), channel_id=1, replica_groups=mesh['band'=64,'ga'=8] {'band'}, use_global_device_ids=true, to_apply=%region_4.5 | all-reduce | flops 524288 | bytes 3145728 | tf_op jit(solution)/shard_map/psum | solution.py:115
  (106 shorter events, 75.4 us)
Async XLA Ops:
  7.2 9.1 %copy-start = (s32[128,128]{1,0:T(8,128)S(1)}, s32[128,128]{1,0:T(8,128)}, u32[]{:S(2)}) copy-start(s32[128,128]{1,0:T(8,128)} %param.5) | copy-start | bytes 196612
  7.2 454.2 %all-reduce.4.cloned.1.call-start = ((), (), s32[]{:S(2)}) async-start(), calls=%async_computation.8 | async-start | bytes 2097152 | tf_op jit(solution)/shard_map/psum | solution.py:14
  17.0 447.0 %copy-start.3 = (bf16[2,16,128,128]{3,2,1,0:T(8,128)(2,1)S(1)}, bf16[2,16,128,128]{3,2,1,0:T(8,128)(2,1)}, u32[]{:S(2)}) copy-start(bf16[2,16,128,128]{3,2,1,0:T(8,128)(2,1)} %param.3) | copy-start | bytes 3145732
  462.6 2.2 copy-start.5
  464.1 0.9 copy-start.7
  476.4 21.0 %all-to-all-start.1 = ((f32[1,16,128,128]{3,1,0,2:T(8,128)}), f32[1,16,128,128]{3,1,0,2:T(8,128)}, u32[]{:S(2)}, u32[]{:S(2)}) async-start(f32[1,16,128,128]{3,1,0,2:T(8,128)} %copy.54), calls=%async_computation.1 | async-start | bytes 2097152 | tf_op jit(solution)/shard_map/all_to_all | solution.py:92
  482.8 1.2 copy-start.9
  491.6 11.3 %copy-start.2 = (f32[16,128,128]{2,1,0:T(8,128)S(1)}, f32[16,128,128]{2,1,0:T(8,128)}, u32[]{:S(2)}) copy-start(f32[16,128,128]{2,1,0:T(8,128)} %convolution_add_fusion.2) | copy-start | bytes 3145732
  497.4 20.0 %all-to-all-start = ((f32[1,16,128,128]{3,1,0,2:T(8,128)}), f32[1,16,128,128]{3,1,0,2:T(8,128)}, u32[]{:S(2)}, u32[]{:S(2)}) async-start(f32[1,16,128,128]{3,1,0,2:T(8,128)} %copy.49), calls=%async_computation | async-start | bytes 2097152 | tf_op jit(solution)/shard_map/all_to_all | solution.py:91
  517.4 20.5 %all-to-all-start.5 = ((f32[1,16,128,128]{3,1,0,2:T(8,128)}), f32[1,16,128,128]{3,1,0,2:T(8,128)S(1)}, u32[]{:S(2)}, u32[]{:S(2)}) async-start(f32[1,16,128,128]{3,1,0,2:T(8,128)} %copy.80), calls=%async_computation.5 | async-start | bytes 2097152 | tf_op jit(solution)/shard_map/all_to_all | solution.py:92
  537.9 20.1 %all-to-all-start.4 = ((f32[1,16,128,128]{3,1,0,2:T(8,128)}), f32[1,16,128,128]{3,1,0,2:T(8,128)S(1)}, u32[]{:S(2)}, u32[]{:S(2)}) async-start(f32[1,16,128,128]{3,1,0,2:T(8,128)} %copy.75), calls=%async_computation.4 | async-start | bytes 2097152 | tf_op jit(solution)/shard_map/all_to_all | solution.py:91
  543.6 1.3 copy-start.10
  558.0 15.4 %all-to-all-start.3 = ((bf16[1,128,16,128]{3,2,0,1:T(8,128)(2,1)}), bf16[1,128,16,128]{3,2,0,1:T(8,128)(2,1)}, u32[]{:S(2)}, u32[]{:S(2)}) async-start(bf16[1,128,16,128]{3,2,0,1:T(8,128)(2,1)} %copy.68), calls=%async_computation.3 | async-start | bytes 1048576 | tf_op jit(solution)/shard_map/all_to_all | solution.py:101
  573.5 15.4 %all-to-all-start.2 = ((bf16[1,128,16,128]{3,2,0,1:T(8,128)(2,1)}), bf16[1,128,16,128]{3,2,0,1:T(8,128)(2,1)S(1)}, u32[]{:S(2)}, u32[]{:S(2)}) async-start(bf16[1,128,16,128]{3,2,0,1:T(8,128)(2,1)} %copy.63), calls=%async_computation.2 | async-start | bytes 1048576 | tf_op jit(solution)/shard_map/all_to_all | solution.py:98
  588.8 14.2 %all-to-all-start.7 = ((bf16[1,128,16,128]{3,2,0,1:T(8,128)(2,1)}), bf16[1,128,16,128]{3,2,0,1:T(8,128)(2,1)S(1)}, u32[]{:S(2)}, u32[]{:S(2)}) async-start(bf16[1,128,16,128]{3,2,0,1:T(8,128)(2,1)} %copy.92), calls=%async_computation.7 | async-start | bytes 1048576 | tf_op jit(solution)/shard_map/all_to_all | solution.py:101
  603.0 14.3 %all-to-all-start.6 = ((bf16[1,128,16,128]{3,2,0,1:T(8,128)(2,1)}), bf16[1,128,16,128]{3,2,0,1:T(8,128)(2,1)}, u32[]{:S(2)}, u32[]{:S(2)}) async-start(bf16[1,128,16,128]{3,2,0,1:T(8,128)(2,1)} %copy.87), calls=%async_computation.6 | async-start | bytes 1048576 | tf_op jit(solution)/shard_map/all_to_all | solution.py:98
  624.3 2.5 copy-start.11
  625.5 1.3 copy-start.4
  625.5 1.5 copy-start.6
  625.6 1.8 copy-start.8
  629.7 228.5 %copy-start.1 = (s32[128,128]{1,0:T(8,128)S(1)}, s32[128,128]{1,0:T(8,128)}, u32[]{:S(2)}) copy-start(s32[128,128]{1,0:T(8,128)} %param.5) | copy-start | bytes 196612
Sparse Core Ops, SparseCore 0:
  16.4 444.9 all-reduce.3
where the time goes:
time: 876 us; the launch traced here: 865 us
  waiting for transfers between devices  477 us (54%)
  blocking collectives  228 us (26%)
  matrix products  64.4 us (7%)
  starting transfers between devices  47.4 us (5%)
  between operations  20.5 us (2%)
  local copies, waits for them, and re-layouts  19.1 us (2%)
  other arithmetic  8.98 us (1%)
    psum x1, waiting for transfers between devices, broadcast(): return lax.psum(jnp.where(mine, array, jnp.zeros_like(array)), axis)  443 us
    psum x1, blocking collectives, shards(): owner_terms = lax.psum(owner_parts, 'band').astype(jnp.bfloat16)  228 us
    dot_general x12, matrix products, along_axis(): real_sin = jnp.einsum(pattern, real_part, sine_table, precision=HIGHEST)  18 us
  transfers between devices with their start and end apart: 9, of which 8 were waited for; matrix products, arithmetic and copies ran while one was open for 7% of the time, Pallas kernels for 0%

commit v1 on v0

v1 whole, which is shorter than its diff:
```python
import math

import jax
import jax.numpy as jnp
import numpy as np
from jax import lax
from jax.experimental import pallas as pl
from jax.experimental.pallas import tpu as pltpu
from jax.sharding import Mesh, PartitionSpec as P

COULOMB = math.pi / 8
GRID = 128
STEPS = 2
ROWS = 16
CHUNK = STEPS * ROWS * 2 * ROWS
BF16 = jnp.bfloat16
F32 = jnp.float32

AXES = ("zh", "zl", "xl", "core", "xh", "y")
SIZES = (8, 2, 2, 2, 2, 4)
GA = ("xh", "y")
QUAD = ("zl", "xl")
VMEM = pl.BlockSpec(memory_space=pltpu.VMEM)


def dft_tables():
    indices = np.arange(GRID)
    angles = (indices[:, None] * indices[None, :] % GRID) * (2.0 * np.pi / GRID)
    cosine, sine = np.cos(angles), np.sin(angles)
    matrix = np.block([[cosine, -sine], [sine, cosine]]).astype(np.float32)
    high = matrix.astype(BF16)
    low = (matrix - high.astype(np.float32)).astype(BF16)
    return np.stack([high, low, high.T, low.T])


def dot(a, b):
    return jnp.dot(a, b, preferred_element_type=F32)


def split(x):
    high = x.astype(BF16)
    return high, (x - high.astype(F32)).astype(BF16)


def right(x, tables, which):
    high, low = split(x)
    return dot(high, tables[which]) + (dot(low, tables[which]) + dot(high, tables[which + 1]))


def left(x, tables, which):
    high, low = split(x)
    return dot(tables[which], high) + (dot(tables[which], low) + dot(tables[which + 1], high))


def left_exact(x, tables, which):
    return dot(tables[which], x) + dot(tables[which + 1], x)


def quarter_swap(x):
    n = GRID
    return jnp.concatenate(
        [
            jnp.concatenate([x[:n, :n], x[n:, :n]], axis=1),
            jnp.concatenate([x[:n, n:], x[n:, n:]], axis=1),
        ],
        axis=0,
    )


def forward_kernel(values, owner, tables, out, scratch):
    n = GRID
    for s in range(STEPS):

        def planes(p, carry):
            field = owner[p // 4, p % 4, :, s].reshape(2 * n, n).astype(F32)
            first = values[0, pl.ds(2 * p, 2)].reshape(2 * n, n).astype(F32)
            second = values[1, pl.ds(2 * p, 2)].reshape(2 * n, n).astype(F32)
            density = jnp.concatenate([first * field, second * field], axis=1)
            along_z = quarter_swap(right(density, tables, 0))
            along_y = left(along_z, tables, 2)
            start = pl.multiple_of(2 * p * n, 2 * n)
            for part in range(2):
                rows = along_y[part * n : (part + 1) * n]
                scratch[2 * s + part, pl.ds(start, n), :] = rows[:, :n]
                scratch[2 * s + part, pl.ds(start + n, n), :] = rows[:, n:]
            return carry

        lax.fori_loop(0, ROWS // 2, planes, 0)

    lane = lax.broadcasted_iota(jnp.int32, (ROWS, n), 1)

    def send(j, carry):
        rest = jnp.zeros((ROWS, n), F32)
        for s in range(STEPS):
            for k in range(ROWS):
                for part in range(2):
                    field = 2 * s + part
                    tile = scratch[field, pl.ds(j * ROWS + k, ROWS, stride=n), :]
                    high = tile.astype(BF16)
                    row = ((s * ROWS + k) * 2 + part) * ROWS
                    out[j, row : row + ROWS] = high
                    if k == 0:
                        low = tile - high.astype(F32)
                        below = low - low.astype(BF16).astype(F32)
                        rest = jnp.where(lane == field, low[:, :1], rest)
                        rest = jnp.where(lane == field + 2 * STEPS, below[:, :1], rest)
        out[j, CHUNK:] = rest.astype(BF16)
        return carry

    lax.fori_loop(0, n // ROWS, send, 0)


def solve_kernel(spectrum, coulomb, tables, out, scratch):
    n = GRID
    rest = spectrum[:, CHUNK:].reshape(n, n).astype(F32)
    lane = lax.broadcasted_iota(jnp.int32, (n, n), 1)
    dropped = coulomb[0, :1, :1] == 0.0
    for s in range(STEPS):

        def pick(k):
            row = pl.multiple_of((s * ROWS + k) * 2 * ROWS, 2 * ROWS)
            return [spectrum[:, pl.ds(row + part * ROWS, ROWS)].reshape(n, n) for part in range(2)]

        def factor(q):
            pair = jnp.concatenate([coulomb[2 * q], coulomb[2 * q + 1]], axis=1)
            return jnp.concatenate([pair, pair], axis=0)

        def keep(q, solved):
            start = pl.multiple_of(q * 4 * n, 4 * n)
            scratch[pl.ds(start, 2 * n), :] = solved[:, :n]
            scratch[pl.ds(start + 2 * n, 2 * n), :] = solved[:, n:]

        def columns(q, carry):
            both = jnp.concatenate(
                [jnp.concatenate(pick(2 * q), axis=0), jnp.concatenate(pick(2 * q + 1), axis=0)],
                axis=1,
            )
            keep(q, left(left_exact(both, tables, 2) * factor(q), tables, 0))
            return carry

        parts = []
        for part, tile in enumerate(pick(0)):
            tile, field = tile.astype(F32), 2 * s + part
            low = rest[:, field : field + 1] + rest[:, field + 2 * STEPS : field + 2 * STEPS + 1]
            column = tile[:, :1] + low
            mean = jnp.sum(column, axis=0, keepdims=True) * (1.0 / n)
            column = column - jnp.where(dropped, mean, 0.0)
            parts.append(jnp.where(lane == 0, column, tile))
        both = jnp.concatenate(
            [jnp.concatenate(parts, axis=0), jnp.concatenate(pick(1), axis=0).astype(F32)], axis=1
        )
        keep(0, left(left(both, tables, 2) * factor(0), tables, 0))
        lax.fori_loop(1, ROWS // 2, columns, 0)

        def send(i, carry):
            for x in range(ROWS):
                for part in range(2):
                    tile = scratch[pl.ds(part * n + i * ROWS + x, ROWS, stride=2 * n), :]
                    out[i, s, x, part] = tile.astype(BF16)
            return carry

        lax.fori_loop(0, n // ROWS, send, 0)


def backward_kernel(solved, values, owner, tables, exchange, terms):
    n = GRID

    def planes(p, carry):
        first = values[0, pl.ds(2 * p, 2)].reshape(2 * n, n).astype(F32)
        second = values[1, pl.ds(2 * p, 2)].reshape(2 * n, n).astype(F32)
        totals = [0.0, 0.0]
        for s in range(STEPS):

            def pick(x):
                return jnp.concatenate(
                    [solved[:, s, x, part].reshape(n, n) for part in range(2)], axis=0
                )

            both = jnp.concatenate([pick(2 * p), pick(2 * p + 1)], axis=1)
            along_y = quarter_swap(left_exact(both, tables, 0))
            potential = right(along_y, tables, 2)
            field = owner[p // 4, p % 4, :, s].reshape(2 * n, n).astype(F32)
            real, imag = potential[:, :n], potential[:, n:]
            totals = [totals[0] + real * field, totals[1] + imag * field]
            term = real * first + imag * second
            terms[p // 4, p % 4, :, s] = term.astype(BF16).reshape(8, 32, n)
        for band in range(2):
            exchange[band, pl.ds(2 * p, 2)] = totals[band].reshape(2, n, n)
        return carry

    lax.fori_loop(0, ROWS // 2, planes, 0)


def call(kernel, outs, scratch, flops):
    return pl.pallas_call(
        kernel,
        out_shape=outs,
        scratch_shapes=scratch,
        compiler_params=pltpu.CompilerParams(vmem_limit_bytes=40 * 1024 * 1024),
        cost_estimate=pl.CostEstimate(flops=flops, bytes_accessed=5 << 20, transcendentals=0),
    )


def exchange_all(x, axes):
    return lax.all_to_all(x, axes, 0, 0, tiled=True)


def gather_all(x, axes, count):
    return exchange_all(jnp.broadcast_to(x[None], (count,) + x.shape), axes)


def pick_source(x, sources):
    return jnp.stack(
        [lax.dynamic_index_in_dim(x[:, s], sources[s], 0, keepdims=False) for s in range(STEPS)]
    )


def spread_owners(orbitals, owners):
    slots, roots = owners % 2, owners // 2
    core, quad, zh = roots % 2, roots // 2 % 4, roots // 8
    rows = ROWS * GRID
    flat = orbitals.reshape(2, rows, GRID)
    picked = pick_source(jnp.stack([flat, flat], 1), slots)
    piece = picked.reshape(STEPS, 2, rows // 2, GRID).swapaxes(0, 1)
    piece = pick_source(exchange_all(piece, "core"), core)
    piece = piece.reshape(STEPS, 4, rows // 8, GRID).swapaxes(0, 1)
    piece = pick_source(exchange_all(piece, QUAD), quad)
    piece = piece.reshape(STEPS, 8, rows // 64, GRID).swapaxes(0, 1)
    piece = pick_source(exchange_all(piece, "zh"), zh)
    piece = gather_all(piece, "zh", 8)
    piece = gather_all(piece, QUAD, 4)
    return lax.all_gather(piece, "core", axis=0, tiled=False)


def total_terms(terms):
    def reduced(x):
        return jnp.sum(x.astype(F32), axis=0).astype(BF16)

    piece = reduced(exchange_all(terms, "core"))
    piece = reduced(exchange_all(piece, QUAD))
    piece = reduced(exchange_all(piece, "zh"))
    piece = gather_all(piece, "zh", 8)
    piece = gather_all(piece, QUAD, 4)
    return lax.all_gather(piece, "core", axis=0, tiled=False)


def coulomb_slab(cutoff, first_row):
    mirrored = jnp.roll(cutoff[::-1, ::-1], (1, 1), (0, 1))
    limits = lax.dynamic_slice_in_dim(jnp.minimum(cutoff, mirrored), first_row, ROWS, 1).T
    full = jnp.arange(GRID, dtype=jnp.int32)
    signed = jnp.where(full < GRID // 2, full, full - GRID)
    own = first_row + jnp.arange(ROWS, dtype=jnp.int32)
    own = jnp.where(own < GRID // 2, own, own - GRID)
    squared = own[:, None, None] ** 2 + signed[None, :, None] ** 2 + signed[None, None, :] ** 2
    inside = (jnp.abs(signed)[None, None, :] <= limits[:, :, None]) & (squared > 0)
    scale = COULOMB * float(GRID) ** 1.5 / float(GRID) ** 3
    return jnp.where(inside, scale / jnp.maximum(squared, 1).astype(F32), 0.0)


def shards(orbitals, owners, cutoff):
    first_row = lax.axis_index(GA) * ROWS
    coulomb = coulomb_slab(cutoff, first_row)
    tables = jnp.asarray(dft_tables())
    owner = spread_owners(orbitals, owners)
    packed = jax.ShapeDtypeStruct((8, STEPS, ROWS, 2, ROWS, GRID), BF16)
    flops = 2 * 2 * STEPS * 3 * 8 * 256**3
    with jax.named_scope("forward_planes"):
        spectrum = call(
            forward_kernel,
            jax.ShapeDtypeStruct((8, CHUNK + ROWS, GRID), BF16),
            [pltpu.VMEM((2 * STEPS, ROWS * GRID, GRID), F32)],
            flops,
        )(orbitals, owner, tables)
    spectrum = exchange_all(spectrum, GA)
    with jax.named_scope("coulomb_solve"):
        solved = call(solve_kernel, packed, [pltpu.VMEM((ROWS * 2 * GRID, GRID), F32)], flops)(
            spectrum, coulomb, tables
        )
    solved = exchange_all(solved, GA)
    with jax.named_scope("backward_planes"):
        exchange, terms = call(
            backward_kernel,
            (
                jax.ShapeDtypeStruct((2, ROWS, GRID, GRID), F32),
                jax.ShapeDtypeStruct((2, 4, 8, STEPS, 32, GRID), BF16),
            ),
            [],
            flops,
        )(solved, orbitals, owner, tables)
    total = total_terms(terms)
    total = jnp.moveaxis(total, 3, 0).reshape(STEPS, ROWS, GRID, GRID)
    return exchange, total


def solution(mesh):
    inner = Mesh(mesh.devices.reshape(SIZES), AXES)
    band, ga = AXES[:4], AXES[4:]
    return jax.shard_map(
        shards,
        mesh=inner,
        in_specs=(P(band, ga, None, None), P(), P()),
        out_specs=(P(band, ga, None, None), P(None, ga, None, None)),
        check_vma=False,
    )
```

time: 876 us -> 305 us (0.35); the launches traced: 865 us -> 304 us
  waiting for transfers between devices: 477 us -> 70.8 us
  blocking collectives: 228 us -> 126 us
  matrix products: 64.4 us -> 0 us
  Pallas kernels: 0 us -> 34.2 us
  starting transfers between devices: 47.4 us -> 29 us
  between operations: 20.5 us -> 29.8 us
    psum x1 -> x0, waiting for transfers between devices: 443 us -> none  [broadcast(): return lax.psum(jnp.where(mine, array, jnp.zeros_like(array)), axis)]
    psum x1 -> x0, blocking collectives: 228 us -> none  [shards(): owner_terms = lax.psum(owner_parts, 'band').astype(jnp.bfloat16)]
    all_to_all x0 -> x8, blocking collectives: none -> 126 us  [exchange_all(): return lax.all_to_all(x, axes, 0, 0, tiled=True)]
    dot_general x48 -> x0, matrix products: 64.4 us -> none  [the longest x12 18 us: along_axis(): real_sin = jnp.einsum(pattern, real_part, sine_table, precision=HIGHEST)]
    pallas_call x0 -> x3, Pallas kernels: none -> 34.2 us  [the longest x1 13.4 us: shards(): call(forward_kernel, jax.ShapeDtypeStruct((8, CHUNK + ROWS, GRID), BF16),...]
    all_gather x0 -> x2, waiting for transfers between devices: none -> 31.1 us  [the longest x1 17.2 us: spread_owners(): return lax.all_gather(piece, 'core', axis=0, tiled=False)]
    all_to_all x8 -> x4, starting transfers between devices: 47.4 us -> 28.9 us  [exchange_all(): return lax.all_to_all(x, axes, 0, 0, tiled=True)]
    all_to_all x8 -> x4, waiting for transfers between devices: 33.5 us -> 39.6 us  [exchange_all(): return lax.all_to_all(x, axes, 0, 0, tiled=True)]
  transfers between devices with their start and end apart: 9 -> 6, of which waited for: 8 -> 5; matrix products, arithmetic and copies ran while one was open for 7% -> 1% of each run, Pallas kernels for 0% -> 0%
where the time goes in v1:
time: 305 us; the launch traced here: 304 us
  blocking collectives  126 us (41%)
  waiting for transfers between devices  70.8 us (23%)
  Pallas kernels  34.2 us (11%)
  between operations  29.8 us (10%)
  starting transfers between devices  29 us (10%)
  local copies, waits for them, and re-layouts  11.1 us (4%)
  other arithmetic  3.59 us (1%)
    all_to_all x8, blocking collectives, exchange_all(): return lax.all_to_all(x, axes, 0, 0, tiled=True)  126 us
    all_to_all x4, waiting for transfers between devices, exchange_all(): return lax.all_to_all(x, axes, 0, 0, tiled=True)  39.6 us
    all_to_all x4, starting transfers between devices, exchange_all(): return lax.all_to_all(x, axes, 0, 0, tiled=True)  28.9 us
    all_gather x1, waiting for transfers between devices, spread_owners(): return lax.all_gather(piece, 'core', axis=0, tiled=False)  17.2 us
    all_gather x1, waiting for transfers between devices, total_terms(): return lax.all_gather(piece, 'core', axis=0, tiled=False)  13.9 us
    pallas_call x1, Pallas kernels, shards(): call(forward_kernel, jax.ShapeDtypeStruct((8, CHUNK + ROWS, GRID), BF16),...  13.4 us
    pallas_call x1, Pallas kernels, shards(): call(solve_kernel, packed, [pltpu.VMEM((ROWS * 2 * GRID, GRID), F32)], fl...  12.4 us
    pallas_call x1, Pallas kernels, shards(): call(backward_kernel, (jax.ShapeDtypeStruct((2, ROWS, GRID, GRID), F32),...  8.39 us
  transfers between devices with their start and end apart: 6, of which 5 were waited for; matrix products, arithmetic and copies ran while one was open for 1% of the time, Pallas kernels for 0%

profile of v1, /device:TPU:1, one launch (start us, length us, event | category | flops | bytes accessed | tf_op | source)
XLA Modules:
  0.0 304.4 jit_solution(13658246338298175461)
XLA Ops:
  12.4 1.3 constant_dynamic-slice_fusion.5
  14.8 10.4 %all-to-all-start = ((bf16[2,2,1024,128]{3,2,1,0:T(8,128)(2,1)}), bf16[2,2,1024,128]{3,2,1,0:T(8,128)(2,1)S(1)}, u32[]{:S(2)}, u32[]{:S(2)}) async-start(bf16[2,2,1024,128]{3,2,1,0:T(8,128)(2,1)} %copy.19), calls=%async_computation | async-start | bytes 2097152 | tf_op jit(solution)/shard_map/all_to_all | solution.py:205
  30.7 3.5 %all-to-all-start.1 = ((bf16[4,2,256,128]{3,2,1,0:T(8,128)(2,1)}), bf16[4,2,256,128]{3,2,1,0:T(8,128)(2,1)S(1)}, u32[]{:S(2)}, u32[]{:S(2)}) async-start(bf16[4,2,256,128]{3,2,1,0:T(8,128)(2,1)} %maximum_bitcast_fusion), calls=%async_computation.1 | async-start | bytes 1048576 | tf_op jit(solution)/shard_map/all_to_all | solution.py:205
  38.2 4.1 %all-to-all-done.1 = bf16[4,2,256,128]{3,2,1,0:T(8,128)(2,1)S(1)} async-done(((bf16[4,2,256,128]{3,2,1,0:T(8,128)(2,1)}), bf16[4,2,256,128]{3,2,1,0:T(8,128)(2,1)S(1)}, u32[]{:S(2)}, u32[]{:S(2)}) %all-to-all-start.1) | async-done | bytes 524320 | tf_op jit(solution)/shard_map/all_to_all | solution.py:205
  43.1 9.4 %all-to-all-start.2 = ((bf16[8,2,32,128]{3,2,1,0:T(8,128)(2,1)}), bf16[8,2,32,128]{3,2,1,0:T(8,128)(2,1)S(1)}, u32[]{:S(2)}, u32[]{:S(2)}) async-start(bf16[8,2,32,128]{3,2,1,0:T(8,128)(2,1)} %maximum_bitcast_fusion.1), calls=%async_computation.2 | async-start | bytes 262144 | tf_op jit(solution)/shard_map/all_to_all | solution.py:205
  56.2 10.3 %all-to-all-done.2 = bf16[8,2,32,128]{3,2,1,0:T(8,128)(2,1)S(1)} async-done(((bf16[8,2,32,128]{3,2,1,0:T(8,128)(2,1)}), bf16[8,2,32,128]{3,2,1,0:T(8,128)(2,1)S(1)}, u32[]{:S(2)}, u32[]{:S(2)}) %all-to-all-start.2) | async-done | bytes 131104 | tf_op jit(solution)/shard_map/all_to_all | solution.py:205
  66.6 17.4 %all_to_all.60 = bf16[8,2,32,128]{3,2,1,0:T(8,128)(2,1)S(1)} all-to-all(bf16[8,2,32,128]{3,2,1,0:T(8,128)(2,1)S(1)} %broadcast_in_dim.12), channel_id=1, replica_groups=mesh['zh'=8,'zl'=2,'xl'=2,'core'=2,'xh'=2,'y'=4] {'zh'}, dimensions={0} | all-to-all | bytes 262144 | tf_op jit(solution)/shard_map/all_to_all | solution.py:205
  84.1 9.1 %all_to_all.61 = bf16[4,8,2,32,128]{4,3,2,1,0:T(8,128)(2,1)} all-to-all(bf16[4,8,2,32,128]{4,3,2,1,0:T(8,128)(2,1)S(1)} %broadcast_in_dim.13), channel_id=1, replica_groups=mesh['zh'=8,'zl'=2,'xl'=2,'core'=2,'xh'=2,'y'=4] {'zl','xl'}, dimensions={0} | all-to-all | bytes 1048576 | tf_op jit(solution)/shard_map/all_to_all | solution.py:205
  93.2 17.2 %all-gather.5.cloned.1.call-done = bf16[8,8,2,32,128]{4,3,2,1,0:T(8,128)(2,1)} async-done(((bf16[4,8,2,32,128]{4,3,2,1,0:T(8,128)(2,1)}), bf16[8,8,2,32,128]{4,3,2,1,0:T(8,128)(2,1)}) %all-gather.5.cloned.1.call-update) | async-done | bytes 1048592 | tf_op jit(solution)/shard_map/all_gather | solution.py:232
  110.5 1.2 copy-done.3
  111.7 13.4 %forward_planes.1 = bf16[8,1040,128]{2,1,0:T(8,128)(2,1)S(1)} custom-call(bf16[2,16,128,128]{3,2,1,0:T(8,128)(2,1)S(1)} %copy-done.1, bf16[2,4,8,2,32,128]{5,4,3,2,1,0:T(8,128)(2,1)S(1)} %bitcast.32, bf16[4,256,256]{2,1,0:T(8,128)(2,1)S(1)} %copy-done.5), custom_call_target="tpu_custom_call" | custom-call | flops 3221225472 | bytes 5242880 | tf_op jit(solution)/shard_map/forward_planes/pallas_call | solution.py:268
  125.2 1.3 copy-done
  126.5 5.6 %all-to-all-start.5 = ((bf16[8,1040,128]{2,1,0:T(8,128)(2,1)}), bf16[8,1040,128]{2,1,0:T(8,128)(2,1)S(1)}, u32[]{:S(2)}, u32[]{:S(2)}) async-start(bf16[8,1040,128]{2,1,0:T(8,128)(2,1)} %copy-done), calls=%async_computation.5 | async-start | bytes 4259840 | tf_op jit(solution)/shard_map/all_to_all | solution.py:205
  133.4 25.2 %all-to-all-done.5.spectrum = bf16[8,1040,128]{2,1,0:T(8,128)(2,1)S(1)} async-done(((bf16[8,1040,128]{2,1,0:T(8,128)(2,1)}), bf16[8,1040,128]{2,1,0:T(8,128)(2,1)S(1)}, u32[]{:S(2)}, u32[]{:S(2)}) %all-to-all-start.5) | async-done | bytes 2129952 | tf_op jit(solution)/shard_map/all_to_all | solution.py:205
  159.7 12.4 %coulomb_solve.1 = bf16[8,2,16,2,16,128]{5,4,3,2,1,0:T(8,128)(2,1)S(1)} custom-call(bf16[8,1040,128]{2,1,0:T(8,128)(2,1)S(1)} %all-to-all-done.5.spectrum, f32[16,128,128]{2,1,0:T(8,128)S(1)} %fusion.2.coulomb, bf16[4,256,256]{2,1,0:T(8,128)(2,1)S(1)} %copy-done.6), custom_call_target="tpu_custom_call" | custom-call | flops 3221225472 | bytes 5242880 | tf_op jit(solution)/shard_map/coulomb_solve/pallas_call | solution.py:276
  172.1 32.0 %all_to_all.62.solved = bf16[8,2,16,2,16,128]{5,4,3,2,1,0:T(8,128)(2,1)S(1)} all-to-all(bf16[8,2,16,2,16,128]{5,4,3,2,1,0:T(8,128)(2,1)S(1)} %coulomb_solve.1), channel_id=1, replica_groups=mesh['zh'=8,'zl'=2,'xl'=2,'core'=2,'xh'=2,'y'=4] {'xh','y'}, dimensions={0} | all-to-all | bytes 4194304 | tf_op jit(solution)/shard_map/all_to_all | solution.py:205
  204.1 8.4 %backward_planes.1 = (f32[2,16,128,128]{3,2,1,0:T(8,128)}, bf16[2,4,8,2,32,128]{5,4,3,2,1,0:T(8,128)(2,1)S(1)}) custom-call(bf16[8,2,16,2,16,128]{5,4,3,2,1,0:T(8,128)(2,1)S(1)} %all_to_all.62.solved, bf16[2,16,128,128]{3,2,1,0:T(8,128)(2,1)S(1)} %copy-done.2, bf16[2,4,8,2,32,128]{5,4,3,2,1,0:T(8,128)(2,1)S(1)} %bitcast.33, bf16[4,256,256]{2,1,0:T(8,128)(2,1)S(1)} %copy-done.7), custom_call_target="tpu_custom_call" | custom-call | flops 3221225472 | bytes 5242880 | tf_op jit(solution)/shard_map/backward_planes/pallas_call | solution.py:281
  212.5 6.6 %all_to_all.63 = bf16[2,4,8,2,32,128]{5,4,3,2,1,0:T(8,128)(2,1)S(1)} all-to-all(bf16[2,4,8,2,32,128]{5,4,3,2,1,0:T(8,128)(2,1)S(1)} %get-tuple-element.5), channel_id=1, replica_groups=mesh['zh'=8,'zl'=2,'xl'=2,'core'=2,'xh'=2,'y'=4] {'core'}, dimensions={0} | all-to-all | bytes 2097152 | tf_op jit(solution)/shard_map/all_to_all | solution.py:205
  219.4 10.0 %all_to_all.64 = bf16[4,8,2,32,128]{4,3,2,1,0:T(8,128)(2,1)S(1)} all-to-all(bf16[4,8,2,32,128]{4,3,2,1,0:T(8,128)(2,1)S(1)} %reduce_sum.36), channel_id=1, replica_groups=mesh['zh'=8,'zl'=2,'xl'=2,'core'=2,'xh'=2,'y'=4] {'zl','xl'}, dimensions={0} | all-to-all | bytes 1048576 | tf_op jit(solution)/shard_map/all_to_all | solution.py:205
  229.5 25.4 %all_to_all.65 = bf16[8,2,32,128]{3,2,1,0:T(8,128)(2,1)S(1)} all-to-all(bf16[8,2,32,128]{3,2,1,0:T(8,128)(2,1)S(1)} %reduce_sum.37), channel_id=1, replica_groups=mesh['zh'=8,'zl'=2,'xl'=2,'core'=2,'xh'=2,'y'=4] {'zh'}, dimensions={0} | all-to-all | bytes 262144 | tf_op jit(solution)/shard_map/all_to_all | solution.py:205
  255.0 17.0 %all_to_all.66 = bf16[8,2,32,128]{3,2,1,0:T(8,128)(2,1)S(1)} all-to-all(bf16[8,2,32,128]{3,2,1,0:T(8,128)(2,1)S(1)} %broadcast_in_dim.15), channel_id=1, replica_groups=mesh['zh'=8,'zl'=2,'xl'=2,'core'=2,'xh'=2,'y'=4] {'zh'}, dimensions={0} | all-to-all | bytes 262144 | tf_op jit(solution)/shard_map/all_to_all | solution.py:205
  272.0 8.4 %all_to_all.67 = bf16[4,8,2,32,128]{4,3,1,2,0:T(8,128)(2,1)S(1)} all-to-all(bf16[4,8,2,32,128]{4,3,1,2,0:T(8,128)(2,1)S(1)} %broadcast_in_dim.16), channel_id=1, replica_groups=mesh['zh'=8,'zl'=2,'xl'=2,'core'=2,'xh'=2,'y'=4] {'zl','xl'}, dimensions={0} | all-to-all | bytes 1048576 | tf_op jit(solution)/shard_map/all_to_all | solution.py:205
  281.3 13.9 %all-gather.7.cloned.1.call-done = bf16[8,8,2,32,128]{4,3,2,1,0:T(8,128)(2,1)} async-done(((bf16[4,8,2,32,128]{4,3,2,1,0:T(8,128)(2,1)}), bf16[8,8,2,32,128]{4,3,2,1,0:T(8,128)(2,1)}) %all-gather.7.cloned.1.call-update) | async-done | bytes 1048592 | tf_op jit(solution)/shard_map/all_gather | solution.py:244
  295.2 2.3 copy.23
  (61 shorter events, 8.7 us)
Async XLA Ops:
  14.8 14.2 %all-to-all-start = ((bf16[2,2,1024,128]{3,2,1,0:T(8,128)(2,1)}), bf16[2,2,1024,128]{3,2,1,0:T(8,128)(2,1)S(1)}, u32[]{:S(2)}, u32[]{:S(2)}) async-start(bf16[2,2,1024,128]{3,2,1,0:T(8,128)(2,1)} %copy.19), calls=%async_computation | async-start | bytes 2097152 | tf_op jit(solution)/shard_map/all_to_all | solution.py:205
  30.7 11.6 %all-to-all-start.1 = ((bf16[4,2,256,128]{3,2,1,0:T(8,128)(2,1)}), bf16[4,2,256,128]{3,2,1,0:T(8,128)(2,1)S(1)}, u32[]{:S(2)}, u32[]{:S(2)}) async-start(bf16[4,2,256,128]{3,2,1,0:T(8,128)(2,1)} %maximum_bitcast_fusion), calls=%async_computation.1 | async-start | bytes 1048576 | tf_op jit(solution)/shard_map/all_to_all | solution.py:205
  42.3 68.1 %copy-start.1 = (bf16[2,16,128,128]{3,2,1,0:T(8,128)(2,1)S(1)}, bf16[2,16,128,128]{3,2,1,0:T(8,128)(2,1)}, u32[]{:S(2)}) copy-start(bf16[2,16,128,128]{3,2,1,0:T(8,128)(2,1)} %values.3) | copy-start | bytes 3145732
  42.3 68.1 %copy-start.5 = (bf16[4,256,256]{2,1,0:T(8,128)(2,1)S(1)}, bf16[4,256,256]{2,1,0:T(8,128)(2,1)}, u32[]{:S(2)}) copy-start(bf16[4,256,256]{2,1,0:T(8,128)(2,1)} %constant.124.clone.tables) | copy-start | bytes 1572868
  43.1 23.5 %all-to-all-start.2 = ((bf16[8,2,32,128]{3,2,1,0:T(8,128)(2,1)}), bf16[8,2,32,128]{3,2,1,0:T(8,128)(2,1)S(1)}, u32[]{:S(2)}, u32[]{:S(2)}) async-start(bf16[8,2,32,128]{3,2,1,0:T(8,128)(2,1)} %maximum_bitcast_fusion.1), calls=%async_computation.2 | async-start | bytes 262144 | tf_op jit(solution)/shard_map/all_to_all | solution.py:205
  52.5 58.0 %all-gather.5.cloned.1.call-start = ((), (), s32[]{:S(2)}) async-start(), calls=%async_computation.12 | async-start | bytes 1572864 | tf_op jit(solution)/shard_map/all_gather | solution.py:232
  110.5 1.2 copy-start.3
  125.1 1.4 copy-start
  126.5 5.6 %copy-start.8 = (s32[128,128]{1,0:T(8,128)S(1)}, s32[128,128]{1,0:T(8,128)}, u32[]{:S(2)}) copy-start(s32[128,128]{1,0:T(8,128)} %param.6) | copy-start | bytes 196612
  126.5 5.8 %slice-start = ((s32[128,128]{1,0:T(8,128)}), s32[1,128]{1,0:T(1,128)S(1)}, s32[]{:S(2)}) async-start(s32[128,128]{1,0:T(8,128)} %param.6), calls=%async_computation.14 | async-start | bytes 1024 | tf_op jit(solution)/shard_map/jit(_roll_static)/slice | solution.py:248
  126.5 32.1 %all-to-all-start.5 = ((bf16[8,1040,128]{2,1,0:T(8,128)(2,1)}), bf16[8,1040,128]{2,1,0:T(8,128)(2,1)S(1)}, u32[]{:S(2)}, u32[]{:S(2)}) async-start(bf16[8,1040,128]{2,1,0:T(8,128)(2,1)} %copy-done), calls=%async_computation.5 | async-start | bytes 4259840 | tf_op jit(solution)/shard_map/all_to_all | solution.py:205
  132.1 163.1 %all-gather.7.cloned.1.call-start = ((), (), s32[]{:S(2)}) async-start(), calls=%async_computation.13 | async-start | bytes 1572864 | tf_op jit(solution)/shard_map/all_gather | solution.py:244
  158.6 1.0 copy-start.6
  172.1 32.0 %copy-start.2 = (bf16[2,16,128,128]{3,2,1,0:T(8,128)(2,1)S(1)}, bf16[2,16,128,128]{3,2,1,0:T(8,128)(2,1)}, u32[]{:S(2)}) copy-start(bf16[2,16,128,128]{3,2,1,0:T(8,128)(2,1)} %values.3) | copy-start | bytes 3145732
  172.1 32.0 %copy-start.4 = (bf16[8,8,2,32,128]{4,3,2,1,0:T(8,128)(2,1)S(1)}, bf16[8,8,2,32,128]{4,3,2,1,0:T(8,128)(2,1)}, u32[]{:S(2)}) copy-start(bf16[8,8,2,32,128]{4,3,2,1,0:T(8,128)(2,1)} %all-gather.5.cloned.1.call-done) | copy-start | bytes 3145732
  172.1 32.0 %copy-start.7 = (bf16[4,256,256]{2,1,0:T(8,128)(2,1)S(1)}, bf16[4,256,256]{2,1,0:T(8,128)(2,1)}, u32[]{:S(2)}) copy-start(bf16[4,256,256]{2,1,0:T(8,128)(2,1)} %constant.124.clone.tables) | copy-start | bytes 1572868
Sparse Core Ops, SparseCore 0:
  93.3 17.0 all-gather.4
  281.4 13.7 all-gather.6

commit v2 on v1

v2 whole, which is shorter than its diff:
```python
import functools
import math

import jax
import jax.numpy as jnp
import numpy as np
from jax import lax
from jax.experimental import pallas as pl
from jax.experimental.pallas import tpu as pltpu
from jax.sharding import Mesh, PartitionSpec as P

COULOMB = math.pi / 8
GRID = 128
STEPS = 2
ROWS = 16
CHUNK = STEPS * ROWS * 2 * ROWS
BF16 = jnp.bfloat16
F32 = jnp.float32

AXES = ("zh", "zl", "xl", "core", "xh", "y")
SIZES = (4, 4, 2, 2, 2, 4)
GA = ("xh", "y")
OCT = ("zl", "xl")
VMEM = pl.BlockSpec(memory_space=pltpu.VMEM)
SMEM = pl.BlockSpec(memory_space=pltpu.SMEM)
HALF = ROWS // 2


def dft_tables():
    indices = np.arange(GRID)
    angles = (indices[:, None] * indices[None, :] % GRID) * (2.0 * np.pi / GRID)
    cosine, sine = np.cos(angles), np.sin(angles)
    matrix = np.block([[cosine, -sine], [sine, cosine]]).astype(np.float32)
    high = matrix.astype(BF16)
    low = (matrix - high.astype(np.float32)).astype(BF16)
    return np.stack([high, low, high.T, low.T])


def dot(a, b):
    return jnp.dot(a, b, preferred_element_type=F32)


def split(x):
    high = x.astype(BF16)
    return high, (x - high.astype(F32)).astype(BF16)


def right(x, tables, which):
    high, low = split(x)
    return dot(high, tables[which]) + (dot(low, tables[which]) + dot(high, tables[which + 1]))


def left(x, tables, which):
    high, low = split(x)
    return dot(tables[which], high) + (dot(tables[which], low) + dot(tables[which + 1], high))


def left_exact(x, tables, which):
    return dot(tables[which], x) + dot(tables[which + 1], x)


def quarter_swap(x):
    n = GRID
    return jnp.concatenate(
        [
            jnp.concatenate([x[:n, :n], x[n:, :n]], axis=1),
            jnp.concatenate([x[:n, n:], x[n:, n:]], axis=1),
        ],
        axis=0,
    )


def halves(core, own, other):
    first = core[0] * HALF
    return [(own, first), (other, HALF - first)]


def forward_kernel(core, values, own, other, tables, out, scratch):
    n = GRID
    for s in range(STEPS):
        for fields, first in halves(core, own, other):
            for p in range(0, HALF, 2):
                field = fields[p : p + 2, s].reshape(2 * n, n).astype(F32)
                pair = pl.ds(first + p, 2)
                left_band = values[0, pair].reshape(2 * n, n).astype(F32)
                right_band = values[1, pair].reshape(2 * n, n).astype(F32)
                density = jnp.concatenate([left_band * field, right_band * field], axis=1)
                along_z = quarter_swap(right(density, tables, 0))
                along_y = left(along_z, tables, 2)
                start = pl.multiple_of((first + p) * n, 2 * n)
                for part in range(2):
                    rows = along_y[part * n : (part + 1) * n]
                    scratch[2 * s + part, pl.ds(start, n), :] = rows[:, :n]
                    scratch[2 * s + part, pl.ds(start + n, n), :] = rows[:, n:]

    lane = lax.broadcasted_iota(jnp.int32, (ROWS, n), 1)

    def send(j, carry):
        rest = jnp.zeros((ROWS, n), F32)
        for s in range(STEPS):
            for k in range(ROWS):
                for part in range(2):
                    field = 2 * s + part
                    tile = scratch[field, pl.ds(j * ROWS + k, ROWS, stride=n), :]
                    high = tile.astype(BF16)
                    row = ((s * ROWS + k) * 2 + part) * ROWS
                    out[j, row : row + ROWS] = high
                    if k == 0:
                        low = tile - high.astype(F32)
                        below = low - low.astype(BF16).astype(F32)
                        rest = jnp.where(lane == field, low[:, :1], rest)
                        rest = jnp.where(lane == field + 2 * STEPS, below[:, :1], rest)
        out[j, CHUNK:] = rest.astype(BF16)
        return carry

    lax.fori_loop(0, n // ROWS, send, 0)


def solve_kernel(spectrum, coulomb, tables, out, scratch):
    n = GRID
    rest = spectrum[:, CHUNK:].reshape(n, n).astype(F32)
    lane = lax.broadcasted_iota(jnp.int32, (n, n), 1)
    dropped = coulomb[0, :1, :1] == 0.0
    for s in range(STEPS):

        def pick(k):
            row = (s * ROWS + k) * 2 * ROWS
            ends = [row + part * ROWS for part in range(2)]
            return [spectrum[:, end : end + ROWS].reshape(n, n) for end in ends]

        def factor(q):
            pair = jnp.concatenate([coulomb[2 * q], coulomb[2 * q + 1]], axis=1)
            return jnp.concatenate([pair, pair], axis=0)

        def keep(q, solved):
            start = q * 4 * n
            scratch[start : start + 2 * n] = solved[:, :n]
            scratch[start + 2 * n : start + 4 * n] = solved[:, n:]

        def columns(q):
            both = jnp.concatenate(
                [jnp.concatenate(pick(2 * q), axis=0), jnp.concatenate(pick(2 * q + 1), axis=0)],
                axis=1,
            )
            keep(q, left(left_exact(both, tables, 2) * factor(q), tables, 0))

        parts = []
        for part, tile in enumerate(pick(0)):
            tile, field = tile.astype(F32), 2 * s + part
            low = rest[:, field : field + 1] + rest[:, field + 2 * STEPS : field + 2 * STEPS + 1]
            column = tile[:, :1] + low
            mean = jnp.sum(column, axis=0, keepdims=True) * (1.0 / n)
            column = column - jnp.where(dropped, mean, 0.0)
            parts.append(jnp.where(lane == 0, column, tile))
        both = jnp.concatenate(
            [jnp.concatenate(parts, axis=0), jnp.concatenate(pick(1), axis=0).astype(F32)], axis=1
        )
        keep(0, left(left(both, tables, 2) * factor(0), tables, 0))
        for q in range(1, ROWS // 2):
            columns(q)

        def send(i, carry):
            for x in range(ROWS):
                for part in range(2):
                    tile = scratch[pl.ds(part * n + i * ROWS + x, ROWS, stride=2 * n), :]
                    out[i, s, x, part] = tile.astype(BF16)
            return carry

        lax.fori_loop(0, n // ROWS, send, 0)


def backward_kernel(core, solved, values, own, other, tables, exchange, keep, send):
    n = GRID
    for (fields, first), terms in zip(halves(core, own, other), (keep, send)):
        for p in range(0, HALF, 2):
            pair = pl.ds(first + p, 2)
            left_band = values[0, pair].reshape(2 * n, n).astype(F32)
            right_band = values[1, pair].reshape(2 * n, n).astype(F32)
            totals = [0.0, 0.0]
            for s in range(STEPS):

                def pick(x):
                    parts = [solved[:, s, x, part].reshape(n, n) for part in range(2)]
                    return jnp.concatenate(parts, axis=0)

                both = jnp.concatenate([pick(first + p), pick(first + p + 1)], axis=1)
                along_y = quarter_swap(left_exact(both, tables, 0))
                potential = right(along_y, tables, 2)
                field = fields[p : p + 2, s].reshape(2 * n, n).astype(F32)
                real, imag = potential[:, :n], potential[:, n:]
                totals = [totals[0] + real * field, totals[1] + imag * field]
                term = real * left_band + imag * right_band
                terms[p : p + 2, s] = term.astype(terms.dtype).reshape(2, n, n)
            for band in range(2):
                exchange[band, pair] = totals[band].reshape(2, n, n)


def pick_slot(owners, orbitals, out):
    for s in range(STEPS):
        slot = lax.rem(owners[s], 2)
        for half in range(2):
            out[half, s] = orbitals[slot, half * HALF : (half + 1) * HALF]


def pick_core(owners, pieces, out):
    for s in range(STEPS):
        core = lax.rem(lax.div(owners[s], 2), 2)
        for x in range(HALF):
            out[x, s] = pieces[core, s, x]


def pick_copies(divisor, count, owners, pieces, out):
    for s in range(STEPS):
        piece = pieces[lax.rem(lax.div(owners[s], divisor), count), s]
        for copy in range(out.shape[0]):
            out[copy, s] = piece


def assemble(core, own, other, out):
    for half, first in halves(core, own, other):
        for s in range(STEPS):
            for x in range(HALF):
                out[s, first + x] = half[x, s]


def call(kernel, outs, scratch, flops, scalars=1, operands=4):
    return pl.pallas_call(
        kernel,
        out_shape=outs,
        in_specs=[SMEM] * scalars + [VMEM] * operands,
        scratch_shapes=scratch,
        compiler_params=pltpu.CompilerParams(vmem_limit_bytes=40 * 1024 * 1024),
        cost_estimate=pl.CostEstimate(flops=flops, bytes_accessed=5 << 20, transcendentals=0),
    )


def exchange_all(x, axes):
    return lax.all_to_all(x, axes, 0, 0, tiled=True)


def gather_all(x, axes, count):
    return exchange_all(jnp.broadcast_to(x[None], (count,) + x.shape), axes)


def swap_cores(x):
    return lax.ppermute(x, "core", [(0, 1), (1, 0)])


def pick(kernel, shape, owners, pieces):
    outs = jax.ShapeDtypeStruct(shape + (GRID, GRID), BF16)
    return call(kernel, outs, [], 1 << 20, operands=1)(owners, pieces)


def spread_owners(orbitals, owners):
    piece = pick(pick_slot, (2, STEPS, HALF), owners, orbitals)
    piece = pick(pick_core, (HALF, STEPS), owners, exchange_all(piece, "core"))
    piece = exchange_all(piece, OCT)
    piece = pick(functools.partial(pick_copies, 4, 8), (4, STEPS), owners, piece)
    piece = exchange_all(piece, "zh")
    piece = pick(functools.partial(pick_copies, 32, 4), (8, STEPS), owners, piece)
    own = exchange_all(piece, OCT)
    return own, swap_cores(own)


def total_terms(keep, send):
    piece = (keep + swap_cores(send).astype(F32)).astype(BF16)
    piece = jnp.sum(exchange_all(piece, OCT).astype(F32), axis=0).astype(BF16)
    piece = gather_all(piece, "zh", 4)
    piece = jnp.sum(piece.astype(F32), axis=0).astype(BF16)
    own = gather_all(piece, OCT, 8)
    return own, swap_cores(own)


def coulomb_slab(cutoff, first_row):
    mirrored = jnp.roll(cutoff[::-1, ::-1], (1, 1), (0, 1))
    limits = lax.dynamic_slice_in_dim(jnp.minimum(cutoff, mirrored), first_row, ROWS, 1).T
    full = jnp.arange(GRID, dtype=jnp.int32)
    signed = jnp.where(full < GRID // 2, full, full - GRID)
    own = first_row + jnp.arange(ROWS, dtype=jnp.int32)
    own = jnp.where(own < GRID // 2, own, own - GRID)
    squared = own[:, None, None] ** 2 + signed[None, :, None] ** 2 + signed[None, None, :] ** 2
    inside = (jnp.abs(signed)[None, None, :] <= limits[:, :, None]) & (squared > 0)
    scale = COULOMB * float(GRID) ** 1.5 / float(GRID) ** 3
    return jnp.where(inside, scale / jnp.maximum(squared, 1).astype(F32), 0.0)


def shards(orbitals, owners, cutoff):
    first_row = lax.axis_index(GA) * ROWS
    coulomb = coulomb_slab(cutoff, first_row)
    tables = jnp.asarray(dft_tables())
    core = lax.axis_index("core").astype(jnp.int32).reshape(1)
    own, other = spread_owners(orbitals, owners)
    flops = 2 * 2 * STEPS * 3 * 8 * 256**3
    with jax.named_scope("forward_planes"):
        spectrum = call(
            forward_kernel,
            jax.ShapeDtypeStruct((8, CHUNK + ROWS, GRID), BF16),
            [pltpu.VMEM((2 * STEPS, ROWS * GRID, GRID), F32)],
            flops,
        )(core, orbitals, own, other, tables)
    spectrum = exchange_all(spectrum, GA)
    with jax.named_scope("coulomb_solve"):
        solved = call(
            solve_kernel,
            jax.ShapeDtypeStruct((8, STEPS, ROWS, 2, ROWS, GRID), BF16),
            [pltpu.VMEM((ROWS * 2 * GRID, GRID), F32)],
            flops,
            scalars=0,
            operands=3,
        )(spectrum, coulomb, tables)
    solved = exchange_all(solved, GA)
    with jax.named_scope("backward_planes"):
        exchange, keep, send = call(
            backward_kernel,
            (
                jax.ShapeDtypeStruct((2, ROWS, GRID, GRID), F32),
                jax.ShapeDtypeStruct((HALF, STEPS, GRID, GRID), F32),
                jax.ShapeDtypeStruct((HALF, STEPS, GRID, GRID), BF16),
            ),
            [],
            flops,
            operands=5,
        )(core, solved, orbitals, own, other, tables)
    own, other = total_terms(keep, send)
    outs = jax.ShapeDtypeStruct((STEPS, ROWS, GRID, GRID), BF16)
    return exchange, call(assemble, outs, [], 1 << 20, operands=2)(core, own, other)


def solution(mesh):
    inner = Mesh(mesh.devices.reshape(SIZES), AXES)
    band, ga = AXES[:4], AXES[4:]
    return jax.shard_map(
        shards,
        mesh=inner,
        in_specs=(P(band, ga, None, None), P(), P()),
        out_specs=(P(band, ga, None, None), P(None, ga, None, None)),
        check_vma=False,
    )
```

time: 305 us -> 240 us (0.79)
  waiting for transfers between devices: 70.8 us -> 28.9 us
  blocking collectives: 126 us -> 157 us
  between operations: 29.8 us -> 0.89 us
  Pallas kernels: 34.2 us -> 22.2 us
  starting transfers between devices: 29 us -> 22.2 us
  local copies, waits for them, and re-layouts: 11.1 us -> 5.93 us
    all_gather x2 -> x0, waiting for transfers between devices: 31.1 us -> none  [the longest x1 17.2 us: spread_owners(): return lax.all_gather(piece, 'core', axis=0, tiled=False)]
    all_to_all x8, blocking collectives: 126 us -> 157 us  [exchange_all(): return lax.all_to_all(x, axes, 0, 0, tiled=True)]
    all_to_all x4 -> x1, starting transfers between devices: 28.9 us -> 6.49 us  [exchange_all(): return lax.all_to_all(x, axes, 0, 0, tiled=True)]
    ppermute x0 -> x3, starting transfers between devices: none -> 15.7 us  [swap_cores(): return lax.ppermute(x, 'core', [(0, 1), (1, 0)])]
    all_to_all x4 -> x1, waiting for transfers between devices: 39.6 us -> 24.4 us  [exchange_all(): return lax.all_to_all(x, axes, 0, 0, tiled=True)]
    pallas_call x1, Pallas kernels: 13.4 us -> 6.22 us  [shards(): call(forward_kernel, jax.ShapeDtypeStruct((8, CHUNK + ROWS, GRID), BF16),...]
    ppermute x0 -> x3, waiting for transfers between devices: none -> 4.54 us  [swap_cores(): return lax.ppermute(x, 'core', [(0, 1), (1, 0)])]
    transpose x2 -> x0, local copies, waits for them, and re-layouts: 3.36 us -> none  [the longest x1 2.32 us: shards(): total = jnp.moveaxis(total, 3, 0).reshape(STEPS, ROWS, GRID, GRID)]
  transfers between devices with their start and end apart: 6 -> 4, of which waited for: 5 -> 4; matrix products, arithmetic and copies ran while one was open for 1% -> 1% of each run, Pallas kernels for 0% -> 0%
where the time goes in v2:
time: 240 us; the launch traced here: 239 us
  blocking collectives  157 us (65%)
  waiting for transfers between devices  28.9 us (12%)
  Pallas kernels  22.2 us (9%)
  starting transfers between devices  22.2 us (9%)
  local copies, waits for them, and re-layouts  5.93 us (2%)
    all_to_all x8, blocking collectives, exchange_all(): return lax.all_to_all(x, axes, 0, 0, tiled=True)  157 us
    all_to_all x1, waiting for transfers between devices, exchange_all(): return lax.all_to_all(x, axes, 0, 0, tiled=True)  24.4 us
    ppermute x3, starting transfers between devices, swap_cores(): return lax.ppermute(x, 'core', [(0, 1), (1, 0)])  15.7 us
    pallas_call x1, Pallas kernels, shards(): call(solve_kernel, jax.ShapeDtypeStruct((8, STEPS, ROWS, 2, ROWS, GRID),...  7.19 us
    all_to_all x1, starting transfers between devices, exchange_all(): return lax.all_to_all(x, axes, 0, 0, tiled=True)  6.49 us
    pallas_call x1, Pallas kernels, shards(): call(forward_kernel, jax.ShapeDtypeStruct((8, CHUNK + ROWS, GRID), BF16),...  6.22 us
    unnamed x26, local copies, waits for them, and re-layouts  5.52 us
    pallas_call x1, Pallas kernels, shards(): call(backward_kernel, (jax.ShapeDtypeStruct((2, ROWS, GRID, GRID), F32),...  5.34 us
  transfers between devices with their start and end apart: 4, of which 4 were waited for; matrix products, arithmetic and copies ran while one was open for 1% of the time, Pallas kernels for 0%

profile of v2, /device:TPU:1, one launch (start us, length us, event | category | flops | bytes accessed | tf_op | source)
XLA Modules:
  0.0 238.8 jit_solution(11006458568747788494)
XLA Ops:
  0.6 1.2 copy-done.1
  3.1 11.1 %all_to_all.45.pieces = bf16[2,2,8,128,128]{4,3,2,1,0:T(8,128)(2,1)S(1)} all-to-all(bf16[2,2,8,128,128]{4,3,2,1,0:T(8,128)(2,1)S(1)} %shard_map.59), channel_id=1, replica_groups=mesh['zh'=4,'zl'=4,'xl'=2,'core'=2,'xh'=2,'y'=4] {'core'}, dimensions={0} | all-to-all | bytes 2097152 | tf_op jit(solution)/shard_map/all_to_all | solution.py:238
  14.8 16.8 %all_to_all.46.pieces = bf16[8,2,128,128]{3,2,1,0:T(8,128)(2,1)S(1)} all-to-all(bf16[8,2,128,128]{3,2,1,0:T(8,128)(2,1)S(1)} %shard_map.60), channel_id=1, replica_groups=mesh['zh'=4,'zl'=4,'xl'=2,'core'=2,'xh'=2,'y'=4] {'zl','xl'}, dimensions={0} | all-to-all | bytes 1048576 | tf_op jit(solution)/shard_map/all_to_all | solution.py:238
  32.2 26.2 %all_to_all.47.pieces = bf16[4,2,128,128]{3,2,1,0:T(8,128)(2,1)S(1)} all-to-all(bf16[4,2,128,128]{3,2,1,0:T(8,128)(2,1)S(1)} %shard_map.61), channel_id=1, replica_groups=mesh['zh'=4,'zl'=4,'xl'=2,'core'=2,'xh'=2,'y'=4] {'zh'}, dimensions={0} | all-to-all | bytes 524288 | tf_op jit(solution)/shard_map/all_to_all | solution.py:238
  59.0 17.1 %all_to_all.48.own = bf16[8,2,128,128]{3,2,1,0:T(8,128)(2,1)S(1)} all-to-all(bf16[8,2,128,128]{3,2,1,0:T(8,128)(2,1)S(1)} %shard_map.62), channel_id=1, replica_groups=mesh['zh'=4,'zl'=4,'xl'=2,'core'=2,'xh'=2,'y'=4] {'zl','xl'}, dimensions={0} | all-to-all | bytes 1048576 | tf_op jit(solution)/shard_map/all_to_all | solution.py:238
  76.1 5.7 %collective-permute-start = (bf16[8,2,128,128]{3,2,1,0:T(8,128)(2,1)S(1)}, bf16[8,2,128,128]{3,2,1,0:T(8,128)(2,1)S(1)}, u32[]{:S(2)}, u32[]{:S(2)}) collective-permute-start(bf16[8,2,128,128]{3,2,1,0:T(8,128)(2,1)S(1)} %all_to_all.48.own), channel_id=1, source_target_pairs={{0,8},{8,0},{1,9},{9,1},{2,10},{10,2},{3,11},{11,3},{4,12},{12,4},... | collective-permute-start | bytes 1572872 | tf_op jit(solution)/shard_map/ppermute | solution.py:246
  81.8 1.5 collective-permute-done.other
  83.3 6.2 %forward_planes.1 = bf16[8,1040,128]{2,1,0:T(8,128)(2,1)S(1)} custom-call(s32[1]{0:T(128)} %bitcast.core, bf16[2,16,128,128]{3,2,1,0:T(8,128)(2,1)S(1)} %copy-done.2, bf16[8,2,128,128]{3,2,1,0:T(8,128)(2,1)S(1)} %all_to_all.48.own, bf16[8,2,128,128]{3,2,1,0:T(8,128)(2,1)S(1)} %collective-permute-done.other, bf16[4,256,256]{2,1,0:T(8,128)(2,1)S(1)} %copy-done.9), custom_call_target="tpu_custom_call" | custom-call | flops 3221225472 | bytes 5242880 | tf_op jit(solution)/shard_map/forward_planes/pallas_call | solution.py:295
  89.6 1.3 copy-done
  90.9 6.5 %all-to-all-start.4 = ((bf16[8,1040,128]{2,1,0:T(8,128)(2,1)}), bf16[8,1040,128]{2,1,0:T(8,128)(2,1)S(1)}, u32[]{:S(2)}, u32[]{:S(2)}) async-start(bf16[8,1040,128]{2,1,0:T(8,128)(2,1)} %copy-done), calls=%async_computation.4 | async-start | bytes 4259840 | tf_op jit(solution)/shard_map/all_to_all | solution.py:238
  98.1 1.5 fusion.2.coulomb
  99.6 24.4 %all-to-all-done.4.spectrum = bf16[8,1040,128]{2,1,0:T(8,128)(2,1)S(1)} async-done(((bf16[8,1040,128]{2,1,0:T(8,128)(2,1)}), bf16[8,1040,128]{2,1,0:T(8,128)(2,1)S(1)}, u32[]{:S(2)}, u32[]{:S(2)}) %all-to-all-start.4) | async-done | bytes 2129952 | tf_op jit(solution)/shard_map/all_to_all | solution.py:238
  124.0 1.2 copy-done.3
  125.2 1.0 copy-done.10
  126.2 7.2 %coulomb_solve.1 = bf16[8,2,16,2,16,128]{5,4,3,2,1,0:T(8,128)(2,1)S(1)} custom-call(bf16[8,1040,128]{2,1,0:T(8,128)(2,1)S(1)} %all-to-all-done.4.spectrum, f32[16,128,128]{2,1,0:T(8,128)S(1)} %copy-done.3, bf16[4,256,256]{2,1,0:T(8,128)(2,1)S(1)} %copy-done.10), custom_call_target="tpu_custom_call" | custom-call | flops 3221225472 | bytes 5242880 | tf_op jit(solution)/shard_map/coulomb_solve/pallas_call | solution.py:303
  133.5 32.0 %all_to_all.49.solved = bf16[8,2,16,2,16,128]{5,4,3,2,1,0:T(8,128)(2,1)S(1)} all-to-all(bf16[8,2,16,2,16,128]{5,4,3,2,1,0:T(8,128)(2,1)S(1)} %coulomb_solve.1), channel_id=1, replica_groups=mesh['zh'=4,'zl'=4,'xl'=2,'core'=2,'xh'=2,'y'=4] {'xh','y'}, dimensions={0} | all-to-all | bytes 4194304 | tf_op jit(solution)/shard_map/all_to_all | solution.py:238
  165.5 5.3 %backward_planes.1 = (f32[2,16,128,128]{3,2,1,0:T(8,128)}, f32[8,2,128,128]{3,2,1,0:T(8,128)S(1)}, bf16[8,2,128,128]{3,2,1,0:T(8,128)(2,1)S(1)}) custom-call(s32[1]{0:T(128)} %bitcast.core, bf16[8,2,16,2,16,128]{5,4,3,2,1,0:T(8,128)(2,1)S(1)} %all_to_all.49.solved, bf16[2,16,128,128]{3,2,1,0:T(8,128)(2,1)S(1)} %copy-done.2, ...), custom_call_target="tpu_custom_call" | custom-call | flops 3221225472 | bytes 5242880 | tf_op jit(solution)/shard_map/backward_planes/pallas_call | solution.py:313
  170.8 4.3 %collective-permute-start.1 = (bf16[8,2,128,128]{3,2,1,0:T(8,128)(2,1)S(1)}, bf16[8,2,128,128]{3,2,1,0:T(8,128)(2,1)S(1)}, u32[]{:S(2)}, u32[]{:S(2)}) collective-permute-start(bf16[8,2,128,128]{3,2,1,0:T(8,128)(2,1)S(1)} %get-tuple-element.7), channel_id=1, source_target_pairs={{0,8},{8,0},{1,9},{9,1},{2,10},{10,2},{3,11},{11,3},{4,12},{12,4},... | collective-permute-start | bytes 1572872 | tf_op jit(solution)/shard_map/ppermute | solution.py:246
  175.2 1.5 collective-permute-done.1
  176.8 16.5 %all_to_all.50 = bf16[8,2,128,128]{3,2,1,0:T(8,128)(2,1)S(1)} all-to-all(bf16[8,2,128,128]{3,2,1,0:T(8,128)(2,1)S(1)} %add_convert_fusion), channel_id=1, replica_groups=mesh['zh'=4,'zl'=4,'xl'=2,'core'=2,'xh'=2,'y'=4] {'zl','xl'}, dimensions={0} | all-to-all | bytes 1048576 | tf_op jit(solution)/shard_map/all_to_all | solution.py:238
  193.5 19.8 %all_to_all.51 = bf16[4,2,128,128]{3,2,1,0:T(8,128)(2,1)S(1)} all-to-all(bf16[4,2,128,128]{3,2,1,0:T(8,128)(2,1)S(1)} %broadcast_in_dim.9), channel_id=1, replica_groups=mesh['zh'=4,'zl'=4,'xl'=2,'core'=2,'xh'=2,'y'=4] {'zh'}, dimensions={0} | all-to-all | bytes 524288 | tf_op jit(solution)/shard_map/all_to_all | solution.py:238
  213.4 17.1 %all_to_all.52.own = bf16[8,2,128,128]{3,2,1,0:T(8,128)(2,1)S(1)} all-to-all(bf16[8,2,128,128]{3,2,1,0:T(8,128)(2,1)S(1)} %broadcast_in_dim.10), channel_id=1, replica_groups=mesh['zh'=4,'zl'=4,'xl'=2,'core'=2,'xh'=2,'y'=4] {'zl','xl'}, dimensions={0} | all-to-all | bytes 1048576 | tf_op jit(solution)/shard_map/all_to_all | solution.py:238
  230.5 5.7 %collective-permute-start.2 = (bf16[8,2,128,128]{3,2,1,0:T(8,128)(2,1)S(1)}, bf16[8,2,128,128]{3,2,1,0:T(8,128)(2,1)S(1)}, u32[]{:S(2)}, u32[]{:S(2)}) collective-permute-start(bf16[8,2,128,128]{3,2,1,0:T(8,128)(2,1)S(1)} %all_to_all.52.own), channel_id=1, source_target_pairs={{0,8},{8,0},{1,9},{9,1},{2,10},{10,2},{3,11},{11,3},{4,12},{12,4},... | collective-permute-start | bytes 1572872 | tf_op jit(solution)/shard_map/ppermute | solution.py:246
  236.3 1.5 collective-permute-done.2.other
  (44 shorter events, 5.1 us)
Async XLA Ops:
  0.6 1.2 copy-start.1
  1.9 0.7 copy-start.6
  14.8 68.5 %copy-start.2 = (bf16[2,16,128,128]{3,2,1,0:T(8,128)(2,1)S(1)}, bf16[2,16,128,128]{3,2,1,0:T(8,128)(2,1)}, u32[]{:S(2)}) copy-start(bf16[2,16,128,128]{3,2,1,0:T(8,128)(2,1)} %values.3) | copy-start | bytes 3145732
  14.8 68.5 %copy-start.9 = (bf16[4,256,256]{2,1,0:T(8,128)(2,1)S(1)}, bf16[4,256,256]{2,1,0:T(8,128)(2,1)}, u32[]{:S(2)}) copy-start(bf16[4,256,256]{2,1,0:T(8,128)(2,1)} %constant.40.clone.tables) | copy-start | bytes 1572868
  76.1 13.5 %copy-start.4 = (bf16[8,2,128,128]{3,2,1,0:T(8,128)(2,1)}, bf16[8,2,128,128]{3,2,1,0:T(8,128)(2,1)S(1)}, u32[]{:S(2)}) copy-start(bf16[8,2,128,128]{3,2,1,0:T(8,128)(2,1)S(1)} %all_to_all.48.own) | copy-start | bytes 1572868
  76.1 7.2 %collective-permute-start = (bf16[8,2,128,128]{3,2,1,0:T(8,128)(2,1)S(1)}, bf16[8,2,128,128]{3,2,1,0:T(8,128)(2,1)S(1)}, u32[]{:S(2)}, u32[]{:S(2)}) collective-permute-start(bf16[8,2,128,128]{3,2,1,0:T(8,128)(2,1)S(1)} %all_to_all.48.own), channel_id=1, source_target_pairs={{0,8},{8,0},{1,9},{9,1},{2,10},{10,2},{3,11},{11,3},{4,12},{12,4},... | collective-permute-start | bytes 1572872 | tf_op jit(solution)/shard_map/ppermute | solution.py:246
  83.3 6.2 %copy-start.7 = (bf16[8,2,128,128]{3,2,1,0:T(8,128)(2,1)}, bf16[8,2,128,128]{3,2,1,0:T(8,128)(2,1)S(1)}, u32[]{:S(2)}) copy-start(bf16[8,2,128,128]{3,2,1,0:T(8,128)(2,1)S(1)} %collective-permute-done.other) | copy-start | bytes 1572868
  89.6 1.3 copy-start
  90.9 6.5 %copy-start.12 = (s32[128,128]{1,0:T(8,128)S(1)}, s32[128,128]{1,0:T(8,128)}, u32[]{:S(2)}) copy-start(s32[128,128]{1,0:T(8,128)} %param.6) | copy-start | bytes 196612
  90.9 6.5 %slice-start = ((s32[128,128]{1,0:T(8,128)}), s32[1,128]{1,0:T(1,128)S(1)}, s32[]{:S(2)}) async-start(s32[128,128]{1,0:T(8,128)} %param.6), calls=%async_computation.9 | async-start | bytes 1024 | tf_op jit(solution)/shard_map/jit(_roll_static)/slice | solution.py:275
  90.9 33.0 %all-to-all-start.4 = ((bf16[8,1040,128]{2,1,0:T(8,128)(2,1)}), bf16[8,1040,128]{2,1,0:T(8,128)(2,1)S(1)}, u32[]{:S(2)}, u32[]{:S(2)}) async-start(bf16[8,1040,128]{2,1,0:T(8,128)(2,1)} %copy-done), calls=%async_computation.4 | async-start | bytes 4259840 | tf_op jit(solution)/shard_map/all_to_all | solution.py:238
  124.0 1.2 copy-start.3
  125.2 1.0 copy-start.10
  133.4 32.0 %copy-start.5 = (bf16[8,2,128,128]{3,2,1,0:T(8,128)(2,1)S(1)}, bf16[8,2,128,128]{3,2,1,0:T(8,128)(2,1)}, u32[]{:S(2)}) copy-start(bf16[8,2,128,128]{3,2,1,0:T(8,128)(2,1)} %copy-done.4) | copy-start | bytes 1572868
  133.5 32.0 %copy-start.8 = (bf16[8,2,128,128]{3,2,1,0:T(8,128)(2,1)S(1)}, bf16[8,2,128,128]{3,2,1,0:T(8,128)(2,1)}, u32[]{:S(2)}) copy-start(bf16[8,2,128,128]{3,2,1,0:T(8,128)(2,1)} %copy-done.7) | copy-start | bytes 1572868
  133.5 32.0 %copy-start.11 = (bf16[4,256,256]{2,1,0:T(8,128)(2,1)S(1)}, bf16[4,256,256]{2,1,0:T(8,128)(2,1)}, u32[]{:S(2)}) copy-start(bf16[4,256,256]{2,1,0:T(8,128)(2,1)} %constant.40.clone.tables) | copy-start | bytes 1572868
  170.8 5.9 %collective-permute-start.1 = (bf16[8,2,128,128]{3,2,1,0:T(8,128)(2,1)S(1)}, bf16[8,2,128,128]{3,2,1,0:T(8,128)(2,1)S(1)}, u32[]{:S(2)}, u32[]{:S(2)}) collective-permute-start(bf16[8,2,128,128]{3,2,1,0:T(8,128)(2,1)S(1)} %get-tuple-element.7), channel_id=1, source_target_pairs={{0,8},{8,0},{1,9},{9,1},{2,10},{10,2},{3,11},{11,3},{4,12},{12,4},... | collective-permute-start | bytes 1572872 | tf_op jit(solution)/shard_map/ppermute | solution.py:246
  230.5 7.2 %collective-permute-start.2 = (bf16[8,2,128,128]{3,2,1,0:T(8,128)(2,1)S(1)}, bf16[8,2,128,128]{3,2,1,0:T(8,128)(2,1)S(1)}, u32[]{:S(2)}, u32[]{:S(2)}) collective-permute-start(bf16[8,2,128,128]{3,2,1,0:T(8,128)(2,1)S(1)} %all_to_all.52.own), channel_id=1, source_target_pairs={{0,8},{8,0},{1,9},{9,1},{2,10},{10,2},{3,11},{11,3},{4,12},{12,4},... | collective-permute-start | bytes 1572872 | tf_op jit(solution)/shard_map/ppermute | solution.py:246

commit v3 on v2

--- a/solution.py
+++ b/solution.py
@@ -7,7 +7,7 @@
 from jax import lax
 from jax.experimental import pallas as pl
 from jax.experimental.pallas import tpu as pltpu
-from jax.sharding import Mesh, PartitionSpec as P
+from jax.sharding import PartitionSpec as P
 
 COULOMB = math.pi / 8
 GRID = 128
@@ -17,10 +17,25 @@
 BF16 = jnp.bfloat16
 F32 = jnp.float32
 
-AXES = ("zh", "zl", "xl", "core", "xh", "y")
-SIZES = (4, 4, 2, 2, 2, 4)
-GA = ("xh", "y")
-OCT = ("zl", "xl")
+SHIFT = 2
+
+
+def place(z, xl, core):
+    return z % 16 * 4 + xl * 2 + core
+
+
+NEAR = [
+    [place(4 * k + j + SHIFT * core, xl, core) for j in range(4) for xl in range(2)]
+    for core in range(2)
+    for k in range(4)
+]
+FAR = [
+    [place(4 * k + j + SHIFT * core, xl, core) for k in range(4)]
+    for core in range(2)
+    for j in range(4)
+    for xl in range(2)
+]
+CORES = [[2 * i, 2 * i + 1] for i in range(32)]
 VMEM = pl.BlockSpec(memory_space=pltpu.VMEM)
 SMEM = pl.BlockSpec(memory_space=pltpu.SMEM)
 HALF = ROWS // 2
@@ -48,6 +63,10 @@
 def right(x, tables, which):
     high, low = split(x)
     return dot(high, tables[which]) + (dot(low, tables[which]) + dot(high, tables[which + 1]))
+
+
+def right_exact(x, tables, which):
+    return dot(x, tables[which]) + dot(x, tables[which + 1])
 
 
 def left(x, tables, which):
@@ -132,6 +151,9 @@
             pair = jnp.concatenate([coulomb[2 * q], coulomb[2 * q + 1]], axis=1)
             return jnp.concatenate([pair, pair], axis=0)
 
+        def inverse(x):
+            return left_exact(x.astype(BF16), tables, 0)
+
         def keep(q, solved):
             start = q * 4 * n
             scratch[start : start + 2 * n] = solved[:, :n]
@@ -142,7 +164,7 @@
                 [jnp.concatenate(pick(2 * q), axis=0), jnp.concatenate(pick(2 * q + 1), axis=0)],
                 axis=1,
             )
-            keep(q, left(left_exact(both, tables, 2) * factor(q), tables, 0))
+            keep(q, inverse(left_exact(both, tables, 2) * factor(q)))
 
         parts = []
         for part, tile in enumerate(pick(0)):
@@ -155,7 +177,7 @@
         both = jnp.concatenate(
             [jnp.concatenate(parts, axis=0), jnp.concatenate(pick(1), axis=0).astype(F32)], axis=1
         )
-        keep(0, left(left(both, tables, 2) * factor(0), tables, 0))
+        keep(0, inverse(left(both, tables, 2) * factor(0)))
         for q in range(1, ROWS // 2):
             columns(q)
 
@@ -185,7 +207,7 @@
 
                 both = jnp.concatenate([pick(first + p), pick(first + p + 1)], axis=1)
                 along_y = quarter_swap(left_exact(both, tables, 0))
-                potential = right(along_y, tables, 2)
+                potential = right_exact(along_y.astype(BF16), tables, 2)
                 field = fields[p : p + 2, s].reshape(2 * n, n).astype(F32)
                 real, imag = potential[:, :n], potential[:, n:]
                 totals = [totals[0] + real * field, totals[1] + imag * field]
@@ -195,23 +217,35 @@
                 exchange[band, pair] = totals[band].reshape(2, n, n)
 
 
-def pick_slot(owners, orbitals, out):
+def pick_slot(owners, core, orbitals, out):
     for s in range(STEPS):
         slot = lax.rem(owners[s], 2)
         for half in range(2):
             out[half, s] = orbitals[slot, half * HALF : (half + 1) * HALF]
 
 
-def pick_core(owners, pieces, out):
-    for s in range(STEPS):
-        core = lax.rem(lax.div(owners[s], 2), 2)
+def pick_core(owners, core, pieces, out):
+    for s in range(STEPS):
+        root = lax.rem(lax.div(owners[s], 2), 2)
         for x in range(HALF):
-            out[x, s] = pieces[core, s, x]
-
-
-def pick_copies(divisor, count, owners, pieces, out):
-    for s in range(STEPS):
-        piece = pieces[lax.rem(lax.div(owners[s], divisor), count), s]
+            out[x, s] = pieces[root, s, x]
+
+
+def root_z(owner, core):
+    return lax.rem(lax.div(owner, 8) + 16 - SHIFT * core, 16)
+
+
+def pick_near(owners, core, pieces, out):
+    for s in range(STEPS):
+        z, xl = root_z(owners[s], core[0]), lax.rem(lax.div(owners[s], 4), 2)
+        piece = pieces[lax.rem(z, 4) * 2 + xl, s]
+        for copy in range(out.shape[0]):
+            out[copy, s] = piece
+
+
+def pick_far(owners, core, pieces, out):
+    for s in range(STEPS):
+        piece = pieces[lax.div(root_z(owners[s], core[0]), 4), s]
         for copy in range(out.shape[0]):
             out[copy, s] = piece
 
@@ -234,40 +268,40 @@
     )
 
 
-def exchange_all(x, axes):
-    return lax.all_to_all(x, axes, 0, 0, tiled=True)
-
-
-def gather_all(x, axes, count):
-    return exchange_all(jnp.broadcast_to(x[None], (count,) + x.shape), axes)
+def exchange_all(x, groups):
+    return lax.all_to_all(x, "band", 0, 0, axis_index_groups=groups, tiled=True)
+
+
+def gather_all(x, groups):
+    return exchange_all(jnp.broadcast_to(x[None], (len(groups[0]),) + x.shape), groups)
+
+
+def exchange_slabs(x):
+    return lax.all_to_all(x, "ga", 0, 0, tiled=True)
 
 
 def swap_cores(x):
-    return lax.ppermute(x, "core", [(0, 1), (1, 0)])
-
-
-def pick(kernel, shape, owners, pieces):
+    return lax.ppermute(x, "band", [(i, i ^ 1) for i in range(64)])
+
+
+def pick(kernel, shape, owners, core, pieces):
     outs = jax.ShapeDtypeStruct(shape + (GRID, GRID), BF16)
-    return call(kernel, outs, [], 1 << 20, operands=1)(owners, pieces)
-
-
-def spread_owners(orbitals, owners):
-    piece = pick(pick_slot, (2, STEPS, HALF), owners, orbitals)
-    piece = pick(pick_core, (HALF, STEPS), owners, exchange_all(piece, "core"))
-    piece = exchange_all(piece, OCT)
-    piece = pick(functools.partial(pick_copies, 4, 8), (4, STEPS), owners, piece)
-    piece = exchange_all(piece, "zh")
-    piece = pick(functools.partial(pick_copies, 32, 4), (8, STEPS), owners, piece)
-    own = exchange_all(piece, OCT)
-    return own, swap_cores(own)
+    return call(kernel, outs, [], 1 << 20, scalars=2, operands=1)(owners, core, pieces)
+
+
+def spread_owners(orbitals, owners, core):
+    piece = pick(pick_slot, (2, STEPS, HALF), owners, core, orbitals)
+    piece = pick(pick_core, (HALF, STEPS), owners, core, exchange_all(piece, CORES))
+    piece = pick(pick_near, (4, STEPS), owners, core, exchange_all(piece, NEAR))
+    piece = pick(pick_far, (8, STEPS), owners, core, exchange_all(piece, FAR))
+    return exchange_all(piece, NEAR)
 
 
 def total_terms(keep, send):
     piece = (keep + swap_cores(send).astype(F32)).astype(BF16)
-    piece = jnp.sum(exchange_all(piece, OCT).astype(F32), axis=0).astype(BF16)
-    piece = gather_all(piece, "zh", 4)
-    piece = jnp.sum(piece.astype(F32), axis=0).astype(BF16)
-    own = gather_all(piece, OCT, 8)
+    piece = jnp.sum(exchange_all(piece, NEAR).astype(F32), axis=0).astype(BF16)
+    piece = jnp.sum(gather_all(piece, FAR).astype(F32), axis=0).astype(BF16)
+    own = gather_all(piece, NEAR)
     return own, swap_cores(own)
 
 
@@ -285,11 +319,13 @@
 
 
 def shards(orbitals, owners, cutoff):
-    first_row = lax.axis_index(GA) * ROWS
-    coulomb = coulomb_slab(cutoff, first_row)
+    first_row = lax.axis_index("ga") * ROWS
     tables = jnp.asarray(dft_tables())
-    core = lax.axis_index("core").astype(jnp.int32).reshape(1)
-    own, other = spread_owners(orbitals, owners)
+    core = (lax.axis_index("band") % 2).astype(jnp.int32).reshape(1)
+    own = spread_owners(orbitals, owners, core)
+    cutoff, first_row, own = lax.optimization_barrier((cutoff, first_row, own))
+    other = swap_cores(own)
+    coulomb, other = lax.optimization_barrier((coulomb_slab(cutoff, first_row), other))
     flops = 2 * 2 * STEPS * 3 * 8 * 256**3
     with jax.named_scope("forward_planes"):
         spectrum = call(
@@ -298,7 +334,7 @@
             [pltpu.VMEM((2 * STEPS, ROWS * GRID, GRID), F32)],
             flops,
         )(core, orbitals, own, other, tables)
-    spectrum = exchange_all(spectrum, GA)
+    spectrum = exchange_slabs(spectrum)
     with jax.named_scope("coulomb_solve"):
         solved = call(
             solve_kernel,
@@ -308,7 +344,7 @@
             scalars=0,
             operands=3,
         )(spectrum, coulomb, tables)
-    solved = exchange_all(solved, GA)
+    solved = exchange_slabs(solved)
     with jax.named_scope("backward_planes"):
         exchange, keep, send = call(
             backward_kernel,
@@ -327,12 +363,10 @@
 
 
 def solution(mesh):
-    inner = Mesh(mesh.devices.reshape(SIZES), AXES)
-    band, ga = AXES[:4], AXES[4:]
     return jax.shard_map(
         shards,
-        mesh=inner,
-        in_specs=(P(band, ga, None, None), P(), P()),
-        out_specs=(P(band, ga, None, None), P(None, ga, None, None)),
+        mesh=mesh,
+        in_specs=(P("band", "ga", None, None), P(), P()),
+        out_specs=(P("band", "ga", None, None), P(None, "ga", None, None)),
         check_vma=False,
     )

time: 240 us -> 232 us (0.967)
  waiting for transfers between devices: 28.9 us -> 13.4 us
  blocking collectives: 157 us -> 167 us
  starting transfers between devices: 22.2 us -> 26.4 us
  local copies, waits for them, and re-layouts: 5.93 us -> 2.3 us
    all_to_all x1, waiting for transfers between devices: 24.4 us -> 9.78 us  [exchange_all(): return lax.all_to_all(x, 'band', 0, 0, axis_index_groups=groups, tiled=True)]
    all_to_all x8, blocking collectives: 157 us -> 167 us  [the longest x6 103 us: exchange_all(): return lax.all_to_all(x, 'band', 0, 0, axis_index_groups=groups, tiled=True)]
    unnamed x26 -> x10, local copies, waits for them, and re-layouts: 5.52 us -> 1.89 us
  transfers between devices with their start and end apart: 4 -> 4, of which waited for: 4 -> 4; matrix products, arithmetic and copies ran while one was open for 1% -> 0% of each run, Pallas kernels for 0% -> 0%
where the time goes in v3:
time: 232 us
  blocking collectives  167 us (72%)
  starting transfers between devices  26.4 us (11%)
  Pallas kernels  20.8 us (9%)
  waiting for transfers between devices  13.4 us (6%)
    all_to_all x6, blocking collectives, exchange_all(): return lax.all_to_all(x, 'band', 0, 0, axis_index_groups=groups, tiled=True)  103 us
    all_to_all x2, blocking collectives, exchange_slabs(): return lax.all_to_all(x, 'ga', 0, 0, tiled=True)  63.7 us
    ppermute x3, starting transfers between devices, swap_cores(): return lax.ppermute(x, 'band', [(i, i ^ 1) for i in range(64)])  17.8 us
    all_to_all x1, waiting for transfers between devices, exchange_all(): return lax.all_to_all(x, 'band', 0, 0, axis_index_groups=groups, tiled=True)  9.78 us
    all_to_all x1, starting transfers between devices, exchange_all(): return lax.all_to_all(x, 'band', 0, 0, axis_index_groups=groups, tiled=True)  8.68 us
    pallas_call x1, Pallas kernels, shards(): call(solve_kernel, jax.ShapeDtypeStruct((8, STEPS, ROWS, 2, ROWS, GRID),...  6.43 us
    pallas_call x1, Pallas kernels, shards(): call(forward_kernel, jax.ShapeDtypeStruct((8, CHUNK + ROWS, GRID), BF16),...  6.22 us
  transfers between devices with their start and end apart: 4, of which 4 were waited for; matrix products, arithmetic and copies ran while one was open for 0% of the time, Pallas kernels for 0%

profile of v3, /device:TPU:1, one launch (start us, length us, event | category | flops | bytes accessed | tf_op | source)
XLA Modules:
  0.0 231.7 jit_solution(16998900198718642675)
XLA Ops:
  0.7 1.2 copy-done
  1.9 0.7 copy-done.2
  2.5 0.6 shard_map.59
  3.1 11.1 %all_to_all.45.pieces = bf16[2,2,8,128,128]{4,3,2,1,0:T(8,128)(2,1)S(1)} all-to-all(bf16[2,2,8,128,128]{4,3,2,1,0:T(8,128)(2,1)S(1)} %shard_map.59), channel_id=1, replica_groups={{0,8},{16,24},{32,40},{48,56},{64,72},{80,88},{96,104},{112,120},{128,1..., dimensions={0} | all-to-all | bytes 2097152 | tf_op jit(solution)/shard_map/all_to_all | solution.py:272
  14.8 16.2 %all_to_all.46.pieces = bf16[8,2,128,128]{3,2,1,0:T(8,128)(2,1)S(1)} all-to-all(bf16[8,2,128,128]{3,2,1,0:T(8,128)(2,1)S(1)} %shard_map.60), channel_id=1, replica_groups={{0,16,32,48,64,80,96,112},{128,144,160,176,192,208,224,240},{256,272,28..., dimensions={0} | all-to-all | bytes 1048576 | tf_op jit(solution)/shard_map/all_to_all | solution.py:272
  31.7 23.8 %all_to_all.47.pieces = bf16[4,2,128,128]{3,2,1,0:T(8,128)(2,1)S(1)} all-to-all(bf16[4,2,128,128]{3,2,1,0:T(8,128)(2,1)S(1)} %shard_map.61), channel_id=1, replica_groups={{0,128,256,384},{16,144,272,400},{32,160,288,416},{48,176,304,432},{64,..., dimensions={0} | all-to-all | bytes 524288 | tf_op jit(solution)/shard_map/all_to_all | solution.py:272
  55.5 1.4 shard_map.62
  56.9 8.7 %all-to-all-start.3 = ((bf16[8,2,128,128]{3,2,1,0:T(8,128)(2,1)}), bf16[8,2,128,128]{3,2,1,0:T(8,128)(2,1)S(1)}, u32[]{:S(2)}, u32[]{:S(2)}) async-start(bf16[8,2,128,128]{3,2,1,0:T(8,128)(2,1)} %shard_map.62), calls=%async_computation.3 | async-start | bytes 1048576 | tf_op jit(solution)/shard_map/all_to_all | solution.py:272
  65.6 9.8 %all-to-all-done.3.own = bf16[8,2,128,128]{3,2,1,0:T(8,128)(2,1)S(1)} async-done(((bf16[8,2,128,128]{3,2,1,0:T(8,128)(2,1)}), bf16[8,2,128,128]{3,2,1,0:T(8,128)(2,1)S(1)}, u32[]{:S(2)}, u32[]{:S(2)}) %all-to-all-start.3) | async-done | bytes 524320 | tf_op jit(solution)/shard_map/all_to_all | solution.py:272
  75.7 5.0 %collective-permute-start = (bf16[8,2,128,128]{3,2,1,0:T(8,128)(2,1)S(1)}, bf16[8,2,128,128]{3,2,1,0:T(8,128)(2,1)S(1)}, u32[]{:S(2)}, u32[]{:S(2)}) collective-permute-start(bf16[8,2,128,128]{3,2,1,0:T(8,128)(2,1)S(1)} %all-to-all-done.3.own), channel_id=1, source_target_pairs={{0,8},{8,0},{16,24},{24,16},{32,40},{40,32},{48,56},{56,48},{64,72... | collective-permute-start | bytes 1572872 | tf_op jit(solution)/shard_map/ppermute | solution.py:284
  81.0 0.6 fusion.2.coulomb
  82.2 6.2 %forward_planes.1 = bf16[8,1040,128]{2,1,0:T(8,128)(2,1)S(1)} custom-call(s32[1]{0:T(128)} %bitcast.core, bf16[2,16,128,128]{3,2,1,0:T(8,128)(2,1)S(1)} %copy-done.1, bf16[8,2,128,128]{3,2,1,0:T(8,128)(2,1)S(1)} %all-to-all-done.3.own, bf16[8,2,128,128]{3,2,1,0:T(8,128)(2,1)S(1)} %collective-permute-done.other, bf16[4,256,256]{2,1,0:T(8,128)(2,1)S(1)} %copy-done.3), custom_call_target="tpu_custom_call" | custom-call | flops 3221225472 | bytes 5242880 | tf_op jit(solution)/shard_map/forward_planes/pallas_call | solution.py:331
  88.4 34.5 %all_to_all.48.spectrum = bf16[8,1040,128]{2,1,0:T(8,128)(2,1)S(1)} all-to-all(bf16[8,1040,128]{2,1,0:T(8,128)(2,1)S(1)} %forward_planes.1), channel_id=1, replica_groups=mesh['band'=64,'ga'=8] {'ga'}, dimensions={0} | all-to-all | bytes 4259840 | tf_op jit(solution)/shard_map/all_to_all | solution.py:280
  122.9 6.4 %coulomb_solve.1 = bf16[8,2,16,2,16,128]{5,4,3,2,1,0:T(8,128)(2,1)S(1)} custom-call(bf16[8,1040,128]{2,1,0:T(8,128)(2,1)S(1)} %all_to_all.48.spectrum, f32[16,128,128]{2,1,0:T(8,128)S(1)} %fusion.2.coulomb, bf16[4,256,256]{2,1,0:T(8,128)(2,1)S(1)} %copy-done.3), custom_call_target="tpu_custom_call" | custom-call | flops 3221225472 | bytes 5242880 | tf_op jit(solution)/shard_map/coulomb_solve/pallas_call | solution.py:339
  129.4 29.2 %all_to_all.49.solved = bf16[8,2,16,2,16,128]{5,4,3,2,1,0:T(8,128)(2,1)S(1)} all-to-all(bf16[8,2,16,2,16,128]{5,4,3,2,1,0:T(8,128)(2,1)S(1)} %coulomb_solve.1), channel_id=1, replica_groups=mesh['band'=64,'ga'=8] {'ga'}, dimensions={0} | all-to-all | bytes 4194304 | tf_op jit(solution)/shard_map/all_to_all | solution.py:280
  158.6 3.9 %backward_planes.1 = (f32[2,16,128,128]{3,2,1,0:T(8,128)}, f32[8,2,128,128]{3,2,1,0:T(8,128)S(1)}, bf16[8,2,128,128]{3,2,1,0:T(8,128)(2,1)S(1)}) custom-call(s32[1]{0:T(128)} %bitcast.core, bf16[8,2,16,2,16,128]{5,4,3,2,1,0:T(8,128)(2,1)S(1)} %all_to_all.49.solved, bf16[2,16,128,128]{3,2,1,0:T(8,128)(2,1)S(1)} %copy-done.1, ...), custom_call_target="tpu_custom_call" | custom-call | flops 3221225472 | bytes 5242880 | tf_op jit(solution)/shard_map/backward_planes/pallas_call | solution.py:349
  162.5 4.8 %collective-permute-start.1 = (bf16[8,2,128,128]{3,2,1,0:T(8,128)(2,1)S(1)}, bf16[8,2,128,128]{3,2,1,0:T(8,128)(2,1)S(1)}, u32[]{:S(2)}, u32[]{:S(2)}) collective-permute-start(bf16[8,2,128,128]{3,2,1,0:T(8,128)(2,1)S(1)} %get-tuple-element.17), channel_id=1, source_target_pairs={{0,8},{8,0},{16,24},{24,16},{32,40},{40,32},{48,56},{56,48},{64,72... | collective-permute-start | bytes 1572872 | tf_op jit(solution)/shard_map/ppermute | solution.py:284
  167.3 1.5 collective-permute-done.1
  168.9 15.6 %all_to_all.50 = bf16[8,2,128,128]{3,2,1,0:T(8,128)(2,1)S(1)} all-to-all(bf16[8,2,128,128]{3,2,1,0:T(8,128)(2,1)S(1)} %add_convert_fusion), channel_id=1, replica_groups={{0,16,32,48,64,80,96,112},{128,144,160,176,192,208,224,240},{256,272,28..., dimensions={0} | all-to-all | bytes 1048576 | tf_op jit(solution)/shard_map/all_to_all | solution.py:272
  184.7 19.2 %all_to_all.51 = bf16[4,2,128,128]{3,2,1,0:T(8,128)(2,1)S(1)} all-to-all(bf16[4,2,128,128]{3,2,1,0:T(8,128)(2,1)S(1)} %broadcast_in_dim.9), channel_id=1, replica_groups={{0,128,256,384},{16,144,272,400},{32,160,288,416},{48,176,304,432},{64,..., dimensions={0} | all-to-all | bytes 524288 | tf_op jit(solution)/shard_map/all_to_all | solution.py:272
  204.0 17.1 %all_to_all.52.own = bf16[8,2,128,128]{3,2,1,0:T(8,128)(2,1)S(1)} all-to-all(bf16[8,2,128,128]{3,2,1,0:T(8,128)(2,1)S(1)} %broadcast_in_dim.10), channel_id=1, replica_groups={{0,16,32,48,64,80,96,112},{128,144,160,176,192,208,224,240},{256,272,28..., dimensions={0} | all-to-all | bytes 1048576 | tf_op jit(solution)/shard_map/all_to_all | solution.py:272
  221.1 8.0 %collective-permute-start.2 = (bf16[8,2,128,128]{3,2,1,0:T(8,128)(2,1)S(1)}, bf16[8,2,128,128]{3,2,1,0:T(8,128)(2,1)S(1)}, u32[]{:S(2)}, u32[]{:S(2)}) collective-permute-start(bf16[8,2,128,128]{3,2,1,0:T(8,128)(2,1)S(1)} %all_to_all.52.own), channel_id=1, source_target_pairs={{0,8},{8,0},{16,24},{24,16},{32,40},{40,32},{48,56},{56,48},{64,72... | collective-permute-start | bytes 1572872 | tf_op jit(solution)/shard_map/ppermute | solution.py:284
  229.2 1.5 collective-permute-done.2.other
  230.7 1.0 shard_map.63
  (28 shorter events, 2.8 us)
Async XLA Ops:
  0.6 1.2 copy-start
  1.9 0.7 copy-start.2
  14.8 60.5 %copy-start.4 = (s32[128,128]{1,0:T(8,128)S(1)}, s32[128,128]{1,0:T(8,128)}, u32[]{:S(2)}) copy-start(s32[128,128]{1,0:T(8,128)} %param.6) | copy-start | bytes 196612
  14.8 60.6 %slice-start = ((s32[128,128]{1,0:T(8,128)}), s32[1,128]{1,0:T(1,128)S(1)}, s32[]{:S(2)}) async-start(s32[128,128]{1,0:T(8,128)} %param.6), calls=%async_computation.9 | async-start | bytes 1024 | tf_op jit(solution)/shard_map/jit(_roll_static)/slice | solution.py:309
  31.7 50.5 %copy-start.1 = (bf16[2,16,128,128]{3,2,1,0:T(8,128)(2,1)S(1)}, bf16[2,16,128,128]{3,2,1,0:T(8,128)(2,1)}, u32[]{:S(2)}) copy-start(bf16[2,16,128,128]{3,2,1,0:T(8,128)(2,1)} %values.3) | copy-start | bytes 3145732
  31.7 50.5 %copy-start.3 = (bf16[4,256,256]{2,1,0:T(8,128)(2,1)S(1)}, bf16[4,256,256]{2,1,0:T(8,128)(2,1)}, u32[]{:S(2)}) copy-start(bf16[4,256,256]{2,1,0:T(8,128)(2,1)} %constant.46.clone.tables) | copy-start | bytes 1572868
  56.9 18.5 %all-to-all-start.3 = ((bf16[8,2,128,128]{3,2,1,0:T(8,128)(2,1)}), bf16[8,2,128,128]{3,2,1,0:T(8,128)(2,1)S(1)}, u32[]{:S(2)}, u32[]{:S(2)}) async-start(bf16[8,2,128,128]{3,2,1,0:T(8,128)(2,1)} %shard_map.62), calls=%async_computation.3 | async-start | bytes 1048576 | tf_op jit(solution)/shard_map/all_to_all | solution.py:272
  75.7 6.5 %collective-permute-start = (bf16[8,2,128,128]{3,2,1,0:T(8,128)(2,1)S(1)}, bf16[8,2,128,128]{3,2,1,0:T(8,128)(2,1)S(1)}, u32[]{:S(2)}, u32[]{:S(2)}) collective-permute-start(bf16[8,2,128,128]{3,2,1,0:T(8,128)(2,1)S(1)} %all-to-all-done.3.own), channel_id=1, source_target_pairs={{0,8},{8,0},{16,24},{24,16},{32,40},{40,32},{48,56},{56,48},{64,72... | collective-permute-start | bytes 1572872 | tf_op jit(solution)/shard_map/ppermute | solution.py:284
  162.5 6.3 %collective-permute-start.1 = (bf16[8,2,128,128]{3,2,1,0:T(8,128)(2,1)S(1)}, bf16[8,2,128,128]{3,2,1,0:T(8,128)(2,1)S(1)}, u32[]{:S(2)}, u32[]{:S(2)}) collective-permute-start(bf16[8,2,128,128]{3,2,1,0:T(8,128)(2,1)S(1)} %get-tuple-element.17), channel_id=1, source_target_pairs={{0,8},{8,0},{16,24},{24,16},{32,40},{40,32},{48,56},{56,48},{64,72... | collective-permute-start | bytes 1572872 | tf_op jit(solution)/shard_map/ppermute | solution.py:284
  221.1 9.5 %collective-permute-start.2 = (bf16[8,2,128,128]{3,2,1,0:T(8,128)(2,1)S(1)}, bf16[8,2,128,128]{3,2,1,0:T(8,128)(2,1)S(1)}, u32[]{:S(2)}, u32[]{:S(2)}) collective-permute-start(bf16[8,2,128,128]{3,2,1,0:T(8,128)(2,1)S(1)} %all_to_all.52.own), channel_id=1, source_target_pairs={{0,8},{8,0},{16,24},{24,16},{32,40},{40,32},{48,56},{56,48},{64,72... | collective-permute-start | bytes 1572872 | tf_op jit(solution)/shard_map/ppermute | solution.py:284

commit v4 on v3

v4 whole, which is shorter than its diff:
```python
import functools
import math

import jax
import jax.numpy as jnp
import numpy as np
from jax import lax
from jax.experimental import pallas as pl
from jax.experimental.pallas import tpu as pltpu
from jax.sharding import PartitionSpec as P

COULOMB = math.pi / 8
GRID = 128
STEPS = 2
FIELDS = 2
ROWS = 16
CHUNK = FIELDS * ROWS * 2 * ROWS
BF16 = jnp.bfloat16
F32 = jnp.float32

SHIFT = 2


def place(z, xl, core):
    return z % 16 * 4 + xl * 2 + core


NEAR = [
    [place(4 * k + j + SHIFT * core, xl, core) for j in range(4) for xl in range(2)]
    for core in range(2)
    for k in range(4)
]
FAR = [
    [place(4 * k + j + SHIFT * core, xl, core) for k in range(4)]
    for core in range(2)
    for j in range(4)
    for xl in range(2)
]
CORES = [[2 * i, 2 * i + 1] for i in range(32)]
LINE = [group[xl::2] for group in NEAR for xl in range(2)]
VMEM = pl.BlockSpec(memory_space=pltpu.VMEM)
SMEM = pl.BlockSpec(memory_space=pltpu.SMEM)
HALF = ROWS // 2


def dft_tables():
    indices = np.arange(GRID)
    angles = (indices[:, None] * indices[None, :] % GRID) * (2.0 * np.pi / GRID)
    cosine, sine = np.cos(angles), np.sin(angles)
    matrix = np.block([[cosine, -sine], [sine, cosine]]).astype(np.float32)
    high = matrix.astype(BF16)
    low = (matrix - high.astype(np.float32)).astype(BF16)
    return np.stack([high, low, high.T, low.T])


def dot(a, b):
    return jnp.dot(a, b, preferred_element_type=F32)


def split(x):
    high = x.astype(BF16)
    return high, (x - high.astype(F32)).astype(BF16)


def right(x, tables, which):
    high, low = split(x)
    return dot(high, tables[which]) + (dot(low, tables[which]) + dot(high, tables[which + 1]))


def right_exact(x, tables, which):
    return dot(x, tables[which]) + dot(x, tables[which + 1])


def left(x, tables, which):
    high, low = split(x)
    return dot(tables[which], high) + (dot(tables[which], low) + dot(tables[which + 1], high))


def left_exact(x, tables, which):
    return dot(tables[which], x) + dot(tables[which + 1], x)


def quarter_swap(x):
    n = GRID
    return jnp.concatenate(
        [
            jnp.concatenate([x[:n, :n], x[n:, :n]], axis=1),
            jnp.concatenate([x[:n, n:], x[n:, n:]], axis=1),
        ],
        axis=0,
    )


def halves(core, own, other):
    first = core[0] * HALF
    return [(own, first), (other, HALF - first)]


def forward_kernel(core, ours, theirs, own, other, tables, out, scratch):
    n = GRID
    for f, values in enumerate((ours, theirs)):
        for owner, first in halves(core, own, other):
            for p in range(HALF // 2):
                field = owner[p].reshape(2 * n, n).astype(F32)
                pair = pl.ds(first + 2 * p, 2)
                bands = [values[band, pair].reshape(2 * n, n).astype(F32) for band in range(2)]
                density = jnp.concatenate([band * field for band in bands], axis=1)
                along_z = quarter_swap(right(density, tables, 0))
                along_y = left(along_z, tables, 2)
                start = pl.multiple_of((first + 2 * p) * n, 2 * n)
                for part in range(2):
                    rows = along_y[part * n : (part + 1) * n]
                    scratch[2 * f + part, pl.ds(start, n), :] = rows[:, :n]
                    scratch[2 * f + part, pl.ds(start + n, n), :] = rows[:, n:]

    lane = lax.broadcasted_iota(jnp.int32, (ROWS, n), 1)

    def send(j, carry):
        rest = jnp.zeros((ROWS, n), F32)
        for f in range(FIELDS):
            for k in range(ROWS):
                for part in range(2):
                    field = 2 * f + part
                    tile = scratch[field, pl.ds(j * ROWS + k, ROWS, stride=n), :]
                    high = tile.astype(BF16)
                    row = ((f * ROWS + k) * 2 + part) * ROWS
                    out[j, row : row + ROWS] = high
                    if k == 0:
                        low = tile - high.astype(F32)
                        below = low - low.astype(BF16).astype(F32)
                        rest = jnp.where(lane == field, low[:, :1], rest)
                        rest = jnp.where(lane == field + 2 * FIELDS, below[:, :1], rest)
        out[j, CHUNK:] = rest.astype(BF16)
        return carry

    lax.fori_loop(0, n // ROWS, send, 0)


def solve_kernel(spectrum, coulomb, tables, out, scratch):
    n = GRID
    rest = spectrum[:, CHUNK:].reshape(n, n).astype(F32)
    lane = lax.broadcasted_iota(jnp.int32, (n, n), 1)
    dropped = coulomb[0, :1, :1] == 0.0
    for f in range(FIELDS):

        def pick(k):
            row = (f * ROWS + k) * 2 * ROWS
            ends = [row + part * ROWS for part in range(2)]
            return [spectrum[:, end : end + ROWS].reshape(n, n) for end in ends]

        def factor(q):
            pair = jnp.concatenate([coulomb[2 * q], coulomb[2 * q + 1]], axis=1)
            return jnp.concatenate([pair, pair], axis=0)

        def inverse(x):
            return left_exact(x.astype(BF16), tables, 0)

        def keep(q, solved):
            start = q * 4 * n
            scratch[start : start + 2 * n] = solved[:, :n]
            scratch[start + 2 * n : start + 4 * n] = solved[:, n:]

        def columns(q):
            both = jnp.concatenate(
                [jnp.concatenate(pick(2 * q), axis=0), jnp.concatenate(pick(2 * q + 1), axis=0)],
                axis=1,
            )
            keep(q, inverse(left_exact(both, tables, 2) * factor(q)))

        parts = []
        for part, tile in enumerate(pick(0)):
            tile, field = tile.astype(F32), 2 * f + part
            low = rest[:, field : field + 1] + rest[:, field + 2 * FIELDS : field + 2 * FIELDS + 1]
            column = tile[:, :1] + low
            mean = jnp.sum(column, axis=0, keepdims=True) * (1.0 / n)
            column = column - jnp.where(dropped, mean, 0.0)
            parts.append(jnp.where(lane == 0, column, tile))
        both = jnp.concatenate(
            [jnp.concatenate(parts, axis=0), jnp.concatenate(pick(1), axis=0).astype(F32)], axis=1
        )
        keep(0, inverse(left(both, tables, 2) * factor(0)))
        for q in range(1, ROWS // 2):
            columns(q)

        def send(i, carry):
            for x in range(ROWS):
                for part in range(2):
                    tile = scratch[pl.ds(part * n + i * ROWS + x, ROWS, stride=2 * n), :]
                    out[i, f, x, part] = tile.astype(BF16)
            return carry

        lax.fori_loop(0, n // ROWS, send, 0)


def backward_kernel(core, solved, ours, theirs, own, other, tables, exchange, passed, keep, send):
    n = GRID
    for (owner, first), terms in zip(halves(core, own, other), (keep, send)):
        for p in range(HALF // 2):
            pair = pl.ds(first + 2 * p, 2)
            field = owner[p].reshape(2 * n, n).astype(F32)
            term = 0.0
            for f, (values, shares) in enumerate(((ours, exchange), (theirs, passed))):

                def pick(x):
                    parts = [solved[:, f, x, part].reshape(n, n) for part in range(2)]
                    return jnp.concatenate(parts, axis=0)

                both = jnp.concatenate([pick(first + 2 * p), pick(first + 2 * p + 1)], axis=1)
                along_y = quarter_swap(left_exact(both, tables, 0))
                potential = right_exact(along_y.astype(BF16), tables, 2)
                for band in range(2):
                    part = potential[:, band * n : (band + 1) * n]
                    share = (part * field).astype(shares.dtype)
                    shares[band, pair] = share.reshape(2, n, n)
                    term = term + part * values[band, pair].reshape(2 * n, n).astype(F32)
            terms[p] = term.astype(terms.dtype).reshape(2, n, n)


def pick_slot(owners, core, orbitals, out):
    for s in range(STEPS):
        slot = lax.rem(owners[s], 2)
        for half in range(2):
            out[half, s] = orbitals[slot, half * HALF : (half + 1) * HALF]


def pick_core(owners, core, pieces, out):
    for s in range(STEPS):
        root = lax.rem(lax.div(owners[s], 2), 2)
        for x in range(HALF // 2):
            out[2 * x + s] = pieces[root, s, 2 * x : 2 * x + 2]


def root_z(owner, core):
    return lax.rem(lax.div(owner, 8) + 16 - SHIFT * core, 16)


def pick_near(owners, core, step, pieces, out):
    owner = owners[step[0]]
    z, xl = root_z(owner, core[0]), lax.rem(lax.div(owner, 4), 2)
    piece = pieces[lax.rem(z, 4) * 2 + xl]
    for copy in range(out.shape[0]):
        out[copy] = piece


def pick_far(owners, core, step, pieces, out):
    piece = pieces[lax.div(root_z(owners[step[0]], core[0]), 4)]
    for copy in range(out.shape[0]):
        out[copy] = piece


def assemble(core, own, other, out):
    for half, first in halves(core, own, other):
        for s in range(STEPS):
            for x in range(HALF // 2):
                out[s, pl.ds(first + 2 * x, 2)] = half[2 * x + s]


def call(kernel, outs, scratch, flops, scalars=1, operands=4):
    return pl.pallas_call(
        kernel,
        out_shape=outs,
        in_specs=[SMEM] * scalars + [VMEM] * operands,
        scratch_shapes=scratch,
        compiler_params=pltpu.CompilerParams(vmem_limit_bytes=40 * 1024 * 1024),
        cost_estimate=pl.CostEstimate(flops=flops, bytes_accessed=5 << 20, transcendentals=0),
    )


def exchange_all(x, groups):
    return lax.all_to_all(x, "band", 0, 0, axis_index_groups=groups, tiled=True)


def gather_all(x, groups):
    return exchange_all(jnp.broadcast_to(x[None], (len(groups[0]),) + x.shape), groups)


def exchange_slabs(x):
    return lax.all_to_all(x, "ga", 0, 0, tiled=True)


def swap(x, bit):
    return lax.ppermute(x, "band", [(i, i ^ bit) for i in range(64)])


def pick(kernel, shape, scalars, pieces):
    outs = jax.ShapeDtypeStruct(shape + (GRID, GRID), BF16)
    return call(kernel, outs, [], 1 << 20, scalars=len(scalars), operands=1)(*scalars, pieces)


def spread_owners(orbitals, owners, core, step):
    piece = pick(pick_slot, (2, STEPS, HALF), (owners, core), orbitals)
    piece = lax.all_to_all(piece, "band", 0, 0, axis_index_groups=CORES, tiled=True)
    piece = exchange_all(pick(pick_core, (8, 2), (owners, core), piece), NEAR)
    orbitals, piece = lax.optimization_barrier((orbitals, piece))
    theirs = swap(orbitals, 2)
    piece = exchange_all(pick(pick_near, (4, 2), (owners, core, step), piece), FAR)
    theirs, piece = lax.optimization_barrier((theirs, piece))
    piece = exchange_all(pick(pick_far, (4, 2), (owners, core, step), piece), LINE)
    return theirs, piece


def total_terms(keep, send, passed):
    piece = (keep + swap(send, 1).astype(F32)).astype(BF16)
    piece = jnp.sum(exchange_all(piece, LINE).astype(F32), axis=0).astype(BF16)
    passed, piece = lax.optimization_barrier((passed, piece))
    passed = swap(passed, 2)
    piece = jnp.sum(gather_all(piece, FAR).astype(F32), axis=0).astype(BF16)
    passed, piece = lax.optimization_barrier((passed, piece))
    own = gather_all(piece, NEAR)
    return own, swap(own, 1), passed


def coulomb_slab(cutoff, first_row):
    mirrored = jnp.roll(cutoff[::-1, ::-1], (1, 1), (0, 1))
    limits = lax.dynamic_slice_in_dim(jnp.minimum(cutoff, mirrored), first_row, ROWS, 1).T
    full = jnp.arange(GRID, dtype=jnp.int32)
    signed = jnp.where(full < GRID // 2, full, full - GRID)
    own = first_row + jnp.arange(ROWS, dtype=jnp.int32)
    own = jnp.where(own < GRID // 2, own, own - GRID)
    squared = own[:, None, None] ** 2 + signed[None, :, None] ** 2 + signed[None, None, :] ** 2
    inside = (jnp.abs(signed)[None, None, :] <= limits[:, :, None]) & (squared > 0)
    scale = COULOMB * float(GRID) ** 1.5 / float(GRID) ** 3
    return jnp.where(inside, scale / jnp.maximum(squared, 1).astype(F32), 0.0)


def shards(orbitals, owners, cutoff):
    first_row = lax.axis_index("ga") * ROWS
    tables = jnp.asarray(dft_tables())
    band = lax.axis_index("band")
    core = (band % 2).astype(jnp.int32).reshape(1)
    step = (band // 2 % 2).astype(jnp.int32).reshape(1)
    theirs, own = spread_owners(orbitals, owners, core, step)
    cutoff, first_row, own = lax.optimization_barrier((cutoff, first_row, own))
    other = swap(own, 1)
    coulomb, other = lax.optimization_barrier((coulomb_slab(cutoff, first_row), other))
    flops = 2 * 2 * FIELDS * 3 * 8 * 256**3
    with jax.named_scope("forward_planes"):
        spectrum = call(
            forward_kernel,
            jax.ShapeDtypeStruct((8, CHUNK + ROWS, GRID), BF16),
            [pltpu.VMEM((2 * FIELDS, ROWS * GRID, GRID), F32)],
            flops,
            operands=5,
        )(core, orbitals, theirs, own, other, tables)
    spectrum = exchange_slabs(spectrum)
    with jax.named_scope("coulomb_solve"):
        solved = call(
            solve_kernel,
            jax.ShapeDtypeStruct((8, FIELDS, ROWS, 2, ROWS, GRID), BF16),
            [pltpu.VMEM((ROWS * 2 * GRID, GRID), F32)],
            flops,
            scalars=0,
            operands=3,
        )(spectrum, coulomb, tables)
    solved = exchange_slabs(solved)
    slab = (2, ROWS, GRID, GRID)
    half = (HALF // 2, 2, GRID, GRID)
    with jax.named_scope("backward_planes"):
        exchange, passed, keep, send = call(
            backward_kernel,
            tuple(
                jax.ShapeDtypeStruct(shape, kind)
                for shape, kind in ((slab, F32), (slab, BF16), (half, F32), (half, BF16))
            ),
            [],
            flops,
            operands=6,
        )(core, solved, orbitals, theirs, own, other, tables)
    own, other, passed = total_terms(keep, send, passed)
    outs = jax.ShapeDtypeStruct((STEPS, ROWS, GRID, GRID), BF16)
    total = call(assemble, outs, [], 1 << 20, operands=2)(core, own, other)
    return exchange + passed.astype(F32), total


def solution(mesh):
    return jax.shard_map(
        shards,
        mesh=mesh,
        in_specs=(P("band", "ga", None, None), P(), P()),
        out_specs=(P("band", "ga", None, None), P(None, "ga", None, None)),
        check_vma=False,
    )
```

time: 232 us -> 227 us (0.978)
  blocking collectives: 167 us -> 159 us
  starting transfers between devices: 26.4 us -> 31.8 us
  waiting for transfers between devices: 13.4 us -> 10.2 us
    all_to_all x6 -> x5, blocking collectives: 103 us -> 83.8 us  [exchange_all(): return lax.all_to_all(x, 'band', 0, 0, axis_index_groups=groups, tiled=True)]
    all_to_all x0 -> x1, blocking collectives: none -> 11.2 us  [spread_owners(): lax.all_to_all(piece, 'band', 0, 0, axis_index_groups=CORES, tiled=True)]
    ppermute x3 -> x5, starting transfers between devices: 17.8 us -> 23.9 us  [swap(): return lax.ppermute(x, 'band', [(i, i ^ bit) for i in range(64)])]
    all_to_all x1, waiting for transfers between devices: 9.78 us -> 3.96 us  [exchange_all(): return lax.all_to_all(x, 'band', 0, 0, axis_index_groups=groups, tiled=True)]
    ppermute x3 -> x5, waiting for transfers between devices: 3.64 us -> 6.21 us  [swap(): return lax.ppermute(x, 'band', [(i, i ^ bit) for i in range(64)])]
  transfers between devices with their start and end apart: 4 -> 6, of which waited for: 4 -> 5; matrix products, arithmetic and copies ran while one was open for 0% -> 1% of each run, Pallas kernels for 0% -> 0%
where the time goes in v4:
time: 227 us; the launch traced here: 226 us
  blocking collectives  159 us (70%)
  starting transfers between devices  31.8 us (14%)
  Pallas kernels  19.4 us (9%)
  waiting for transfers between devices  10.2 us (4%)
  other arithmetic  2.63 us (1%)
  local copies, waits for them, and re-layouts  2.34 us (1%)
    all_to_all x5, blocking collectives, exchange_all(): return lax.all_to_all(x, 'band', 0, 0, axis_index_groups=groups, tiled=True)  83.8 us
    all_to_all x2, blocking collectives, exchange_slabs(): return lax.all_to_all(x, 'ga', 0, 0, tiled=True)  63.8 us
    ppermute x5, starting transfers between devices, swap(): return lax.ppermute(x, 'band', [(i, i ^ bit) for i in range(64)])  23.9 us
    all_to_all x1, blocking collectives, spread_owners(): lax.all_to_all(piece, 'band', 0, 0, axis_index_groups=CORES, tiled=True)  11.2 us
    all_to_all x1, starting transfers between devices, exchange_all(): return lax.all_to_all(x, 'band', 0, 0, axis_index_groups=groups, tiled=True)  7.9 us
    pallas_call x1, Pallas kernels, shards(): call(solve_kernel, jax.ShapeDtypeStruct((8, FIELDS, ROWS, 2, ROWS, GRID),...  6.43 us
    pallas_call x1, Pallas kernels, shards(): call(forward_kernel, jax.ShapeDtypeStruct((8, CHUNK + ROWS, GRID), BF16),...  6.24 us
    ppermute x5, waiting for transfers between devices, swap(): return lax.ppermute(x, 'band', [(i, i ^ bit) for i in range(64)])  6.21 us
  transfers between devices with their start and end apart: 6, of which 5 were waited for; matrix products, arithmetic and copies ran while one was open for 1% of the time, Pallas kernels for 0%

profile of v4, /device:TPU:1, one launch (start us, length us, event | category | flops | bytes accessed | tf_op | source)
XLA Modules:
  0.0 226.2 jit_solution(7479313608080898561)
XLA Ops:
  0.7 1.2 copy-done
  3.2 11.2 %all_to_all.45.pieces = bf16[2,2,8,128,128]{4,3,2,1,0:T(8,128)(2,1)S(1)} all-to-all(bf16[2,2,8,128,128]{4,3,2,1,0:T(8,128)(2,1)S(1)} %shard_map.59), channel_id=1, replica_groups={{0,8},{16,24},{32,40},{48,56},{64,72},{80,88},{96,104},{112,120},{128,1..., dimensions={0} | all-to-all | bytes 2097152 | tf_op jit(solution)/shard_map/all_to_all | solution.py:292
  15.0 16.2 %all_to_all.46.pieces = bf16[8,2,128,128]{3,2,1,0:T(8,128)(2,1)S(1)} all-to-all(bf16[8,2,128,128]{3,2,1,0:T(8,128)(2,1)S(1)} %shard_map.60), channel_id=1, replica_groups={{0,16,32,48,64,80,96,112},{128,144,160,176,192,208,224,240},{256,272,28..., dimensions={0} | all-to-all | bytes 1048576 | tf_op jit(solution)/shard_map/all_to_all | solution.py:270
  31.2 3.0 %collective-permute-start = (bf16[2,16,128,128]{3,2,1,0:T(8,128)(2,1)S(1)}, bf16[2,16,128,128]{3,2,1,0:T(8,128)(2,1)S(1)}, u32[]{:S(2)}, u32[]{:S(2)}) collective-permute-start(bf16[2,16,128,128]{3,2,1,0:T(8,128)(2,1)S(1)} %copy-done.1), channel_id=1, source_target_pairs={{0,16},{8,24},{16,0},{24,8},{32,48},{40,56},{48,32},{56,40},{64,80... | collective-permute-start | bytes 3145736 | tf_op jit(solution)/shard_map/ppermute | solution.py:282
  34.9 22.3 %all_to_all.47.pieces = bf16[4,2,128,128]{3,2,1,0:T(8,128)(2,1)S(1)} all-to-all(bf16[4,2,128,128]{3,2,1,0:T(8,128)(2,1)S(1)} %shard_map.61), channel_id=1, replica_groups={{0,128,256,384},{16,144,272,400},{32,160,288,416},{48,176,304,432},{64,..., dimensions={0} | all-to-all | bytes 524288 | tf_op jit(solution)/shard_map/all_to_all | solution.py:270
  57.5 1.3 shard_map.62
  58.8 7.9 %all-to-all-start.3 = ((bf16[4,2,128,128]{3,2,1,0:T(8,128)(2,1)}), bf16[4,2,128,128]{3,2,1,0:T(8,128)(2,1)S(1)}, u32[]{:S(2)}, u32[]{:S(2)}) async-start(bf16[4,2,128,128]{3,2,1,0:T(8,128)(2,1)} %shard_map.62), calls=%async_computation.3 | async-start | bytes 524288 | tf_op jit(solution)/shard_map/all_to_all | solution.py:270
  66.7 4.0 %all-to-all-done.3.own = bf16[4,2,128,128]{3,2,1,0:T(8,128)(2,1)S(1)} async-done(((bf16[4,2,128,128]{3,2,1,0:T(8,128)(2,1)}), bf16[4,2,128,128]{3,2,1,0:T(8,128)(2,1)S(1)}, u32[]{:S(2)}, u32[]{:S(2)}) %all-to-all-start.3) | async-done | bytes 262176 | tf_op jit(solution)/shard_map/all_to_all | solution.py:270
  71.0 6.5 %collective-permute-start.1 = (bf16[4,2,128,128]{3,2,1,0:T(8,128)(2,1)S(1)}, bf16[4,2,128,128]{3,2,1,0:T(8,128)(2,1)S(1)}, u32[]{:S(2)}, u32[]{:S(2)}) collective-permute-start(bf16[4,2,128,128]{3,2,1,0:T(8,128)(2,1)S(1)} %all-to-all-done.3.own), channel_id=1, source_target_pairs={{0,8},{8,0},{16,24},{24,16},{32,40},{40,32},{48,56},{56,48},{64,72... | collective-permute-start | bytes 786440 | tf_op jit(solution)/shard_map/ppermute | solution.py:282
  78.7 6.2 %forward_planes.1 = bf16[8,1040,128]{2,1,0:T(8,128)(2,1)S(1)} custom-call(s32[1]{0:T(128)} %bitcast.core, bf16[2,16,128,128]{3,2,1,0:T(8,128)(2,1)S(1)} %copy-done.1, bf16[2,16,128,128]{3,2,1,0:T(8,128)(2,1)S(1)} %collective-permute-done.theirs, bf16[4,2,128,128]{3,2,1,0:T(8,128)(2,1)S(1)} %all-to-all-done.3.own, ...), custom_call_target="tpu_custom_call" | custom-call | flops 3221225472 | bytes 5242880 | tf_op jit(solution)/shard_map/forward_planes/pallas_call | solution.py:338
  85.0 34.5 %all_to_all.48.spectrum = bf16[8,1040,128]{2,1,0:T(8,128)(2,1)S(1)} all-to-all(bf16[8,1040,128]{2,1,0:T(8,128)(2,1)S(1)} %forward_planes.1), channel_id=1, replica_groups=mesh['band'=64,'ga'=8] {'ga'}, dimensions={0} | all-to-all | bytes 4259840 | tf_op jit(solution)/shard_map/all_to_all | solution.py:278
  119.5 6.4 %coulomb_solve.1 = bf16[8,2,16,2,16,128]{5,4,3,2,1,0:T(8,128)(2,1)S(1)} custom-call(bf16[8,1040,128]{2,1,0:T(8,128)(2,1)S(1)} %all_to_all.48.spectrum, f32[16,128,128]{2,1,0:T(8,128)S(1)} %fusion.2.coulomb, bf16[4,256,256]{2,1,0:T(8,128)(2,1)S(1)} %copy-done.9), custom_call_target="tpu_custom_call" | custom-call | flops 3221225472 | bytes 5242880 | tf_op jit(solution)/shard_map/coulomb_solve/pallas_call | solution.py:347
  125.9 29.3 %all_to_all.49.solved = bf16[8,2,16,2,16,128]{5,4,3,2,1,0:T(8,128)(2,1)S(1)} all-to-all(bf16[8,2,16,2,16,128]{5,4,3,2,1,0:T(8,128)(2,1)S(1)} %coulomb_solve.1), channel_id=1, replica_groups=mesh['band'=64,'ga'=8] {'ga'}, dimensions={0} | all-to-all | bytes 4194304 | tf_op jit(solution)/shard_map/all_to_all | solution.py:278
  155.3 2.7 %backward_planes.1 = (f32[2,16,128,128]{3,2,1,0:T(8,128)S(1)}, bf16[2,16,128,128]{3,2,1,0:T(8,128)(2,1)S(1)}, f32[4,2,128,128]{3,2,1,0:T(8,128)S(1)}, bf16[4,2,128,128]{3,2,1,0:T(8,128)(2,1)S(1)}) custom-call(s32[1]{0:T(128)} %bitcast.core, bf16[8,2,16,2,16,128]{5,4,3,2,1,0:T(8,128)(2,1)S(1)} %all_to_all.49.solved, bf16[2,16,128,128]{3,2,1,0:T(8,128)(2,1)S(1)} %copy-done.1, ...), custom_call_target="tpu_custom_call" | custom-call | flops 3221225472 | bytes 5242880 | tf_op jit(solution)/shard_map/backward_planes/pallas_call | solution.py:359
  158.0 4.8 %collective-permute-start.2 = (bf16[4,2,128,128]{3,2,1,0:T(8,128)(2,1)S(1)}, bf16[4,2,128,128]{3,2,1,0:T(8,128)(2,1)S(1)}, u32[]{:S(2)}, u32[]{:S(2)}) collective-permute-start(bf16[4,2,128,128]{3,2,1,0:T(8,128)(2,1)S(1)} %get-tuple-element.31), channel_id=1, source_target_pairs={{0,8},{8,0},{16,24},{24,16},{32,40},{40,32},{48,56},{56,48},{64,72... | collective-permute-start | bytes 786440 | tf_op jit(solution)/shard_map/ppermute | solution.py:282
  162.7 1.1 collective-permute-done.2
  164.0 12.7 %all_to_all.50 = bf16[4,2,128,128]{3,2,1,0:T(8,128)(2,1)S(1)} all-to-all(bf16[4,2,128,128]{3,2,1,0:T(8,128)(2,1)S(1)} %add_convert_fusion), channel_id=1, replica_groups={{0,32,64,96},{16,48,80,112},{128,160,192,224},{144,176,208,240},{256,28..., dimensions={0} | all-to-all | bytes 524288 | tf_op jit(solution)/shard_map/all_to_all | solution.py:270
  176.7 1.9 collective-permute-start.3
  178.7 18.8 %all_to_all.51 = bf16[4,2,128,128]{3,2,1,0:T(8,128)(2,1)S(1)} all-to-all(bf16[4,2,128,128]{3,2,1,0:T(8,128)(2,1)S(1)} %broadcast_in_dim.9), channel_id=1, replica_groups={{0,128,256,384},{16,144,272,400},{32,160,288,416},{48,176,304,432},{64,..., dimensions={0} | all-to-all | bytes 524288 | tf_op jit(solution)/shard_map/all_to_all | solution.py:270
  197.6 4.5 %collective-permute-done.3 = bf16[2,16,128,128]{3,2,1,0:T(8,128)(2,1)S(1)} collective-permute-done((bf16[2,16,128,128]{3,2,1,0:T(8,128)(2,1)}, bf16[2,16,128,128]{3,2,1,0:T(8,128)(2,1)S(1)}, u32[]{:S(2)}, u32[]{:S(2)}) %collective-permute-start.3) | collective-permute-done | bytes 1048608 | tf_op jit(solution)/shard_map/ppermute | solution.py:282
  202.2 13.7 %all_to_all.52.own = bf16[8,2,128,128]{3,2,1,0:T(8,128)(2,1)S(1)} all-to-all(bf16[8,2,128,128]{3,2,1,0:T(8,128)(2,1)S(1)} %broadcast_in_dim.10), channel_id=1, replica_groups={{0,16,32,48,64,80,96,112},{128,144,160,176,192,208,224,240},{256,272,28..., dimensions={0} | all-to-all | bytes 1048576 | tf_op jit(solution)/shard_map/all_to_all | solution.py:270
  215.9 7.7 %collective-permute-start.4 = (bf16[8,2,128,128]{3,2,1,0:T(8,128)(2,1)S(1)}, bf16[8,2,128,128]{3,2,1,0:T(8,128)(2,1)S(1)}, u32[]{:S(2)}, u32[]{:S(2)}) collective-permute-start(bf16[8,2,128,128]{3,2,1,0:T(8,128)(2,1)S(1)} %all_to_all.52.own), channel_id=1, source_target_pairs={{0,8},{8,0},{16,24},{24,16},{32,40},{40,32},{48,56},{56,48},{64,72... | collective-permute-start | bytes 1572872 | tf_op jit(solution)/shard_map/ppermute | solution.py:282
  223.6 1.6 convert_add_fusion
  225.2 1.0 shard_map.63
  (47 shorter events, 4.5 us)
Async XLA Ops:
  0.6 1.2 copy-start
  1.9 0.7 copy-start.2
  3.1 28.1 %copy-start.1 = (bf16[2,16,128,128]{3,2,1,0:T(8,128)(2,1)S(1)}, bf16[2,16,128,128]{3,2,1,0:T(8,128)(2,1)}, u32[]{:S(2)}) copy-start(bf16[2,16,128,128]{3,2,1,0:T(8,128)(2,1)} %ours.3) | copy-start | bytes 3145732
  3.2 31.1 %copy-start.3 = (s32[2]{0:T(128)S(1)}, s32[2]{0:T(128)}, u32[]{:S(2)}) copy-start(s32[2]{0:T(128)} %owners.7) | copy-start | bytes 28
  15.0 55.7 %copy-start.11 = (s32[128,128]{1,0:T(8,128)S(1)}, s32[128,128]{1,0:T(8,128)}, u32[]{:S(2)}) copy-start(s32[128,128]{1,0:T(8,128)} %param.6) | copy-start | bytes 196612
  15.0 55.7 %slice-start = ((s32[128,128]{1,0:T(8,128)}), s32[1,128]{1,0:T(1,128)S(1)}, s32[]{:S(2)}) async-start(s32[128,128]{1,0:T(8,128)} %param.6), calls=%async_computation.9 | async-start | bytes 1024 | tf_op jit(solution)/shard_map/jit(_roll_static)/slice | solution.py:314
  31.2 26.3 %collective-permute-start = (bf16[2,16,128,128]{3,2,1,0:T(8,128)(2,1)S(1)}, bf16[2,16,128,128]{3,2,1,0:T(8,128)(2,1)S(1)}, u32[]{:S(2)}, u32[]{:S(2)}) collective-permute-start(bf16[2,16,128,128]{3,2,1,0:T(8,128)(2,1)S(1)} %copy-done.1), channel_id=1, source_target_pairs={{0,16},{8,24},{16,0},{24,8},{32,48},{40,56},{48,32},{56,40},{64,80... | collective-permute-start | bytes 3145736 | tf_op jit(solution)/shard_map/ppermute | solution.py:282
  34.9 43.8 %copy-start.9 = (bf16[4,256,256]{2,1,0:T(8,128)(2,1)S(1)}, bf16[4,256,256]{2,1,0:T(8,128)(2,1)}, u32[]{:S(2)}) copy-start(bf16[4,256,256]{2,1,0:T(8,128)(2,1)} %constant.61.clone.tables) | copy-start | bytes 1572868
  57.5 27.5 %copy-start.4 = (bf16[2,16,128,128]{3,2,1,0:T(8,128)(2,1)}, bf16[2,16,128,128]{3,2,1,0:T(8,128)(2,1)S(1)}, u32[]{:S(2)}) copy-start(bf16[2,16,128,128]{3,2,1,0:T(8,128)(2,1)S(1)} %collective-permute-done.theirs) | copy-start | bytes 3145732
  58.8 11.9 %all-to-all-start.3 = ((bf16[4,2,128,128]{3,2,1,0:T(8,128)(2,1)}), bf16[4,2,128,128]{3,2,1,0:T(8,128)(2,1)S(1)}, u32[]{:S(2)}, u32[]{:S(2)}) async-start(bf16[4,2,128,128]{3,2,1,0:T(8,128)(2,1)} %shard_map.62), calls=%async_computation.3 | async-start | bytes 524288 | tf_op jit(solution)/shard_map/all_to_all | solution.py:270
  71.0 7.7 %collective-permute-start.1 = (bf16[4,2,128,128]{3,2,1,0:T(8,128)(2,1)S(1)}, bf16[4,2,128,128]{3,2,1,0:T(8,128)(2,1)S(1)}, u32[]{:S(2)}, u32[]{:S(2)}) collective-permute-start(bf16[4,2,128,128]{3,2,1,0:T(8,128)(2,1)S(1)} %all-to-all-done.3.own), channel_id=1, source_target_pairs={{0,8},{8,0},{16,24},{24,16},{32,40},{40,32},{48,56},{56,48},{64,72... | collective-permute-start | bytes 786440 | tf_op jit(solution)/shard_map/ppermute | solution.py:282
  78.7 6.3 %copy-start.7 = (bf16[4,2,128,128]{3,2,1,0:T(8,128)(2,1)}, bf16[4,2,128,128]{3,2,1,0:T(8,128)(2,1)S(1)}, u32[]{:S(2)}) copy-start(bf16[4,2,128,128]{3,2,1,0:T(8,128)(2,1)S(1)} %collective-permute-done.1.other) | copy-start | bytes 786436
  125.9 29.4 %copy-start.5 = (bf16[2,16,128,128]{3,2,1,0:T(8,128)(2,1)S(1)}, bf16[2,16,128,128]{3,2,1,0:T(8,128)(2,1)}, u32[]{:S(2)}) copy-start(bf16[2,16,128,128]{3,2,1,0:T(8,128)(2,1)} %copy-done.4) | copy-start | bytes 3145732
  125.9 29.4 %copy-start.8 = (bf16[4,2,128,128]{3,2,1,0:T(8,128)(2,1)S(1)}, bf16[4,2,128,128]{3,2,1,0:T(8,128)(2,1)}, u32[]{:S(2)}) copy-start(bf16[4,2,128,128]{3,2,1,0:T(8,128)(2,1)} %copy-done.7) | copy-start | bytes 786436
  125.9 29.4 %copy-start.10 = (bf16[4,256,256]{2,1,0:T(8,128)(2,1)S(1)}, bf16[4,256,256]{2,1,0:T(8,128)(2,1)}, u32[]{:S(2)}) copy-start(bf16[4,256,256]{2,1,0:T(8,128)(2,1)} %constant.61.clone.tables) | copy-start | bytes 1572868
  157.9 6.0 %copy-start.6 = (bf16[2,16,128,128]{3,2,1,0:T(8,128)(2,1)}, bf16[2,16,128,128]{3,2,1,0:T(8,128)(2,1)S(1)}, u32[]{:S(2)}) copy-start(bf16[2,16,128,128]{3,2,1,0:T(8,128)(2,1)S(1)} %get-tuple-element.32) | copy-start | bytes 3145732
  158.0 5.9 %collective-permute-start.2 = (bf16[4,2,128,128]{3,2,1,0:T(8,128)(2,1)S(1)}, bf16[4,2,128,128]{3,2,1,0:T(8,128)(2,1)S(1)}, u32[]{:S(2)}, u32[]{:S(2)}) collective-permute-start(bf16[4,2,128,128]{3,2,1,0:T(8,128)(2,1)S(1)} %get-tuple-element.31), channel_id=1, source_target_pairs={{0,8},{8,0},{16,24},{24,16},{32,40},{40,32},{48,56},{56,48},{64,72... | collective-permute-start | bytes 786440 | tf_op jit(solution)/shard_map/ppermute | solution.py:282
  176.7 25.4 %collective-permute-start.3 = (bf16[2,16,128,128]{3,2,1,0:T(8,128)(2,1)}, bf16[2,16,128,128]{3,2,1,0:T(8,128)(2,1)S(1)}, u32[]{:S(2)}, u32[]{:S(2)}) collective-permute-start(bf16[2,16,128,128]{3,2,1,0:T(8,128)(2,1)} %copy-done.6), channel_id=1, source_target_pairs={{0,16},{8,24},{16,0},{24,8},{32,48},{40,56},{48,32},{56,40},{64,80... | collective-permute-start | bytes 3145736 | tf_op jit(solution)/shard_map/ppermute | solution.py:282
  215.9 9.3 %collective-permute-start.4 = (bf16[8,2,128,128]{3,2,1,0:T(8,128)(2,1)S(1)}, bf16[8,2,128,128]{3,2,1,0:T(8,128)(2,1)S(1)}, u32[]{:S(2)}, u32[]{:S(2)}) collective-permute-start(bf16[8,2,128,128]{3,2,1,0:T(8,128)(2,1)S(1)} %all_to_all.52.own), channel_id=1, source_target_pairs={{0,8},{8,0},{16,24},{24,16},{32,40},{40,32},{48,56},{56,48},{64,72... | collective-permute-start | bytes 1572872 | tf_op jit(solution)/shard_map/ppermute | solution.py:282

commit v5 on v4

--- a/solution.py
+++ b/solution.py
@@ -14,6 +14,8 @@
 STEPS = 2
 FIELDS = 2
 ROWS = 16
+PLANE = GRID + 4
+PAIR = 2 * GRID + 4
 CHUNK = FIELDS * ROWS * 2 * ROWS
 BF16 = jnp.bfloat16
 F32 = jnp.float32
@@ -107,11 +109,11 @@
                 density = jnp.concatenate([band * field for band in bands], axis=1)
                 along_z = quarter_swap(right(density, tables, 0))
                 along_y = left(along_z, tables, 2)
-                start = pl.multiple_of((first + 2 * p) * n, 2 * n)
+                start = pl.multiple_of((first + 2 * p) * PLANE, 8)
                 for part in range(2):
                     rows = along_y[part * n : (part + 1) * n]
                     scratch[2 * f + part, pl.ds(start, n), :] = rows[:, :n]
-                    scratch[2 * f + part, pl.ds(start + n, n), :] = rows[:, n:]
+                    scratch[2 * f + part, pl.ds(start + PLANE, n), :] = rows[:, n:]
 
     lane = lax.broadcasted_iota(jnp.int32, (ROWS, n), 1)
 
@@ -121,7 +123,7 @@
             for k in range(ROWS):
                 for part in range(2):
                     field = 2 * f + part
-                    tile = scratch[field, pl.ds(j * ROWS + k, ROWS, stride=n), :]
+                    tile = scratch[field, pl.ds(j * ROWS + k, ROWS, stride=PLANE), :]
                     high = tile.astype(BF16)
                     row = ((f * ROWS + k) * 2 + part) * ROWS
                     out[j, row : row + ROWS] = high
@@ -156,9 +158,9 @@
             return left_exact(x.astype(BF16), tables, 0)
 
         def keep(q, solved):
-            start = q * 4 * n
+            start = q * 2 * PAIR
             scratch[start : start + 2 * n] = solved[:, :n]
-            scratch[start + 2 * n : start + 4 * n] = solved[:, n:]
+            scratch[start + PAIR : start + PAIR + 2 * n] = solved[:, n:]
 
         def columns(q):
             both = jnp.concatenate(
@@ -185,7 +187,7 @@
         def send(i, carry):
             for x in range(ROWS):
                 for part in range(2):
-                    tile = scratch[pl.ds(part * n + i * ROWS + x, ROWS, stride=2 * n), :]
+                    tile = scratch[pl.ds(part * n + i * ROWS + x, ROWS, stride=PAIR), :]
                     out[i, f, x, part] = tile.astype(BF16)
             return carry
 
@@ -216,11 +218,16 @@
             terms[p] = term.astype(terms.dtype).reshape(2, n, n)
 
 
-def pick_slot(owners, core, orbitals, out):
+def pick_slot(owners, core, step, first_row, orbitals, out, sems):
+    copies = []
     for s in range(STEPS):
         slot = lax.rem(owners[s], 2)
         for half in range(2):
-            out[half, s] = orbitals[slot, half * HALF : (half + 1) * HALF]
+            piece = orbitals.at[slot, pl.ds(half * HALF, HALF)]
+            copies.append(pltpu.make_async_copy(piece, out.at[half, s], sems.at[s, half]))
+            copies[-1].start()
+    for copy in copies:
+        copy.wait()
 
 
 def pick_core(owners, core, pieces, out):
@@ -261,7 +268,7 @@
         out_shape=outs,
         in_specs=[SMEM] * scalars + [VMEM] * operands,
         scratch_shapes=scratch,
-        compiler_params=pltpu.CompilerParams(vmem_limit_bytes=40 * 1024 * 1024),
+        compiler_params=pltpu.CompilerParams(vmem_limit_bytes=20 * 1024 * 1024),
         cost_estimate=pl.CostEstimate(flops=flops, bytes_accessed=5 << 20, transcendentals=0),
     )
 
@@ -287,8 +294,15 @@
     return call(kernel, outs, [], 1 << 20, scalars=len(scalars), operands=1)(*scalars, pieces)
 
 
-def spread_owners(orbitals, owners, core, step):
-    piece = pick(pick_slot, (2, STEPS, HALF), (owners, core), orbitals)
+def spread_owners(orbitals, owners, core, step, first_row):
+    piece = pl.pallas_call(
+        pick_slot,
+        out_shape=jax.ShapeDtypeStruct((2, STEPS, HALF, GRID, GRID), BF16),
+        in_specs=[SMEM] * 4 + [pl.BlockSpec(memory_space=pl.ANY)],
+        out_specs=VMEM,
+        scratch_shapes=[pltpu.SemaphoreType.DMA((STEPS, 2))],
+        compiler_params=pltpu.CompilerParams(vmem_limit_bytes=20 * 1024 * 1024),
+    )(owners, core, step, first_row.reshape(1), orbitals)
     piece = lax.all_to_all(piece, "band", 0, 0, axis_index_groups=CORES, tiled=True)
     piece = exchange_all(pick(pick_core, (8, 2), (owners, core), piece), NEAR)
     orbitals, piece = lax.optimization_barrier((orbitals, piece))
@@ -313,23 +327,23 @@
 def coulomb_slab(cutoff, first_row):
     mirrored = jnp.roll(cutoff[::-1, ::-1], (1, 1), (0, 1))
     limits = lax.dynamic_slice_in_dim(jnp.minimum(cutoff, mirrored), first_row, ROWS, 1).T
-    full = jnp.arange(GRID, dtype=jnp.int32)
-    signed = jnp.where(full < GRID // 2, full, full - GRID)
-    own = first_row + jnp.arange(ROWS, dtype=jnp.int32)
+    signed = np.arange(GRID, dtype=np.int32)
+    signed = np.where(signed < GRID // 2, signed, signed - GRID).astype(np.int32)
+    own = first_row + np.arange(ROWS, dtype=np.int32)
     own = jnp.where(own < GRID // 2, own, own - GRID)
     squared = own[:, None, None] ** 2 + signed[None, :, None] ** 2 + signed[None, None, :] ** 2
-    inside = (jnp.abs(signed)[None, None, :] <= limits[:, :, None]) & (squared > 0)
+    inside = (np.abs(signed)[None, None, :] <= limits[:, :, None]) & (squared > 0)
     scale = COULOMB * float(GRID) ** 1.5 / float(GRID) ** 3
     return jnp.where(inside, scale / jnp.maximum(squared, 1).astype(F32), 0.0)
 
 
 def shards(orbitals, owners, cutoff):
-    first_row = lax.axis_index("ga") * ROWS
+    first_row = (lax.axis_index("ga") * ROWS).astype(jnp.int32)
     tables = jnp.asarray(dft_tables())
     band = lax.axis_index("band")
     core = (band % 2).astype(jnp.int32).reshape(1)
     step = (band // 2 % 2).astype(jnp.int32).reshape(1)
-    theirs, own = spread_owners(orbitals, owners, core, step)
+    theirs, own = spread_owners(orbitals, owners, core, step, first_row)
     cutoff, first_row, own = lax.optimization_barrier((cutoff, first_row, own))
     other = swap(own, 1)
     coulomb, other = lax.optimization_barrier((coulomb_slab(cutoff, first_row), other))
@@ -338,7 +352,7 @@
         spectrum = call(
             forward_kernel,
             jax.ShapeDtypeStruct((8, CHUNK + ROWS, GRID), BF16),
-            [pltpu.VMEM((2 * FIELDS, ROWS * GRID, GRID), F32)],
+            [pltpu.VMEM((2 * FIELDS, ROWS * PLANE, GRID), F32)],
             flops,
             operands=5,
         )(core, orbitals, theirs, own, other, tables)
@@ -347,7 +361,7 @@
         solved = call(
             solve_kernel,
             jax.ShapeDtypeStruct((8, FIELDS, ROWS, 2, ROWS, GRID), BF16),
-            [pltpu.VMEM((ROWS * 2 * GRID, GRID), F32)],
+            [pltpu.VMEM((ROWS * PAIR, GRID), F32)],
             flops,
             scalars=0,
             operands=3,

time: 227 us -> 223 us (0.982)
  blocking collectives: 159 us -> 169 us
  starting transfers between devices: 31.8 us -> 25.4 us
  Pallas kernels: 19.4 us -> 15.1 us
  waiting for transfers between devices: 10.2 us -> 6.2 us
    all_to_all x5 -> x6, blocking collectives: 83.8 us -> 94.2 us  [exchange_all(): return lax.all_to_all(x, 'band', 0, 0, axis_index_groups=groups, tiled=True)]
    all_to_all x1 -> x0, starting transfers between devices: 7.9 us -> none  [exchange_all(): return lax.all_to_all(x, 'band', 0, 0, axis_index_groups=groups, tiled=True)]
    all_to_all x1 -> x0, waiting for transfers between devices: 3.96 us -> none  [exchange_all(): return lax.all_to_all(x, 'band', 0, 0, axis_index_groups=groups, tiled=True)]
  transfers between devices with their start and end apart: 6 -> 5, of which waited for: 5 -> 4; matrix products, arithmetic and copies ran while one was open for 1% -> 1% of each run, Pallas kernels for 0% -> 0%
where the time goes in v5:
time: 223 us; the launch traced here: 222 us
  blocking collectives  169 us (76%)
  starting transfers between devices  25.4 us (11%)
  Pallas kernels  15.1 us (7%)
  waiting for transfers between devices  6.2 us (3%)
  other arithmetic  2.63 us (1%)
  local copies, waits for them, and re-layouts  2.34 us (1%)
    all_to_all x6, blocking collectives, exchange_all(): return lax.all_to_all(x, 'band', 0, 0, axis_index_groups=groups, tiled=True)  94.2 us
    all_to_all x2, blocking collectives, exchange_slabs(): return lax.all_to_all(x, 'ga', 0, 0, tiled=True)  63.8 us
    ppermute x5, starting transfers between devices, swap(): return lax.ppermute(x, 'band', [(i, i ^ bit) for i in range(64)])  25.4 us
    all_to_all x1, blocking collectives, spread_owners(): lax.all_to_all(piece, 'band', 0, 0, axis_index_groups=CORES, tiled=True)  11.2 us
    ppermute x5, waiting for transfers between devices, swap(): return lax.ppermute(x, 'band', [(i, i ^ bit) for i in range(64)])  6.2 us
    pallas_call x1, Pallas kernels, shards(): call(forward_kernel, jax.ShapeDtypeStruct((8, CHUNK + ROWS, GRID), BF16),...  4.66 us
  transfers between devices with their start and end apart: 5, of which 4 were waited for; matrix products, arithmetic and copies ran while one was open for 1% of the time, Pallas kernels for 0%

profile of v5, /device:TPU:1, one launch (start us, length us, event | category | flops | bytes accessed | tf_op | source)
XLA Modules:
  0.0 221.9 jit_solution(2327976729880952101)
XLA Ops:
  0.7 1.2 copy-done
  1.9 0.7 copy-done.2
  2.5 0.7 shard_map.95
  3.2 11.2 %all_to_all.45.pieces = bf16[2,2,8,128,128]{4,3,2,1,0:T(8,128)(2,1)S(1)} all-to-all(bf16[2,2,8,128,128]{4,3,2,1,0:T(8,128)(2,1)S(1)} %shard_map.95), channel_id=1, replica_groups={{0,8},{16,24},{32,40},{48,56},{64,72},{80,88},{96,104},{112,120},{128,1..., dimensions={0} | all-to-all | bytes 2097152 | tf_op jit(solution)/shard_map/all_to_all | solution.py:306
  15.1 16.2 %all_to_all.46.pieces = bf16[8,2,128,128]{3,2,1,0:T(8,128)(2,1)S(1)} all-to-all(bf16[8,2,128,128]{3,2,1,0:T(8,128)(2,1)S(1)} %shard_map.96), channel_id=1, replica_groups={{0,16,32,48,64,80,96,112},{128,144,160,176,192,208,224,240},{256,272,28..., dimensions={0} | all-to-all | bytes 1048576 | tf_op jit(solution)/shard_map/all_to_all | solution.py:277
  31.3 3.1 %collective-permute-start = (bf16[2,16,128,128]{3,2,1,0:T(8,128)(2,1)S(1)}, bf16[2,16,128,128]{3,2,1,0:T(8,128)(2,1)S(1)}, u32[]{:S(2)}, u32[]{:S(2)}) collective-permute-start(bf16[2,16,128,128]{3,2,1,0:T(8,128)(2,1)S(1)} %copy-done.1), channel_id=1, source_target_pairs={{0,16},{8,24},{16,0},{24,8},{32,48},{40,56},{48,32},{56,40},{64,80... | collective-permute-start | bytes 3145736 | tf_op jit(solution)/shard_map/ppermute | solution.py:289
  35.1 22.2 %all_to_all.47.pieces = bf16[4,2,128,128]{3,2,1,0:T(8,128)(2,1)S(1)} all-to-all(bf16[4,2,128,128]{3,2,1,0:T(8,128)(2,1)S(1)} %shard_map.97), channel_id=1, replica_groups={{0,128,256,384},{16,144,272,400},{32,160,288,416},{48,176,304,432},{64,..., dimensions={0} | all-to-all | bytes 524288 | tf_op jit(solution)/shard_map/all_to_all | solution.py:277
  58.3 11.6 %all_to_all.48.own = bf16[4,2,128,128]{3,2,1,0:T(8,128)(2,1)S(1)} all-to-all(bf16[4,2,128,128]{3,2,1,0:T(8,128)(2,1)S(1)} %shard_map.98), channel_id=1, replica_groups={{0,32,64,96},{16,48,80,112},{128,160,192,224},{144,176,208,240},{256,28..., dimensions={0} | all-to-all | bytes 524288 | tf_op jit(solution)/shard_map/all_to_all | solution.py:277
  70.3 6.8 %collective-permute-start.1 = (bf16[4,2,128,128]{3,2,1,0:T(8,128)(2,1)S(1)}, bf16[4,2,128,128]{3,2,1,0:T(8,128)(2,1)S(1)}, u32[]{:S(2)}, u32[]{:S(2)}) collective-permute-start(bf16[4,2,128,128]{3,2,1,0:T(8,128)(2,1)S(1)} %all_to_all.48.own), channel_id=1, source_target_pairs={{0,8},{8,0},{16,24},{24,16},{32,40},{40,32},{48,56},{56,48},{64,72... | collective-permute-start | bytes 786440 | tf_op jit(solution)/shard_map/ppermute | solution.py:289
  78.2 4.7 %forward_planes.1 = bf16[8,1040,128]{2,1,0:T(8,128)(2,1)S(1)} custom-call(s32[1]{0:T(128)} %bitcast.core, bf16[2,16,128,128]{3,2,1,0:T(8,128)(2,1)S(1)} %copy-done.1, bf16[2,16,128,128]{3,2,1,0:T(8,128)(2,1)S(1)} %collective-permute-done.theirs, bf16[4,2,128,128]{3,2,1,0:T(8,128)(2,1)S(1)} %all_to_all.48.own, ...), custom_call_target="tpu_custom_call" | custom-call | flops 3221225472 | bytes 5242880 | tf_op jit(solution)/shard_map/forward_planes/pallas_call | solution.py:352
  82.9 34.5 %all_to_all.49.spectrum = bf16[8,1040,128]{2,1,0:T(8,128)(2,1)S(1)} all-to-all(bf16[8,1040,128]{2,1,0:T(8,128)(2,1)S(1)} %forward_planes.1), channel_id=1, replica_groups=mesh['band'=64,'ga'=8] {'ga'}, dimensions={0} | all-to-all | bytes 4259840 | tf_op jit(solution)/shard_map/all_to_all | solution.py:285
  117.4 4.3 %coulomb_solve.1 = bf16[8,2,16,2,16,128]{5,4,3,2,1,0:T(8,128)(2,1)S(1)} custom-call(bf16[8,1040,128]{2,1,0:T(8,128)(2,1)S(1)} %all_to_all.49.spectrum, f32[16,128,128]{2,1,0:T(8,128)S(1)} %fusion.2.coulomb, bf16[4,256,256]{2,1,0:T(8,128)(2,1)S(1)} %copy-done.8), custom_call_target="tpu_custom_call" | custom-call | flops 3221225472 | bytes 5242880 | tf_op jit(solution)/shard_map/coulomb_solve/pallas_call | solution.py:361
  121.7 29.3 %all_to_all.50.solved = bf16[8,2,16,2,16,128]{5,4,3,2,1,0:T(8,128)(2,1)S(1)} all-to-all(bf16[8,2,16,2,16,128]{5,4,3,2,1,0:T(8,128)(2,1)S(1)} %coulomb_solve.1), channel_id=1, replica_groups=mesh['band'=64,'ga'=8] {'ga'}, dimensions={0} | all-to-all | bytes 4194304 | tf_op jit(solution)/shard_map/all_to_all | solution.py:285
  151.1 2.6 %backward_planes.1 = (f32[2,16,128,128]{3,2,1,0:T(8,128)S(1)}, bf16[2,16,128,128]{3,2,1,0:T(8,128)(2,1)S(1)}, f32[4,2,128,128]{3,2,1,0:T(8,128)S(1)}, bf16[4,2,128,128]{3,2,1,0:T(8,128)(2,1)S(1)}) custom-call(s32[1]{0:T(128)} %bitcast.core, bf16[8,2,16,2,16,128]{5,4,3,2,1,0:T(8,128)(2,1)S(1)} %all_to_all.50.solved, bf16[2,16,128,128]{3,2,1,0:T(8,128)(2,1)S(1)} %copy-done.1, ...), custom_call_target="tpu_custom_call" | custom-call | flops 3221225472 | bytes 5242880 | tf_op jit(solution)/shard_map/backward_planes/pallas_call | solution.py:373
  153.8 4.8 %collective-permute-start.2 = (bf16[4,2,128,128]{3,2,1,0:T(8,128)(2,1)S(1)}, bf16[4,2,128,128]{3,2,1,0:T(8,128)(2,1)S(1)}, u32[]{:S(2)}, u32[]{:S(2)}) collective-permute-start(bf16[4,2,128,128]{3,2,1,0:T(8,128)(2,1)S(1)} %get-tuple-element.31), channel_id=1, source_target_pairs={{0,8},{8,0},{16,24},{24,16},{32,40},{40,32},{48,56},{56,48},{64,72... | collective-permute-start | bytes 786440 | tf_op jit(solution)/shard_map/ppermute | solution.py:289
  158.6 1.1 collective-permute-done.2
  159.8 12.1 %all_to_all.51 = bf16[4,2,128,128]{3,2,1,0:T(8,128)(2,1)S(1)} all-to-all(bf16[4,2,128,128]{3,2,1,0:T(8,128)(2,1)S(1)} %add_convert_fusion), channel_id=1, replica_groups={{0,32,64,96},{16,48,80,112},{128,160,192,224},{144,176,208,240},{256,28..., dimensions={0} | all-to-all | bytes 524288 | tf_op jit(solution)/shard_map/all_to_all | solution.py:277
  171.9 1.9 collective-permute-start.3
  173.9 18.6 %all_to_all.52 = bf16[4,2,128,128]{3,2,1,0:T(8,128)(2,1)S(1)} all-to-all(bf16[4,2,128,128]{3,2,1,0:T(8,128)(2,1)S(1)} %broadcast_in_dim.9), channel_id=1, replica_groups={{0,128,256,384},{16,144,272,400},{32,160,288,416},{48,176,304,432},{64,..., dimensions={0} | all-to-all | bytes 524288 | tf_op jit(solution)/shard_map/all_to_all | solution.py:277
  192.5 4.4 %collective-permute-done.3 = bf16[2,16,128,128]{3,2,1,0:T(8,128)(2,1)S(1)} collective-permute-done((bf16[2,16,128,128]{3,2,1,0:T(8,128)(2,1)}, bf16[2,16,128,128]{3,2,1,0:T(8,128)(2,1)S(1)}, u32[]{:S(2)}, u32[]{:S(2)}) %collective-permute-start.3) | collective-permute-done | bytes 1048608 | tf_op jit(solution)/shard_map/ppermute | solution.py:289
  196.9 13.5 %all_to_all.53.own = bf16[8,2,128,128]{3,2,1,0:T(8,128)(2,1)S(1)} all-to-all(bf16[8,2,128,128]{3,2,1,0:T(8,128)(2,1)S(1)} %broadcast_in_dim.10), channel_id=1, replica_groups={{0,16,32,48,64,80,96,112},{128,144,160,176,192,208,224,240},{256,272,28..., dimensions={0} | all-to-all | bytes 1048576 | tf_op jit(solution)/shard_map/all_to_all | solution.py:277
  210.5 8.8 %collective-permute-start.4 = (bf16[8,2,128,128]{3,2,1,0:T(8,128)(2,1)S(1)}, bf16[8,2,128,128]{3,2,1,0:T(8,128)(2,1)S(1)}, u32[]{:S(2)}, u32[]{:S(2)}) collective-permute-start(bf16[8,2,128,128]{3,2,1,0:T(8,128)(2,1)S(1)} %all_to_all.53.own), channel_id=1, source_target_pairs={{0,8},{8,0},{16,24},{24,16},{32,40},{40,32},{48,56},{56,48},{64,72... | collective-permute-start | bytes 1572872 | tf_op jit(solution)/shard_map/ppermute | solution.py:289
  219.2 1.6 convert_add_fusion
  220.8 1.0 shard_map.99
  (47 shorter events, 4.0 us)
Async XLA Ops:
  0.7 1.2 copy-start
  1.9 0.7 copy-start.2
  3.2 28.1 %copy-start.1 = (bf16[2,16,128,128]{3,2,1,0:T(8,128)(2,1)S(1)}, bf16[2,16,128,128]{3,2,1,0:T(8,128)(2,1)}, u32[]{:S(2)}) copy-start(bf16[2,16,128,128]{3,2,1,0:T(8,128)(2,1)} %ours.3) | copy-start | bytes 3145732
  15.0 54.9 %copy-start.10 = (s32[128,128]{1,0:T(8,128)S(1)}, s32[128,128]{1,0:T(8,128)}, u32[]{:S(2)}) copy-start(s32[128,128]{1,0:T(8,128)} %param.10) | copy-start | bytes 196612
  15.1 54.9 %slice-start = ((s32[128,128]{1,0:T(8,128)}), s32[1,128]{1,0:T(1,128)S(1)}, s32[]{:S(2)}) async-start(s32[128,128]{1,0:T(8,128)} %param.10), calls=%async_computation.9 | async-start | bytes 1024 | tf_op jit(solution)/shard_map/jit(_roll_static)/slice | solution.py:328
  15.1 62.0 %copy-start.11 = (s32[128]{0:T(128)S(1)}, s32[128]{0:T(128)}, u32[]{:S(2)}) copy-start(s32[128]{0:T(128)} %constant.72) | copy-start | bytes 1540
  15.1 62.2 %copy-start.12 = (s32[128]{0:T(128)S(1)}, s32[128]{0:T(128)}, u32[]{:S(2)}) copy-start(s32[128]{0:T(128)} %constant.71) | copy-start | bytes 1540
  31.3 46.9 %copy-start.8 = (bf16[4,256,256]{2,1,0:T(8,128)(2,1)S(1)}, bf16[4,256,256]{2,1,0:T(8,128)(2,1)}, u32[]{:S(2)}) copy-start(bf16[4,256,256]{2,1,0:T(8,128)(2,1)} %constant.66.clone.tables) | copy-start | bytes 1572868
  31.3 26.4 %collective-permute-start = (bf16[2,16,128,128]{3,2,1,0:T(8,128)(2,1)S(1)}, bf16[2,16,128,128]{3,2,1,0:T(8,128)(2,1)S(1)}, u32[]{:S(2)}, u32[]{:S(2)}) collective-permute-start(bf16[2,16,128,128]{3,2,1,0:T(8,128)(2,1)S(1)} %copy-done.1), channel_id=1, source_target_pairs={{0,16},{8,24},{16,0},{24,8},{32,48},{40,56},{48,32},{56,40},{64,80... | collective-permute-start | bytes 3145736 | tf_op jit(solution)/shard_map/ppermute | solution.py:289
  57.7 25.1 %copy-start.3 = (bf16[2,16,128,128]{3,2,1,0:T(8,128)(2,1)}, bf16[2,16,128,128]{3,2,1,0:T(8,128)(2,1)S(1)}, u32[]{:S(2)}) copy-start(bf16[2,16,128,128]{3,2,1,0:T(8,128)(2,1)S(1)} %collective-permute-done.theirs) | copy-start | bytes 3145732
  70.3 7.9 %collective-permute-start.1 = (bf16[4,2,128,128]{3,2,1,0:T(8,128)(2,1)S(1)}, bf16[4,2,128,128]{3,2,1,0:T(8,128)(2,1)S(1)}, u32[]{:S(2)}, u32[]{:S(2)}) collective-permute-start(bf16[4,2,128,128]{3,2,1,0:T(8,128)(2,1)S(1)} %all_to_all.48.own), channel_id=1, source_target_pairs={{0,8},{8,0},{16,24},{24,16},{32,40},{40,32},{48,56},{56,48},{64,72... | collective-permute-start | bytes 786440 | tf_op jit(solution)/shard_map/ppermute | solution.py:289
  78.2 4.7 %copy-start.6 = (bf16[4,2,128,128]{3,2,1,0:T(8,128)(2,1)}, bf16[4,2,128,128]{3,2,1,0:T(8,128)(2,1)S(1)}, u32[]{:S(2)}) copy-start(bf16[4,2,128,128]{3,2,1,0:T(8,128)(2,1)S(1)} %collective-permute-done.1.other) | copy-start | bytes 786436
  121.7 29.4 %copy-start.4 = (bf16[2,16,128,128]{3,2,1,0:T(8,128)(2,1)S(1)}, bf16[2,16,128,128]{3,2,1,0:T(8,128)(2,1)}, u32[]{:S(2)}) copy-start(bf16[2,16,128,128]{3,2,1,0:T(8,128)(2,1)} %copy-done.3) | copy-start | bytes 3145732
  121.7 29.4 %copy-start.7 = (bf16[4,2,128,128]{3,2,1,0:T(8,128)(2,1)S(1)}, bf16[4,2,128,128]{3,2,1,0:T(8,128)(2,1)}, u32[]{:S(2)}) copy-start(bf16[4,2,128,128]{3,2,1,0:T(8,128)(2,1)} %copy-done.6) | copy-start | bytes 786436
  121.7 29.4 %copy-start.9 = (bf16[4,256,256]{2,1,0:T(8,128)(2,1)S(1)}, bf16[4,256,256]{2,1,0:T(8,128)(2,1)}, u32[]{:S(2)}) copy-start(bf16[4,256,256]{2,1,0:T(8,128)(2,1)} %constant.66.clone.tables) | copy-start | bytes 1572868
  153.7 6.0 %copy-start.5 = (bf16[2,16,128,128]{3,2,1,0:T(8,128)(2,1)}, bf16[2,16,128,128]{3,2,1,0:T(8,128)(2,1)S(1)}, u32[]{:S(2)}) copy-start(bf16[2,16,128,128]{3,2,1,0:T(8,128)(2,1)S(1)} %get-tuple-element.32) | copy-start | bytes 3145732
  153.8 5.9 %collective-permute-start.2 = (bf16[4,2,128,128]{3,2,1,0:T(8,128)(2,1)S(1)}, bf16[4,2,128,128]{3,2,1,0:T(8,128)(2,1)S(1)}, u32[]{:S(2)}, u32[]{:S(2)}) collective-permute-start(bf16[4,2,128,128]{3,2,1,0:T(8,128)(2,1)S(1)} %get-tuple-element.31), channel_id=1, source_target_pairs={{0,8},{8,0},{16,24},{24,16},{32,40},{40,32},{48,56},{56,48},{64,72... | collective-permute-start | bytes 786440 | tf_op jit(solution)/shard_map/ppermute | solution.py:289
  171.9 24.9 %collective-permute-start.3 = (bf16[2,16,128,128]{3,2,1,0:T(8,128)(2,1)}, bf16[2,16,128,128]{3,2,1,0:T(8,128)(2,1)S(1)}, u32[]{:S(2)}, u32[]{:S(2)}) collective-permute-start(bf16[2,16,128,128]{3,2,1,0:T(8,128)(2,1)} %copy-done.5), channel_id=1, source_target_pairs={{0,16},{8,24},{16,0},{24,8},{32,48},{40,56},{48,32},{56,40},{64,80... | collective-permute-start | bytes 3145736 | tf_op jit(solution)/shard_map/ppermute | solution.py:289
  210.5 10.3 %collective-permute-start.4 = (bf16[8,2,128,128]{3,2,1,0:T(8,128)(2,1)S(1)}, bf16[8,2,128,128]{3,2,1,0:T(8,128)(2,1)S(1)}, u32[]{:S(2)}, u32[]{:S(2)}) collective-permute-start(bf16[8,2,128,128]{3,2,1,0:T(8,128)(2,1)S(1)} %all_to_all.53.own), channel_id=1, source_target_pairs={{0,8},{8,0},{16,24},{24,16},{32,40},{40,32},{48,56},{56,48},{64,72... | collective-permute-start | bytes 1572872 | tf_op jit(solution)/shard_map/ppermute | solution.py:289

commit v6 on v5

--- a/solution.py
+++ b/solution.py
@@ -27,15 +27,19 @@
     return z % 16 * 4 + xl * 2 + core
 
 
+def near_z(k, j, core):
+    return 4 * k + (j + core) % 4 + SHIFT * core
+
+
 NEAR = [
-    [place(4 * k + j + SHIFT * core, xl, core) for j in range(4) for xl in range(2)]
+    [place(near_z(k, j, core), xl, core) for j in range(4) for xl in range(2)]
     for core in range(2)
     for k in range(4)
 ]
 FAR = [
-    [place(4 * k + j + SHIFT * core, xl, core) for k in range(4)]
+    [place(4 * quarter + z, xl, core) for quarter in (0, 1, 3, 2)]
     for core in range(2)
-    for j in range(4)
+    for z in range(4)
     for xl in range(2)
 ]
 CORES = [[2 * i, 2 * i + 1] for i in range(32)]
@@ -218,7 +222,7 @@
             terms[p] = term.astype(terms.dtype).reshape(2, n, n)
 
 
-def pick_slot(owners, core, step, first_row, orbitals, out, sems):
+def pick_slot(owners, core, step, carry, first_row, orbitals, out, sems):
     copies = []
     for s in range(STEPS):
         slot = lax.rem(owners[s], 2)
@@ -244,13 +248,14 @@
 def pick_near(owners, core, step, pieces, out):
     owner = owners[step[0]]
     z, xl = root_z(owner, core[0]), lax.rem(lax.div(owner, 4), 2)
-    piece = pieces[lax.rem(z, 4) * 2 + xl]
+    piece = pieces[lax.rem(lax.rem(z, 4) + 4 - core[0], 4) * 2 + xl]
     for copy in range(out.shape[0]):
         out[copy] = piece
 
 
-def pick_far(owners, core, step, pieces, out):
-    piece = pieces[lax.div(root_z(owners[step[0]], core[0]), 4)]
+def pick_far(owners, core, step, carry, pieces, out):
+    quarter = lax.rem(lax.div(root_z(owners[step[0]], core[0]), 4) + carry[0], 4)
+    piece = pieces[quarter + jnp.where(quarter == 2, 1, 0) - jnp.where(quarter == 3, 1, 0)]
     for copy in range(out.shape[0]):
         out[copy] = piece
 
@@ -294,22 +299,22 @@
     return call(kernel, outs, [], 1 << 20, scalars=len(scalars), operands=1)(*scalars, pieces)
 
 
-def spread_owners(orbitals, owners, core, step, first_row):
+def spread_owners(orbitals, owners, core, step, carry, first_row):
     piece = pl.pallas_call(
         pick_slot,
         out_shape=jax.ShapeDtypeStruct((2, STEPS, HALF, GRID, GRID), BF16),
-        in_specs=[SMEM] * 4 + [pl.BlockSpec(memory_space=pl.ANY)],
+        in_specs=[SMEM] * 5 + [pl.BlockSpec(memory_space=pl.ANY)],
         out_specs=VMEM,
         scratch_shapes=[pltpu.SemaphoreType.DMA((STEPS, 2))],
         compiler_params=pltpu.CompilerParams(vmem_limit_bytes=20 * 1024 * 1024),
-    )(owners, core, step, first_row.reshape(1), orbitals)
+    )(owners, core, step, carry, first_row.reshape(1), orbitals)
     piece = lax.all_to_all(piece, "band", 0, 0, axis_index_groups=CORES, tiled=True)
     piece = exchange_all(pick(pick_core, (8, 2), (owners, core), piece), NEAR)
     orbitals, piece = lax.optimization_barrier((orbitals, piece))
     theirs = swap(orbitals, 2)
     piece = exchange_all(pick(pick_near, (4, 2), (owners, core, step), piece), FAR)
     theirs, piece = lax.optimization_barrier((theirs, piece))
-    piece = exchange_all(pick(pick_far, (4, 2), (owners, core, step), piece), LINE)
+    piece = exchange_all(pick(pick_far, (4, 2), (owners, core, step, carry), piece), LINE)
     return theirs, piece
 
 
@@ -343,7 +348,8 @@
     band = lax.axis_index("band")
     core = (band % 2).astype(jnp.int32).reshape(1)
     step = (band // 2 % 2).astype(jnp.int32).reshape(1)
-    theirs, own = spread_owners(orbitals, owners, core, step, first_row)
+    carry = jnp.where((band % 2 == 1) & (band // 4 % 4 < SHIFT), 1, 0).astype(jnp.int32).reshape(1)
+    theirs, own = spread_owners(orbitals, owners, core, step, carry, first_row)
     cutoff, first_row, own = lax.optimization_barrier((cutoff, first_row, own))
     other = swap(own, 1)
     coulomb, other = lax.optimization_barrier((coulomb_slab(cutoff, first_row), other))

time: 223 us -> 221 us (level)
  starting transfers between devices: 25.4 us -> 16.9 us
  blocking collectives: 169 us -> 174 us
  waiting for transfers between devices: 6.2 us -> 9.02 us
    ppermute x5, starting transfers between devices: 25.4 us -> 16.9 us  [swap(): return lax.ppermute(x, 'band', [(i, i ^ bit) for i in range(64)])]
    all_to_all x6, blocking collectives: 94.2 us -> 98.5 us  [exchange_all(): return lax.all_to_all(x, 'band', 0, 0, axis_index_groups=groups, tiled=True)]
    ppermute x5, waiting for transfers between devices: 6.2 us -> 9.02 us  [swap(): return lax.ppermute(x, 'band', [(i, i ^ bit) for i in range(64)])]
  transfers between devices with their start and end apart: 5 -> 5, of which waited for: 4 -> 3; matrix products, arithmetic and copies ran while one was open for 1% -> 1% of each run, Pallas kernels for 0% -> 0%
where the time goes in v6:
time: 221 us
  blocking collectives  174 us (79%)
  starting transfers between devices  16.9 us (8%)
  Pallas kernels  15.1 us (7%)
  waiting for transfers between devices  9.02 us (4%)
  other arithmetic  2.63 us (1%)
  local copies, waits for them, and re-layouts  2.34 us (1%)
    all_to_all x6, blocking collectives, exchange_all(): return lax.all_to_all(x, 'band', 0, 0, axis_index_groups=groups, tiled=True)  98.5 us
    all_to_all x2, blocking collectives, exchange_slabs(): return lax.all_to_all(x, 'ga', 0, 0, tiled=True)  63.9 us
    ppermute x5, starting transfers between devices, swap(): return lax.ppermute(x, 'band', [(i, i ^ bit) for i in range(64)])  16.9 us
    all_to_all x1, blocking collectives, spread_owners(): lax.all_to_all(piece, 'band', 0, 0, axis_index_groups=CORES, tiled=True)  11.2 us
    ppermute x5, waiting for transfers between devices, swap(): return lax.ppermute(x, 'band', [(i, i ^ bit) for i in range(64)])  9.02 us
    pallas_call x1, Pallas kernels, shards(): call(forward_kernel, jax.ShapeDtypeStruct((8, CHUNK + ROWS, GRID), BF16),...  4.66 us
  transfers between devices with their start and end apart: 5, of which 3 were waited for; matrix products, arithmetic and copies ran while one was open for 1% of the time, Pallas kernels for 0%

profile of v6, /device:TPU:1, one launch (start us, length us, event | category | flops | bytes accessed | tf_op | source)
XLA Modules:
  0.0 220.6 jit_solution(5084315571112639015)
XLA Ops:
  0.7 1.2 copy-done
  1.9 0.7 copy-done.2
  2.6 0.7 shard_map.95
  3.3 11.2 %all_to_all.45.pieces = bf16[2,2,8,128,128]{4,3,2,1,0:T(8,128)(2,1)S(1)} all-to-all(bf16[2,2,8,128,128]{4,3,2,1,0:T(8,128)(2,1)S(1)} %shard_map.95), channel_id=1, replica_groups={{0,8},{16,24},{32,40},{48,56},{64,72},{80,88},{96,104},{112,120},{128,1..., dimensions={0} | all-to-all | bytes 2097152 | tf_op jit(solution)/shard_map/all_to_all | solution.py:311
  15.1 16.8 %all_to_all.46.pieces = bf16[8,2,128,128]{3,2,1,0:T(8,128)(2,1)S(1)} all-to-all(bf16[8,2,128,128]{3,2,1,0:T(8,128)(2,1)S(1)} %shard_map.96), channel_id=1, replica_groups={{0,16,32,48,64,80,96,112},{128,144,160,176,192,208,224,240},{256,272,28..., dimensions={0} | all-to-all | bytes 1048576 | tf_op jit(solution)/shard_map/all_to_all | solution.py:282
  31.9 3.2 %collective-permute-start = (bf16[2,16,128,128]{3,2,1,0:T(8,128)(2,1)S(1)}, bf16[2,16,128,128]{3,2,1,0:T(8,128)(2,1)S(1)}, u32[]{:S(2)}, u32[]{:S(2)}) collective-permute-start(bf16[2,16,128,128]{3,2,1,0:T(8,128)(2,1)S(1)} %copy-done.1), channel_id=1, source_target_pairs={{0,16},{8,24},{16,0},{24,8},{32,48},{40,56},{48,32},{56,40},{64,80... | collective-permute-start | bytes 3145736 | tf_op jit(solution)/shard_map/ppermute | solution.py:294
  35.7 25.7 %all_to_all.47.pieces = bf16[4,2,128,128]{3,2,1,0:T(8,128)(2,1)S(1)} all-to-all(bf16[4,2,128,128]{3,2,1,0:T(8,128)(2,1)S(1)} %shard_map.97), channel_id=1, replica_groups={{0,128,384,256},{16,144,400,272},{32,160,416,288},{48,176,432,304},{64,..., dimensions={0} | all-to-all | bytes 524288 | tf_op jit(solution)/shard_map/all_to_all | solution.py:282
  62.0 12.3 %all_to_all.48.own = bf16[4,2,128,128]{3,2,1,0:T(8,128)(2,1)S(1)} all-to-all(bf16[4,2,128,128]{3,2,1,0:T(8,128)(2,1)S(1)} %shard_map.98), channel_id=1, replica_groups={{0,32,64,96},{16,48,80,112},{128,160,192,224},{144,176,208,240},{256,28..., dimensions={0} | all-to-all | bytes 524288 | tf_op jit(solution)/shard_map/all_to_all | solution.py:282
  74.7 3.8 %collective-permute-start.1 = (bf16[4,2,128,128]{3,2,1,0:T(8,128)(2,1)S(1)}, bf16[4,2,128,128]{3,2,1,0:T(8,128)(2,1)S(1)}, u32[]{:S(2)}, u32[]{:S(2)}) collective-permute-start(bf16[4,2,128,128]{3,2,1,0:T(8,128)(2,1)S(1)} %all_to_all.48.own), channel_id=1, source_target_pairs={{0,8},{8,0},{16,24},{24,16},{32,40},{40,32},{48,56},{56,48},{64,72... | collective-permute-start | bytes 786440 | tf_op jit(solution)/shard_map/ppermute | solution.py:294
  79.7 4.7 %forward_planes.1 = bf16[8,1040,128]{2,1,0:T(8,128)(2,1)S(1)} custom-call(s32[1]{0:T(128)} %bitcast.core, bf16[2,16,128,128]{3,2,1,0:T(8,128)(2,1)S(1)} %copy-done.1, bf16[2,16,128,128]{3,2,1,0:T(8,128)(2,1)S(1)} %collective-permute-done.theirs, bf16[4,2,128,128]{3,2,1,0:T(8,128)(2,1)S(1)} %all_to_all.48.own, ...), custom_call_target="tpu_custom_call" | custom-call | flops 3221225472 | bytes 5242880 | tf_op jit(solution)/shard_map/forward_planes/pallas_call | solution.py:358
  84.3 34.6 %all_to_all.49.spectrum = bf16[8,1040,128]{2,1,0:T(8,128)(2,1)S(1)} all-to-all(bf16[8,1040,128]{2,1,0:T(8,128)(2,1)S(1)} %forward_planes.1), channel_id=1, replica_groups=mesh['band'=64,'ga'=8] {'ga'}, dimensions={0} | all-to-all | bytes 4259840 | tf_op jit(solution)/shard_map/all_to_all | solution.py:290
  118.9 4.3 %coulomb_solve.1 = bf16[8,2,16,2,16,128]{5,4,3,2,1,0:T(8,128)(2,1)S(1)} custom-call(bf16[8,1040,128]{2,1,0:T(8,128)(2,1)S(1)} %all_to_all.49.spectrum, f32[16,128,128]{2,1,0:T(8,128)S(1)} %fusion.2.coulomb, bf16[4,256,256]{2,1,0:T(8,128)(2,1)S(1)} %copy-done.8), custom_call_target="tpu_custom_call" | custom-call | flops 3221225472 | bytes 5242880 | tf_op jit(solution)/shard_map/coulomb_solve/pallas_call | solution.py:367
  123.3 29.3 %all_to_all.50.solved = bf16[8,2,16,2,16,128]{5,4,3,2,1,0:T(8,128)(2,1)S(1)} all-to-all(bf16[8,2,16,2,16,128]{5,4,3,2,1,0:T(8,128)(2,1)S(1)} %coulomb_solve.1), channel_id=1, replica_groups=mesh['band'=64,'ga'=8] {'ga'}, dimensions={0} | all-to-all | bytes 4194304 | tf_op jit(solution)/shard_map/all_to_all | solution.py:290
  152.6 2.6 %backward_planes.1 = (f32[2,16,128,128]{3,2,1,0:T(8,128)S(1)}, bf16[2,16,128,128]{3,2,1,0:T(8,128)(2,1)S(1)}, f32[4,2,128,128]{3,2,1,0:T(8,128)S(1)}, bf16[4,2,128,128]{3,2,1,0:T(8,128)(2,1)S(1)}) custom-call(s32[1]{0:T(128)} %bitcast.core, bf16[8,2,16,2,16,128]{5,4,3,2,1,0:T(8,128)(2,1)S(1)} %all_to_all.50.solved, bf16[2,16,128,128]{3,2,1,0:T(8,128)(2,1)S(1)} %copy-done.1, ...), custom_call_target="tpu_custom_call" | custom-call | flops 3221225472 | bytes 5242880 | tf_op jit(solution)/shard_map/backward_planes/pallas_call | solution.py:379
  155.3 4.8 %collective-permute-start.2 = (bf16[4,2,128,128]{3,2,1,0:T(8,128)(2,1)S(1)}, bf16[4,2,128,128]{3,2,1,0:T(8,128)(2,1)S(1)}, u32[]{:S(2)}, u32[]{:S(2)}) collective-permute-start(bf16[4,2,128,128]{3,2,1,0:T(8,128)(2,1)S(1)} %get-tuple-element.31), channel_id=1, source_target_pairs={{0,8},{8,0},{16,24},{24,16},{32,40},{40,32},{48,56},{56,48},{64,72... | collective-permute-start | bytes 786440 | tf_op jit(solution)/shard_map/ppermute | solution.py:294
  160.1 1.1 collective-permute-done.2
  161.3 11.0 %all_to_all.51 = bf16[4,2,128,128]{3,2,1,0:T(8,128)(2,1)S(1)} all-to-all(bf16[4,2,128,128]{3,2,1,0:T(8,128)(2,1)S(1)} %add_convert_fusion), channel_id=1, replica_groups={{0,32,64,96},{16,48,80,112},{128,160,192,224},{144,176,208,240},{256,28..., dimensions={0} | all-to-all | bytes 524288 | tf_op jit(solution)/shard_map/all_to_all | solution.py:282
  172.4 1.9 collective-permute-start.3
  174.3 16.7 %all_to_all.52 = bf16[4,2,128,128]{3,2,1,0:T(8,128)(2,1)S(1)} all-to-all(bf16[4,2,128,128]{3,2,1,0:T(8,128)(2,1)S(1)} %broadcast_in_dim.9), channel_id=1, replica_groups={{0,128,384,256},{16,144,400,272},{32,160,416,288},{48,176,432,304},{64,..., dimensions={0} | all-to-all | bytes 524288 | tf_op jit(solution)/shard_map/all_to_all | solution.py:282
  191.1 7.6 %collective-permute-done.3 = bf16[2,16,128,128]{3,2,1,0:T(8,128)(2,1)S(1)} collective-permute-done((bf16[2,16,128,128]{3,2,1,0:T(8,128)(2,1)}, bf16[2,16,128,128]{3,2,1,0:T(8,128)(2,1)S(1)}, u32[]{:S(2)}, u32[]{:S(2)}) %collective-permute-start.3) | collective-permute-done | bytes 1048608 | tf_op jit(solution)/shard_map/ppermute | solution.py:294
  198.8 16.0 %all_to_all.53.own = bf16[8,2,128,128]{3,2,1,0:T(8,128)(2,1)S(1)} all-to-all(bf16[8,2,128,128]{3,2,1,0:T(8,128)(2,1)S(1)} %broadcast_in_dim.10), channel_id=1, replica_groups={{0,16,32,48,64,80,96,112},{128,144,160,176,192,208,224,240},{256,272,28..., dimensions={0} | all-to-all | bytes 1048576 | tf_op jit(solution)/shard_map/all_to_all | solution.py:282
  214.8 3.1 %collective-permute-start.4 = (bf16[8,2,128,128]{3,2,1,0:T(8,128)(2,1)S(1)}, bf16[8,2,128,128]{3,2,1,0:T(8,128)(2,1)S(1)}, u32[]{:S(2)}, u32[]{:S(2)}) collective-permute-start(bf16[8,2,128,128]{3,2,1,0:T(8,128)(2,1)S(1)} %all_to_all.53.own), channel_id=1, source_target_pairs={{0,8},{8,0},{16,24},{24,16},{32,40},{40,32},{48,56},{56,48},{64,72... | collective-permute-start | bytes 1572872 | tf_op jit(solution)/shard_map/ppermute | solution.py:294
  218.0 1.6 convert_add_fusion
  219.5 1.0 shard_map.99
  (47 shorter events, 3.5 us)
Async XLA Ops:
  0.7 1.2 copy-start
  1.9 0.7 copy-start.2
  3.3 28.7 %copy-start.1 = (bf16[2,16,128,128]{3,2,1,0:T(8,128)(2,1)S(1)}, bf16[2,16,128,128]{3,2,1,0:T(8,128)(2,1)}, u32[]{:S(2)}) copy-start(bf16[2,16,128,128]{3,2,1,0:T(8,128)(2,1)} %ours.3) | copy-start | bytes 3145732
  15.1 59.2 %copy-start.10 = (s32[128,128]{1,0:T(8,128)S(1)}, s32[128,128]{1,0:T(8,128)}, u32[]{:S(2)}) copy-start(s32[128,128]{1,0:T(8,128)} %param.10) | copy-start | bytes 196612
  15.1 59.3 %slice-start = ((s32[128,128]{1,0:T(8,128)}), s32[1,128]{1,0:T(1,128)S(1)}, s32[]{:S(2)}) async-start(s32[128,128]{1,0:T(8,128)} %param.10), calls=%async_computation.9 | async-start | bytes 1024 | tf_op jit(solution)/shard_map/jit(_roll_static)/slice | solution.py:333
  15.1 63.4 %copy-start.11 = (s32[128]{0:T(128)S(1)}, s32[128]{0:T(128)}, u32[]{:S(2)}) copy-start(s32[128]{0:T(128)} %constant.93) | copy-start | bytes 1540
  15.1 63.7 %copy-start.12 = (s32[128]{0:T(128)S(1)}, s32[128]{0:T(128)}, u32[]{:S(2)}) copy-start(s32[128]{0:T(128)} %constant.92) | copy-start | bytes 1540
  31.9 47.7 %copy-start.8 = (bf16[4,256,256]{2,1,0:T(8,128)(2,1)S(1)}, bf16[4,256,256]{2,1,0:T(8,128)(2,1)}, u32[]{:S(2)}) copy-start(bf16[4,256,256]{2,1,0:T(8,128)(2,1)} %constant.87.clone.tables) | copy-start | bytes 1572868
  31.9 29.5 %collective-permute-start = (bf16[2,16,128,128]{3,2,1,0:T(8,128)(2,1)S(1)}, bf16[2,16,128,128]{3,2,1,0:T(8,128)(2,1)S(1)}, u32[]{:S(2)}, u32[]{:S(2)}) collective-permute-start(bf16[2,16,128,128]{3,2,1,0:T(8,128)(2,1)S(1)} %copy-done.1), channel_id=1, source_target_pairs={{0,16},{8,24},{16,0},{24,8},{32,48},{40,56},{48,32},{56,40},{64,80... | collective-permute-start | bytes 3145736 | tf_op jit(solution)/shard_map/ppermute | solution.py:294
  61.4 22.9 %copy-start.3 = (bf16[2,16,128,128]{3,2,1,0:T(8,128)(2,1)}, bf16[2,16,128,128]{3,2,1,0:T(8,128)(2,1)S(1)}, u32[]{:S(2)}) copy-start(bf16[2,16,128,128]{3,2,1,0:T(8,128)(2,1)S(1)} %collective-permute-done.theirs) | copy-start | bytes 3145732
  74.7 5.0 %collective-permute-start.1 = (bf16[4,2,128,128]{3,2,1,0:T(8,128)(2,1)S(1)}, bf16[4,2,128,128]{3,2,1,0:T(8,128)(2,1)S(1)}, u32[]{:S(2)}, u32[]{:S(2)}) collective-permute-start(bf16[4,2,128,128]{3,2,1,0:T(8,128)(2,1)S(1)} %all_to_all.48.own), channel_id=1, source_target_pairs={{0,8},{8,0},{16,24},{24,16},{32,40},{40,32},{48,56},{56,48},{64,72... | collective-permute-start | bytes 786440 | tf_op jit(solution)/shard_map/ppermute | solution.py:294
  79.7 4.7 %copy-start.6 = (bf16[4,2,128,128]{3,2,1,0:T(8,128)(2,1)}, bf16[4,2,128,128]{3,2,1,0:T(8,128)(2,1)S(1)}, u32[]{:S(2)}) copy-start(bf16[4,2,128,128]{3,2,1,0:T(8,128)(2,1)S(1)} %collective-permute-done.1.other) | copy-start | bytes 786436
  123.2 29.4 %copy-start.4 = (bf16[2,16,128,128]{3,2,1,0:T(8,128)(2,1)S(1)}, bf16[2,16,128,128]{3,2,1,0:T(8,128)(2,1)}, u32[]{:S(2)}) copy-start(bf16[2,16,128,128]{3,2,1,0:T(8,128)(2,1)} %copy-done.3) | copy-start | bytes 3145732
  123.3 29.4 %copy-start.7 = (bf16[4,2,128,128]{3,2,1,0:T(8,128)(2,1)S(1)}, bf16[4,2,128,128]{3,2,1,0:T(8,128)(2,1)}, u32[]{:S(2)}) copy-start(bf16[4,2,128,128]{3,2,1,0:T(8,128)(2,1)} %copy-done.6) | copy-start | bytes 786436
  123.3 29.4 %copy-start.9 = (bf16[4,256,256]{2,1,0:T(8,128)(2,1)S(1)}, bf16[4,256,256]{2,1,0:T(8,128)(2,1)}, u32[]{:S(2)}) copy-start(bf16[4,256,256]{2,1,0:T(8,128)(2,1)} %constant.87.clone.tables) | copy-start | bytes 1572868
  155.3 6.0 %copy-start.5 = (bf16[2,16,128,128]{3,2,1,0:T(8,128)(2,1)}, bf16[2,16,128,128]{3,2,1,0:T(8,128)(2,1)S(1)}, u32[]{:S(2)}) copy-start(bf16[2,16,128,128]{3,2,1,0:T(8,128)(2,1)S(1)} %get-tuple-element.32) | copy-start | bytes 3145732
  155.3 5.9 %collective-permute-start.2 = (bf16[4,2,128,128]{3,2,1,0:T(8,128)(2,1)S(1)}, bf16[4,2,128,128]{3,2,1,0:T(8,128)(2,1)S(1)}, u32[]{:S(2)}, u32[]{:S(2)}) collective-permute-start(bf16[4,2,128,128]{3,2,1,0:T(8,128)(2,1)S(1)} %get-tuple-element.31), channel_id=1, source_target_pairs={{0,8},{8,0},{16,24},{24,16},{32,40},{40,32},{48,56},{56,48},{64,72... | collective-permute-start | bytes 786440 | tf_op jit(solution)/shard_map/ppermute | solution.py:294
  172.4 26.4 %collective-permute-start.3 = (bf16[2,16,128,128]{3,2,1,0:T(8,128)(2,1)}, bf16[2,16,128,128]{3,2,1,0:T(8,128)(2,1)S(1)}, u32[]{:S(2)}, u32[]{:S(2)}) collective-permute-start(bf16[2,16,128,128]{3,2,1,0:T(8,128)(2,1)} %copy-done.5), channel_id=1, source_target_pairs={{0,16},{8,24},{16,0},{24,8},{32,48},{40,56},{48,32},{56,40},{64,80... | collective-permute-start | bytes 3145736 | tf_op jit(solution)/shard_map/ppermute | solution.py:294
  214.8 4.7 %collective-permute-start.4 = (bf16[8,2,128,128]{3,2,1,0:T(8,128)(2,1)S(1)}, bf16[8,2,128,128]{3,2,1,0:T(8,128)(2,1)S(1)}, u32[]{:S(2)}, u32[]{:S(2)}) collective-permute-start(bf16[8,2,128,128]{3,2,1,0:T(8,128)(2,1)S(1)} %all_to_all.53.own), channel_id=1, source_target_pairs={{0,8},{8,0},{16,24},{24,16},{32,40},{40,32},{48,56},{56,48},{64,72... | collective-permute-start | bytes 1572872 | tf_op jit(solution)/shard_map/ppermute | solution.py:294

commit v7 on v6

--- a/solution.py
+++ b/solution.py
@@ -20,7 +20,7 @@
 BF16 = jnp.bfloat16
 F32 = jnp.float32
 
-SHIFT = 2
+SHIFT = 0
 
 
 def place(z, xl, core):
@@ -42,7 +42,6 @@
     for z in range(4)
     for xl in range(2)
 ]
-CORES = [[2 * i, 2 * i + 1] for i in range(32)]
 LINE = [group[xl::2] for group in NEAR for xl in range(2)]
 VMEM = pl.BlockSpec(memory_space=pltpu.VMEM)
 SMEM = pl.BlockSpec(memory_space=pltpu.SMEM)
@@ -222,23 +221,27 @@
             terms[p] = term.astype(terms.dtype).reshape(2, n, n)
 
 
-def pick_slot(owners, core, step, carry, first_row, orbitals, out, sems):
-    copies = []
+def pick_slot(owners, core, step, carry, first_row, orbitals, keep, send):
+    first = core[0] * HALF
     for s in range(STEPS):
         slot = lax.rem(owners[s], 2)
-        for half in range(2):
-            piece = orbitals.at[slot, pl.ds(half * HALF, HALF)]
-            copies.append(pltpu.make_async_copy(piece, out.at[half, s], sems.at[s, half]))
-            copies[-1].start()
-    for copy in copies:
-        copy.wait()
-
-
-def pick_core(owners, core, pieces, out):
+        keep[s] = orbitals[slot, pl.ds(first, HALF)]
+        send[s] = orbitals[slot, pl.ds(HALF - first, HALF)]
+
+
+def pick_core(owners, core, kept, received, out):
     for s in range(STEPS):
-        root = lax.rem(lax.div(owners[s], 2), 2)
-        for x in range(HALF // 2):
-            out[2 * x + s] = pieces[root, s, 2 * x : 2 * x + 2]
+        ours = lax.rem(lax.div(owners[s], 2), 2) == core[0]
+
+        @pl.when(ours)
+        def _():
+            for x in range(HALF // 2):
+                out[2 * x + s] = kept[s, 2 * x : 2 * x + 2]
+
+        @pl.when(jnp.logical_not(ours))
+        def _():
+            for x in range(HALF // 2):
+                out[2 * x + s] = received[s, 2 * x : 2 * x + 2]
 
 
 def root_z(owner, core):
@@ -294,22 +297,17 @@
     return lax.ppermute(x, "band", [(i, i ^ bit) for i in range(64)])
 
 
-def pick(kernel, shape, scalars, pieces):
+def pick(kernel, shape, scalars, *pieces):
     outs = jax.ShapeDtypeStruct(shape + (GRID, GRID), BF16)
-    return call(kernel, outs, [], 1 << 20, scalars=len(scalars), operands=1)(*scalars, pieces)
+    return call(kernel, outs, [], 1 << 20, scalars=len(scalars), operands=len(pieces))(*scalars, *pieces)
 
 
 def spread_owners(orbitals, owners, core, step, carry, first_row):
-    piece = pl.pallas_call(
-        pick_slot,
-        out_shape=jax.ShapeDtypeStruct((2, STEPS, HALF, GRID, GRID), BF16),
-        in_specs=[SMEM] * 5 + [pl.BlockSpec(memory_space=pl.ANY)],
-        out_specs=VMEM,
-        scratch_shapes=[pltpu.SemaphoreType.DMA((STEPS, 2))],
-        compiler_params=pltpu.CompilerParams(vmem_limit_bytes=20 * 1024 * 1024),
-    )(owners, core, step, carry, first_row.reshape(1), orbitals)
-    piece = lax.all_to_all(piece, "band", 0, 0, axis_index_groups=CORES, tiled=True)
-    piece = exchange_all(pick(pick_core, (8, 2), (owners, core), piece), NEAR)
+    half = jax.ShapeDtypeStruct((STEPS, HALF, GRID, GRID), BF16)
+    scalars = (owners, core, step, carry, first_row.reshape(1))
+    keep, send = call(pick_slot, (half, half), [], 1 << 20, scalars=5, operands=1)(*scalars, orbitals)
+    received = swap(send, 1)
+    piece = exchange_all(pick(pick_core, (8, 2), (owners, core), keep, received), NEAR)
     orbitals, piece = lax.optimization_barrier((orbitals, piece))
     theirs = swap(orbitals, 2)
     piece = exchange_all(pick(pick_near, (4, 2), (owners, core, step), piece), FAR)

time: 221 us -> 218 us (0.986)
  starting transfers between devices: 16.9 us -> 30 us
  blocking collectives: 174 us -> 161 us
  waiting for transfers between devices: 9.02 us -> 5.54 us
    ppermute x5 -> x6, starting transfers between devices: 16.9 us -> 30 us  [swap(): return lax.ppermute(x, 'band', [(i, i ^ bit) for i in range(64)])]
    all_to_all x1 -> x0, blocking collectives: 11.2 us -> none  [spread_owners(): lax.all_to_all(piece, 'band', 0, 0, axis_index_groups=CORES, tiled=True)]
    ppermute x5 -> x6, waiting for transfers between devices: 9.02 us -> 5.54 us  [swap(): return lax.ppermute(x, 'band', [(i, i ^ bit) for i in range(64)])]
  transfers between devices with their start and end apart: 5 -> 6, of which waited for: 3 -> 4; matrix products, arithmetic and copies ran while one was open for 1% -> 1% of each run, Pallas kernels for 0% -> 0%
where the time goes in v7:
time: 218 us; the launch traced here: 217 us
  blocking collectives  161 us (74%)
  starting transfers between devices  30 us (14%)
  Pallas kernels  15.1 us (7%)
  waiting for transfers between devices  5.54 us (3%)
  other arithmetic  2.63 us (1%)
  local copies, waits for them, and re-layouts  2.34 us (1%)
    all_to_all x6, blocking collectives, exchange_all(): return lax.all_to_all(x, 'band', 0, 0, axis_index_groups=groups, tiled=True)  96.8 us
    all_to_all x2, blocking collectives, exchange_slabs(): return lax.all_to_all(x, 'ga', 0, 0, tiled=True)  63.8 us
    ppermute x6, starting transfers between devices, swap(): return lax.ppermute(x, 'band', [(i, i ^ bit) for i in range(64)])  30 us
    ppermute x6, waiting for transfers between devices, swap(): return lax.ppermute(x, 'band', [(i, i ^ bit) for i in range(64)])  5.54 us
    pallas_call x1, Pallas kernels, shards(): call(forward_kernel, jax.ShapeDtypeStruct((8, CHUNK + ROWS, GRID), BF16),...  4.66 us
  transfers between devices with their start and end apart: 6, of which 4 were waited for; matrix products, arithmetic and copies ran while one was open for 1% of the time, Pallas kernels for 0%

profile of v7, /device:TPU:1, one launch (start us, length us, event | category | flops | bytes accessed | tf_op | source)
XLA Modules:
  0.0 217.2 jit_solution(1885205230955552609)
XLA Ops:
  0.7 1.2 copy-done
  1.9 0.7 copy-done.2
  3.2 8.8 %collective-permute-start = (bf16[2,8,128,128]{3,2,1,0:T(8,128)(2,1)S(1)}, bf16[2,8,128,128]{3,2,1,0:T(8,128)(2,1)S(1)}, u32[]{:S(2)}, u32[]{:S(2)}) collective-permute-start(bf16[2,8,128,128]{3,2,1,0:T(8,128)(2,1)S(1)} %get-tuple-element.22), channel_id=1, source_target_pairs={{0,8},{8,0},{16,24},{24,16},{32,40},{40,32},{48,56},{56,48},{64,72... | collective-permute-start | bytes 1572872 | tf_op jit(solution)/shard_map/ppermute | solution.py:297
  12.0 1.5 collective-permute-done.received
  14.2 14.9 %all_to_all.40.pieces = bf16[8,2,128,128]{3,2,1,0:T(8,128)(2,1)S(1)} all-to-all(bf16[8,2,128,128]{3,2,1,0:T(8,128)(2,1)S(1)} %shard_map.96), channel_id=1, replica_groups={{0,16,32,48,64,80,96,112},{128,144,160,176,192,208,224,240},{256,272,28..., dimensions={0} | all-to-all | bytes 1048576 | tf_op jit(solution)/shard_map/all_to_all | solution.py:285
  29.1 3.4 %collective-permute-start.1 = (bf16[2,16,128,128]{3,2,1,0:T(8,128)(2,1)S(1)}, bf16[2,16,128,128]{3,2,1,0:T(8,128)(2,1)S(1)}, u32[]{:S(2)}, u32[]{:S(2)}) collective-permute-start(bf16[2,16,128,128]{3,2,1,0:T(8,128)(2,1)S(1)} %copy-done.1), channel_id=1, source_target_pairs={{0,16},{8,24},{16,0},{24,8},{32,48},{40,56},{48,32},{56,40},{64,80... | collective-permute-start | bytes 3145736 | tf_op jit(solution)/shard_map/ppermute | solution.py:297
  33.1 28.0 %all_to_all.41.pieces = bf16[4,2,128,128]{3,2,1,0:T(8,128)(2,1)S(1)} all-to-all(bf16[4,2,128,128]{3,2,1,0:T(8,128)(2,1)S(1)} %shard_map.97), channel_id=1, replica_groups={{0,128,384,256},{16,144,400,272},{32,160,416,288},{48,176,432,304},{64,..., dimensions={0} | all-to-all | bytes 524288 | tf_op jit(solution)/shard_map/all_to_all | solution.py:285
  61.7 7.3 %all_to_all.42.own = bf16[4,2,128,128]{3,2,1,0:T(8,128)(2,1)S(1)} all-to-all(bf16[4,2,128,128]{3,2,1,0:T(8,128)(2,1)S(1)} %shard_map.98), channel_id=1, replica_groups={{0,32,64,96},{16,48,80,112},{128,160,192,224},{144,176,208,240},{256,28..., dimensions={0} | all-to-all | bytes 524288 | tf_op jit(solution)/shard_map/all_to_all | solution.py:285
  69.4 7.1 %collective-permute-start.2 = (bf16[4,2,128,128]{3,2,1,0:T(8,128)(2,1)S(1)}, bf16[4,2,128,128]{3,2,1,0:T(8,128)(2,1)S(1)}, u32[]{:S(2)}, u32[]{:S(2)}) collective-permute-start(bf16[4,2,128,128]{3,2,1,0:T(8,128)(2,1)S(1)} %all_to_all.42.own), channel_id=1, source_target_pairs={{0,8},{8,0},{16,24},{24,16},{32,40},{40,32},{48,56},{56,48},{64,72... | collective-permute-start | bytes 786440 | tf_op jit(solution)/shard_map/ppermute | solution.py:297
  77.7 4.7 %forward_planes.1 = bf16[8,1040,128]{2,1,0:T(8,128)(2,1)S(1)} custom-call(s32[1]{0:T(128)} %bitcast.core, bf16[2,16,128,128]{3,2,1,0:T(8,128)(2,1)S(1)} %copy-done.1, bf16[2,16,128,128]{3,2,1,0:T(8,128)(2,1)S(1)} %collective-permute-done.1.theirs, bf16[4,2,128,128]{3,2,1,0:T(8,128)(2,1)S(1)} %all_to_all.42.own, ...), custom_call_target="tpu_custom_call" | custom-call | flops 3221225472 | bytes 5242880 | tf_op jit(solution)/shard_map/forward_planes/pallas_call | solution.py:356
  82.4 34.5 %all_to_all.43.spectrum = bf16[8,1040,128]{2,1,0:T(8,128)(2,1)S(1)} all-to-all(bf16[8,1040,128]{2,1,0:T(8,128)(2,1)S(1)} %forward_planes.1), channel_id=1, replica_groups=mesh['band'=64,'ga'=8] {'ga'}, dimensions={0} | all-to-all | bytes 4259840 | tf_op jit(solution)/shard_map/all_to_all | solution.py:293
  116.9 4.3 %coulomb_solve.1 = bf16[8,2,16,2,16,128]{5,4,3,2,1,0:T(8,128)(2,1)S(1)} custom-call(bf16[8,1040,128]{2,1,0:T(8,128)(2,1)S(1)} %all_to_all.43.spectrum, f32[16,128,128]{2,1,0:T(8,128)S(1)} %fusion.2.coulomb, bf16[4,256,256]{2,1,0:T(8,128)(2,1)S(1)} %copy-done.8), custom_call_target="tpu_custom_call" | custom-call | flops 3221225472 | bytes 5242880 | tf_op jit(solution)/shard_map/coulomb_solve/pallas_call | solution.py:365
  121.2 29.3 %all_to_all.44.solved = bf16[8,2,16,2,16,128]{5,4,3,2,1,0:T(8,128)(2,1)S(1)} all-to-all(bf16[8,2,16,2,16,128]{5,4,3,2,1,0:T(8,128)(2,1)S(1)} %coulomb_solve.1), channel_id=1, replica_groups=mesh['band'=64,'ga'=8] {'ga'}, dimensions={0} | all-to-all | bytes 4194304 | tf_op jit(solution)/shard_map/all_to_all | solution.py:293
  150.6 2.6 %backward_planes.1 = (f32[2,16,128,128]{3,2,1,0:T(8,128)S(1)}, bf16[2,16,128,128]{3,2,1,0:T(8,128)(2,1)S(1)}, f32[4,2,128,128]{3,2,1,0:T(8,128)S(1)}, bf16[4,2,128,128]{3,2,1,0:T(8,128)(2,1)S(1)}) custom-call(s32[1]{0:T(128)} %bitcast.core, bf16[8,2,16,2,16,128]{5,4,3,2,1,0:T(8,128)(2,1)S(1)} %all_to_all.44.solved, bf16[2,16,128,128]{3,2,1,0:T(8,128)(2,1)S(1)} %copy-done.1, ...), custom_call_target="tpu_custom_call" | custom-call | flops 3221225472 | bytes 5242880 | tf_op jit(solution)/shard_map/backward_planes/pallas_call | solution.py:377
  153.2 4.8 %collective-permute-start.3 = (bf16[4,2,128,128]{3,2,1,0:T(8,128)(2,1)S(1)}, bf16[4,2,128,128]{3,2,1,0:T(8,128)(2,1)S(1)}, u32[]{:S(2)}, u32[]{:S(2)}) collective-permute-start(bf16[4,2,128,128]{3,2,1,0:T(8,128)(2,1)S(1)} %get-tuple-element.35), channel_id=1, source_target_pairs={{0,8},{8,0},{16,24},{24,16},{32,40},{40,32},{48,56},{56,48},{64,72... | collective-permute-start | bytes 786440 | tf_op jit(solution)/shard_map/ppermute | solution.py:297
  158.0 1.1 collective-permute-done.3
  159.2 9.0 %all_to_all.45 = bf16[4,2,128,128]{3,2,1,0:T(8,128)(2,1)S(1)} all-to-all(bf16[4,2,128,128]{3,2,1,0:T(8,128)(2,1)S(1)} %add_convert_fusion), channel_id=1, replica_groups={{0,32,64,96},{16,48,80,112},{128,160,192,224},{144,176,208,240},{256,28..., dimensions={0} | all-to-all | bytes 524288 | tf_op jit(solution)/shard_map/all_to_all | solution.py:285
  168.3 1.9 collective-permute-start.4
  170.2 19.2 %all_to_all.46 = bf16[4,2,128,128]{3,2,1,0:T(8,128)(2,1)S(1)} all-to-all(bf16[4,2,128,128]{3,2,1,0:T(8,128)(2,1)S(1)} %broadcast_in_dim.9), channel_id=1, replica_groups={{0,128,384,256},{16,144,400,272},{32,160,416,288},{48,176,432,304},{64,..., dimensions={0} | all-to-all | bytes 524288 | tf_op jit(solution)/shard_map/all_to_all | solution.py:285
  189.5 2.6 %collective-permute-done.4 = bf16[2,16,128,128]{3,2,1,0:T(8,128)(2,1)S(1)} collective-permute-done((bf16[2,16,128,128]{3,2,1,0:T(8,128)(2,1)}, bf16[2,16,128,128]{3,2,1,0:T(8,128)(2,1)S(1)}, u32[]{:S(2)}, u32[]{:S(2)}) %collective-permute-start.4) | collective-permute-done | bytes 1048608 | tf_op jit(solution)/shard_map/ppermute | solution.py:297
  192.2 18.3 %all_to_all.47.own = bf16[8,2,128,128]{3,2,1,0:T(8,128)(2,1)S(1)} all-to-all(bf16[8,2,128,128]{3,2,1,0:T(8,128)(2,1)S(1)} %broadcast_in_dim.10), channel_id=1, replica_groups={{0,16,32,48,64,80,96,112},{128,144,160,176,192,208,224,240},{256,272,28..., dimensions={0} | all-to-all | bytes 1048576 | tf_op jit(solution)/shard_map/all_to_all | solution.py:285
  210.5 4.1 %collective-permute-start.5 = (bf16[8,2,128,128]{3,2,1,0:T(8,128)(2,1)S(1)}, bf16[8,2,128,128]{3,2,1,0:T(8,128)(2,1)S(1)}, u32[]{:S(2)}, u32[]{:S(2)}) collective-permute-start(bf16[8,2,128,128]{3,2,1,0:T(8,128)(2,1)S(1)} %all_to_all.47.own), channel_id=1, source_target_pairs={{0,8},{8,0},{16,24},{24,16},{32,40},{40,32},{48,56},{56,48},{64,72... | collective-permute-start | bytes 1572872 | tf_op jit(solution)/shard_map/ppermute | solution.py:297
  214.6 1.6 convert_add_fusion
  216.2 1.0 shard_map.99
  (48 shorter events, 4.2 us)
Async XLA Ops:
  0.7 1.2 copy-start
  1.9 0.7 copy-start.2
  2.6 26.5 %copy-start.1 = (bf16[2,16,128,128]{3,2,1,0:T(8,128)(2,1)S(1)}, bf16[2,16,128,128]{3,2,1,0:T(8,128)(2,1)}, u32[]{:S(2)}) copy-start(bf16[2,16,128,128]{3,2,1,0:T(8,128)(2,1)} %ours.3) | copy-start | bytes 3145732
  3.2 10.3 %collective-permute-start = (bf16[2,8,128,128]{3,2,1,0:T(8,128)(2,1)S(1)}, bf16[2,8,128,128]{3,2,1,0:T(8,128)(2,1)S(1)}, u32[]{:S(2)}, u32[]{:S(2)}) collective-permute-start(bf16[2,8,128,128]{3,2,1,0:T(8,128)(2,1)S(1)} %get-tuple-element.22), channel_id=1, source_target_pairs={{0,8},{8,0},{16,24},{24,16},{32,40},{40,32},{48,56},{56,48},{64,72... | collective-permute-start | bytes 1572872 | tf_op jit(solution)/shard_map/ppermute | solution.py:297
  14.1 55.0 %copy-start.10 = (s32[128,128]{1,0:T(8,128)S(1)}, s32[128,128]{1,0:T(8,128)}, u32[]{:S(2)}) copy-start(s32[128,128]{1,0:T(8,128)} %param.10) | copy-start | bytes 196612
  14.1 55.0 %slice-start = ((s32[128,128]{1,0:T(8,128)}), s32[1,128]{1,0:T(1,128)S(1)}, s32[]{:S(2)}) async-start(s32[128,128]{1,0:T(8,128)} %param.10), calls=%async_computation.8 | async-start | bytes 1024 | tf_op jit(solution)/shard_map/jit(_roll_static)/slice | solution.py:331
  14.1 62.4 %copy-start.11 = (s32[128]{0:T(128)S(1)}, s32[128]{0:T(128)}, u32[]{:S(2)}) copy-start(s32[128]{0:T(128)} %constant.93) | copy-start | bytes 1540
  14.2 62.7 %copy-start.12 = (s32[128]{0:T(128)S(1)}, s32[128]{0:T(128)}, u32[]{:S(2)}) copy-start(s32[128]{0:T(128)} %constant.92) | copy-start | bytes 1540
  29.1 48.6 %copy-start.8 = (bf16[4,256,256]{2,1,0:T(8,128)(2,1)S(1)}, bf16[4,256,256]{2,1,0:T(8,128)(2,1)}, u32[]{:S(2)}) copy-start(bf16[4,256,256]{2,1,0:T(8,128)(2,1)} %constant.87.clone.tables) | copy-start | bytes 1572868
  29.1 32.0 %collective-permute-start.1 = (bf16[2,16,128,128]{3,2,1,0:T(8,128)(2,1)S(1)}, bf16[2,16,128,128]{3,2,1,0:T(8,128)(2,1)S(1)}, u32[]{:S(2)}, u32[]{:S(2)}) collective-permute-start(bf16[2,16,128,128]{3,2,1,0:T(8,128)(2,1)S(1)} %copy-done.1), channel_id=1, source_target_pairs={{0,16},{8,24},{16,0},{24,8},{32,48},{40,56},{48,32},{56,40},{64,80... | collective-permute-start | bytes 3145736 | tf_op jit(solution)/shard_map/ppermute | solution.py:297
  61.1 21.2 %copy-start.3 = (bf16[2,16,128,128]{3,2,1,0:T(8,128)(2,1)}, bf16[2,16,128,128]{3,2,1,0:T(8,128)(2,1)S(1)}, u32[]{:S(2)}) copy-start(bf16[2,16,128,128]{3,2,1,0:T(8,128)(2,1)S(1)} %collective-permute-done.1.theirs) | copy-start | bytes 3145732
  69.4 8.3 %collective-permute-start.2 = (bf16[4,2,128,128]{3,2,1,0:T(8,128)(2,1)S(1)}, bf16[4,2,128,128]{3,2,1,0:T(8,128)(2,1)S(1)}, u32[]{:S(2)}, u32[]{:S(2)}) collective-permute-start(bf16[4,2,128,128]{3,2,1,0:T(8,128)(2,1)S(1)} %all_to_all.42.own), channel_id=1, source_target_pairs={{0,8},{8,0},{16,24},{24,16},{32,40},{40,32},{48,56},{56,48},{64,72... | collective-permute-start | bytes 786440 | tf_op jit(solution)/shard_map/ppermute | solution.py:297
  77.7 4.7 %copy-start.6 = (bf16[4,2,128,128]{3,2,1,0:T(8,128)(2,1)}, bf16[4,2,128,128]{3,2,1,0:T(8,128)(2,1)S(1)}, u32[]{:S(2)}) copy-start(bf16[4,2,128,128]{3,2,1,0:T(8,128)(2,1)S(1)} %collective-permute-done.2.other) | copy-start | bytes 786436
  121.2 29.4 %copy-start.4 = (bf16[2,16,128,128]{3,2,1,0:T(8,128)(2,1)S(1)}, bf16[2,16,128,128]{3,2,1,0:T(8,128)(2,1)}, u32[]{:S(2)}) copy-start(bf16[2,16,128,128]{3,2,1,0:T(8,128)(2,1)} %copy-done.3) | copy-start | bytes 3145732
  121.2 29.4 %copy-start.7 = (bf16[4,2,128,128]{3,2,1,0:T(8,128)(2,1)S(1)}, bf16[4,2,128,128]{3,2,1,0:T(8,128)(2,1)}, u32[]{:S(2)}) copy-start(bf16[4,2,128,128]{3,2,1,0:T(8,128)(2,1)} %copy-done.6) | copy-start | bytes 786436
  121.2 29.4 %copy-start.9 = (bf16[4,256,256]{2,1,0:T(8,128)(2,1)S(1)}, bf16[4,256,256]{2,1,0:T(8,128)(2,1)}, u32[]{:S(2)}) copy-start(bf16[4,256,256]{2,1,0:T(8,128)(2,1)} %constant.87.clone.tables) | copy-start | bytes 1572868
  153.2 6.0 %copy-start.5 = (bf16[2,16,128,128]{3,2,1,0:T(8,128)(2,1)}, bf16[2,16,128,128]{3,2,1,0:T(8,128)(2,1)S(1)}, u32[]{:S(2)}) copy-start(bf16[2,16,128,128]{3,2,1,0:T(8,128)(2,1)S(1)} %get-tuple-element.36) | copy-start | bytes 3145732
  153.2 5.9 %collective-permute-start.3 = (bf16[4,2,128,128]{3,2,1,0:T(8,128)(2,1)S(1)}, bf16[4,2,128,128]{3,2,1,0:T(8,128)(2,1)S(1)}, u32[]{:S(2)}, u32[]{:S(2)}) collective-permute-start(bf16[4,2,128,128]{3,2,1,0:T(8,128)(2,1)S(1)} %get-tuple-element.35), channel_id=1, source_target_pairs={{0,8},{8,0},{16,24},{24,16},{32,40},{40,32},{48,56},{56,48},{64,72... | collective-permute-start | bytes 786440 | tf_op jit(solution)/shard_map/ppermute | solution.py:297
  168.3 23.9 %collective-permute-start.4 = (bf16[2,16,128,128]{3,2,1,0:T(8,128)(2,1)}, bf16[2,16,128,128]{3,2,1,0:T(8,128)(2,1)S(1)}, u32[]{:S(2)}, u32[]{:S(2)}) collective-permute-start(bf16[2,16,128,128]{3,2,1,0:T(8,128)(2,1)} %copy-done.5), channel_id=1, source_target_pairs={{0,16},{8,24},{16,0},{24,8},{32,48},{40,56},{48,32},{56,40},{64,80... | collective-permute-start | bytes 3145736 | tf_op jit(solution)/shard_map/ppermute | solution.py:297
  210.5 5.7 %collective-permute-start.5 = (bf16[8,2,128,128]{3,2,1,0:T(8,128)(2,1)S(1)}, bf16[8,2,128,128]{3,2,1,0:T(8,128)(2,1)S(1)}, u32[]{:S(2)}, u32[]{:S(2)}) collective-permute-start(bf16[8,2,128,128]{3,2,1,0:T(8,128)(2,1)S(1)} %all_to_all.47.own), channel_id=1, source_target_pairs={{0,8},{8,0},{16,24},{24,16},{32,40},{40,32},{48,56},{56,48},{64,72... | collective-permute-start | bytes 1572872 | tf_op jit(solution)/shard_map/ppermute | solution.py:297

commit v8 on v7

--- a/solution.py
+++ b/solution.py
@@ -42,6 +42,7 @@
     for z in range(4)
     for xl in range(2)
 ]
+SLABS = [[band * 8 + (7 - g if band % 2 else g) for g in range(8)] for band in range(64)]
 LINE = [group[xl::2] for group in NEAR for xl in range(2)]
 VMEM = pl.BlockSpec(memory_space=pltpu.VMEM)
 SMEM = pl.BlockSpec(memory_space=pltpu.SMEM)
@@ -55,7 +56,10 @@
     matrix = np.block([[cosine, -sine], [sine, cosine]]).astype(np.float32)
     high = matrix.astype(BF16)
     low = (matrix - high.astype(np.float32)).astype(BF16)
-    return np.stack([high, low, high.T, low.T])
+    plain = np.stack([high, low, high.T, low.T])
+    order = np.arange(2 * GRID).reshape(2, GRID // ROWS, ROWS)[:, ::-1].reshape(-1)
+    turned = np.stack([high[order], low[order], high.T[:, order], low.T[:, order]])
+    return plain, np.concatenate([plain, turned])
 
 
 def dot(a, b):
@@ -141,8 +145,9 @@
     lax.fori_loop(0, n // ROWS, send, 0)
 
 
-def solve_kernel(spectrum, coulomb, tables, out, scratch):
+def solve_kernel(core, spectrum, coulomb, tables, out, scratch):
     n = GRID
+    first = core[0] * 4
     rest = spectrum[:, CHUNK:].reshape(n, n).astype(F32)
     lane = lax.broadcasted_iota(jnp.int32, (n, n), 1)
     dropped = coulomb[0, :1, :1] == 0.0
@@ -158,7 +163,7 @@
             return jnp.concatenate([pair, pair], axis=0)
 
         def inverse(x):
-            return left_exact(x.astype(BF16), tables, 0)
+            return left_exact(x.astype(BF16), tables, first)
 
         def keep(q, solved):
             start = q * 2 * PAIR
@@ -170,7 +175,7 @@
                 [jnp.concatenate(pick(2 * q), axis=0), jnp.concatenate(pick(2 * q + 1), axis=0)],
                 axis=1,
             )
-            keep(q, inverse(left_exact(both, tables, 2) * factor(q)))
+            keep(q, inverse(left_exact(both, tables, first + 2) * factor(q)))
 
         parts = []
         for part, tile in enumerate(pick(0)):
@@ -183,7 +188,7 @@
         both = jnp.concatenate(
             [jnp.concatenate(parts, axis=0), jnp.concatenate(pick(1), axis=0).astype(F32)], axis=1
         )
-        keep(0, inverse(left(both, tables, 2) * factor(0)))
+        keep(0, inverse(left(both, tables, first + 2) * factor(0)))
         for q in range(1, ROWS // 2):
             columns(q)
 
@@ -290,7 +295,7 @@
 
 
 def exchange_slabs(x):
-    return lax.all_to_all(x, "ga", 0, 0, tiled=True)
+    return lax.all_to_all(x, ("band", "ga"), 0, 0, axis_index_groups=SLABS, tiled=True)
 
 
 def swap(x, bit):
@@ -341,8 +346,9 @@
 
 
 def shards(orbitals, owners, cutoff):
-    first_row = (lax.axis_index("ga") * ROWS).astype(jnp.int32)
-    tables = jnp.asarray(dft_tables())
+    slab = lax.axis_index("ga")
+    first_row = (jnp.where(lax.axis_index("band") % 2 == 1, 7 - slab, slab) * ROWS).astype(jnp.int32)
+    tables, both_tables = (jnp.asarray(table) for table in dft_tables())
     band = lax.axis_index("band")
     core = (band % 2).astype(jnp.int32).reshape(1)
     step = (band // 2 % 2).astype(jnp.int32).reshape(1)
@@ -367,9 +373,8 @@
             jax.ShapeDtypeStruct((8, FIELDS, ROWS, 2, ROWS, GRID), BF16),
             [pltpu.VMEM((ROWS * PAIR, GRID), F32)],
             flops,
-            scalars=0,
             operands=3,
-        )(spectrum, coulomb, tables)
+        )(core, spectrum, coulomb, both_tables)
     solved = exchange_slabs(solved)
     slab = (2, ROWS, GRID, GRID)
     half = (HALF // 2, 2, GRID, GRID)

time: 218 us -> 215 us (0.986)
  no operation moved by 1% of the time
where the time goes in v8:
time: 215 us
  blocking collectives  160 us (74%)
  starting transfers between devices  28 us (13%)
  Pallas kernels  15.1 us (7%)
  waiting for transfers between devices  5.43 us (3%)
  other arithmetic  2.63 us (1%)
  local copies, waits for them, and re-layouts  2.34 us (1%)
    all_to_all x6, blocking collectives, exchange_all(): return lax.all_to_all(x, 'band', 0, 0, axis_index_groups=groups, tiled=True)  96.8 us
    all_to_all x2, blocking collectives, exchange_slabs(): lax.all_to_all(x, ('band', 'ga'), 0, 0, axis_index_groups=SLABS, tiled=True)  63.3 us
    ppermute x6, starting transfers between devices, swap(): return lax.ppermute(x, 'band', [(i, i ^ bit) for i in range(64)])  28 us
    ppermute x6, waiting for transfers between devices, swap(): return lax.ppermute(x, 'band', [(i, i ^ bit) for i in range(64)])  5.43 us
    pallas_call x1, Pallas kernels, shards(): call(forward_kernel, jax.ShapeDtypeStruct((8, CHUNK + ROWS, GRID), BF16),...  4.66 us
    pallas_call x1, Pallas kernels, shards(): call(solve_kernel, jax.ShapeDtypeStruct((8, FIELDS, ROWS, 2, ROWS, GRID),...  4.31 us
  transfers between devices with their start and end apart: 6, of which 4 were waited for; matrix products, arithmetic and copies ran while one was open for 1% of the time, Pallas kernels for 0%

profile of v8, /device:TPU:1, one launch (start us, length us, event | category | flops | bytes accessed | tf_op | source)
XLA Modules:
  0.0 214.6 jit_solution(18103062242837644574)
XLA Ops:
  0.7 1.2 copy-done
  1.9 0.7 copy-done.2
  3.2 8.8 %collective-permute-start = (bf16[2,8,128,128]{3,2,1,0:T(8,128)(2,1)S(1)}, bf16[2,8,128,128]{3,2,1,0:T(8,128)(2,1)S(1)}, u32[]{:S(2)}, u32[]{:S(2)}) collective-permute-start(bf16[2,8,128,128]{3,2,1,0:T(8,128)(2,1)S(1)} %get-tuple-element.22), channel_id=1, source_target_pairs={{0,8},{8,0},{16,24},{24,16},{32,40},{40,32},{48,56},{56,48},{64,72... | collective-permute-start | bytes 1572872 | tf_op jit(solution)/shard_map/ppermute | solution.py:302
  12.0 1.5 collective-permute-done.received
  14.2 14.9 %all_to_all.40.pieces = bf16[8,2,128,128]{3,2,1,0:T(8,128)(2,1)S(1)} all-to-all(bf16[8,2,128,128]{3,2,1,0:T(8,128)(2,1)S(1)} %shard_map.105), channel_id=1, replica_groups={{0,16,32,48,64,80,96,112},{128,144,160,176,192,208,224,240},{256,272,28..., dimensions={0} | all-to-all | bytes 1048576 | tf_op jit(solution)/shard_map/all_to_all | solution.py:290
  29.1 3.4 %collective-permute-start.1 = (bf16[2,16,128,128]{3,2,1,0:T(8,128)(2,1)S(1)}, bf16[2,16,128,128]{3,2,1,0:T(8,128)(2,1)S(1)}, u32[]{:S(2)}, u32[]{:S(2)}) collective-permute-start(bf16[2,16,128,128]{3,2,1,0:T(8,128)(2,1)S(1)} %copy-done.1), channel_id=1, source_target_pairs={{0,16},{8,24},{16,0},{24,8},{32,48},{40,56},{48,32},{56,40},{64,80... | collective-permute-start | bytes 3145736 | tf_op jit(solution)/shard_map/ppermute | solution.py:302
  33.1 28.0 %all_to_all.41.pieces = bf16[4,2,128,128]{3,2,1,0:T(8,128)(2,1)S(1)} all-to-all(bf16[4,2,128,128]{3,2,1,0:T(8,128)(2,1)S(1)} %shard_map.106), channel_id=1, replica_groups={{0,128,384,256},{16,144,400,272},{32,160,416,288},{48,176,432,304},{64,..., dimensions={0} | all-to-all | bytes 524288 | tf_op jit(solution)/shard_map/all_to_all | solution.py:290
  61.7 7.3 %all_to_all.42.own = bf16[4,2,128,128]{3,2,1,0:T(8,128)(2,1)S(1)} all-to-all(bf16[4,2,128,128]{3,2,1,0:T(8,128)(2,1)S(1)} %shard_map.107), channel_id=1, replica_groups={{0,32,64,96},{16,48,80,112},{128,160,192,224},{144,176,208,240},{256,28..., dimensions={0} | all-to-all | bytes 524288 | tf_op jit(solution)/shard_map/all_to_all | solution.py:290
  69.4 7.1 %collective-permute-start.2 = (bf16[4,2,128,128]{3,2,1,0:T(8,128)(2,1)S(1)}, bf16[4,2,128,128]{3,2,1,0:T(8,128)(2,1)S(1)}, u32[]{:S(2)}, u32[]{:S(2)}) collective-permute-start(bf16[4,2,128,128]{3,2,1,0:T(8,128)(2,1)S(1)} %all_to_all.42.own), channel_id=1, source_target_pairs={{0,8},{8,0},{16,24},{24,16},{32,40},{40,32},{48,56},{56,48},{64,72... | collective-permute-start | bytes 786440 | tf_op jit(solution)/shard_map/ppermute | solution.py:302
  77.7 4.7 %forward_planes.1 = bf16[8,1040,128]{2,1,0:T(8,128)(2,1)S(1)} custom-call(s32[1]{0:T(128)} %bitcast.core, bf16[2,16,128,128]{3,2,1,0:T(8,128)(2,1)S(1)} %copy-done.1, bf16[2,16,128,128]{3,2,1,0:T(8,128)(2,1)S(1)} %collective-permute-done.1.theirs, bf16[4,2,128,128]{3,2,1,0:T(8,128)(2,1)S(1)} %all_to_all.42.own, ...), custom_call_target="tpu_custom_call" | custom-call | flops 3221225472 | bytes 5242880 | tf_op jit(solution)/shard_map/forward_planes/pallas_call | solution.py:362
  82.4 31.8 %all_to_all.43.spectrum = bf16[8,1040,128]{2,1,0:T(8,128)(2,1)S(1)} all-to-all(bf16[8,1040,128]{2,1,0:T(8,128)(2,1)S(1)} %forward_planes.1), channel_id=1, replica_groups={{0,1,2,3,4,5,6,7},{15,14,13,12,11,10,9,8},{16,17,18,19,20,21,22,23},{31..., dimensions={0} | all-to-all | bytes 4259840 | tf_op jit(solution)/shard_map/all_to_all | solution.py:298
  114.2 4.3 %coulomb_solve.1 = bf16[8,2,16,2,16,128]{5,4,3,2,1,0:T(8,128)(2,1)S(1)} custom-call(s32[1]{0:T(128)} %bitcast.core, bf16[8,1040,128]{2,1,0:T(8,128)(2,1)S(1)} %all_to_all.43.spectrum, f32[16,128,128]{2,1,0:T(8,128)S(1)} %fusion.2.coulomb, bf16[8,256,256]{2,1,0:T(8,128)(2,1)S(1)} %copy-done.8), custom_call_target="tpu_custom_call" | custom-call | flops 3221225472 | bytes 5242880 | tf_op jit(solution)/shard_map/coulomb_solve/pallas_call | solution.py:371
  118.5 31.5 %all_to_all.44.solved = bf16[8,2,16,2,16,128]{5,4,3,2,1,0:T(8,128)(2,1)S(1)} all-to-all(bf16[8,2,16,2,16,128]{5,4,3,2,1,0:T(8,128)(2,1)S(1)} %coulomb_solve.1), channel_id=1, replica_groups={{0,1,2,3,4,5,6,7},{15,14,13,12,11,10,9,8},{16,17,18,19,20,21,22,23},{31..., dimensions={0} | all-to-all | bytes 4194304 | tf_op jit(solution)/shard_map/all_to_all | solution.py:298
  150.1 2.6 %backward_planes.1 = (f32[2,16,128,128]{3,2,1,0:T(8,128)S(1)}, bf16[2,16,128,128]{3,2,1,0:T(8,128)(2,1)S(1)}, f32[4,2,128,128]{3,2,1,0:T(8,128)S(1)}, bf16[4,2,128,128]{3,2,1,0:T(8,128)(2,1)S(1)}) custom-call(s32[1]{0:T(128)} %bitcast.core, bf16[8,2,16,2,16,128]{5,4,3,2,1,0:T(8,128)(2,1)S(1)} %all_to_all.44.solved, bf16[2,16,128,128]{3,2,1,0:T(8,128)(2,1)S(1)} %copy-done.1, ...), custom_call_target="tpu_custom_call" | custom-call | flops 3221225472 | bytes 5242880 | tf_op jit(solution)/shard_map/backward_planes/pallas_call | solution.py:382
  152.7 2.7 %collective-permute-start.3 = (bf16[4,2,128,128]{3,2,1,0:T(8,128)(2,1)S(1)}, bf16[4,2,128,128]{3,2,1,0:T(8,128)(2,1)S(1)}, u32[]{:S(2)}, u32[]{:S(2)}) collective-permute-start(bf16[4,2,128,128]{3,2,1,0:T(8,128)(2,1)S(1)} %get-tuple-element.35), channel_id=1, source_target_pairs={{0,8},{8,0},{16,24},{24,16},{32,40},{40,32},{48,56},{56,48},{64,72... | collective-permute-start | bytes 786440 | tf_op jit(solution)/shard_map/ppermute | solution.py:302
  155.5 1.1 collective-permute-done.3
  156.7 9.0 %all_to_all.45 = bf16[4,2,128,128]{3,2,1,0:T(8,128)(2,1)S(1)} all-to-all(bf16[4,2,128,128]{3,2,1,0:T(8,128)(2,1)S(1)} %add_convert_fusion), channel_id=1, replica_groups={{0,32,64,96},{16,48,80,112},{128,160,192,224},{144,176,208,240},{256,28..., dimensions={0} | all-to-all | bytes 524288 | tf_op jit(solution)/shard_map/all_to_all | solution.py:290
  165.7 1.9 collective-permute-start.4
  167.7 19.3 %all_to_all.46 = bf16[4,2,128,128]{3,2,1,0:T(8,128)(2,1)S(1)} all-to-all(bf16[4,2,128,128]{3,2,1,0:T(8,128)(2,1)S(1)} %broadcast_in_dim.9), channel_id=1, replica_groups={{0,128,384,256},{16,144,400,272},{32,160,416,288},{48,176,432,304},{64,..., dimensions={0} | all-to-all | bytes 524288 | tf_op jit(solution)/shard_map/all_to_all | solution.py:290
  187.1 2.5 %collective-permute-done.4 = bf16[2,16,128,128]{3,2,1,0:T(8,128)(2,1)S(1)} collective-permute-done((bf16[2,16,128,128]{3,2,1,0:T(8,128)(2,1)}, bf16[2,16,128,128]{3,2,1,0:T(8,128)(2,1)S(1)}, u32[]{:S(2)}, u32[]{:S(2)}) %collective-permute-start.4) | collective-permute-done | bytes 1048608 | tf_op jit(solution)/shard_map/ppermute | solution.py:302
  189.7 18.2 %all_to_all.47.own = bf16[8,2,128,128]{3,2,1,0:T(8,128)(2,1)S(1)} all-to-all(bf16[8,2,128,128]{3,2,1,0:T(8,128)(2,1)S(1)} %broadcast_in_dim.10), channel_id=1, replica_groups={{0,16,32,48,64,80,96,112},{128,144,160,176,192,208,224,240},{256,272,28..., dimensions={0} | all-to-all | bytes 1048576 | tf_op jit(solution)/shard_map/all_to_all | solution.py:290
  207.9 4.1 %collective-permute-start.5 = (bf16[8,2,128,128]{3,2,1,0:T(8,128)(2,1)S(1)}, bf16[8,2,128,128]{3,2,1,0:T(8,128)(2,1)S(1)}, u32[]{:S(2)}, u32[]{:S(2)}) collective-permute-start(bf16[8,2,128,128]{3,2,1,0:T(8,128)(2,1)S(1)} %all_to_all.47.own), channel_id=1, source_target_pairs={{0,8},{8,0},{16,24},{24,16},{32,40},{40,32},{48,56},{56,48},{64,72... | collective-permute-start | bytes 1572872 | tf_op jit(solution)/shard_map/ppermute | solution.py:302
  212.0 1.6 convert_add_fusion
  213.6 1.0 shard_map.108
  (50 shorter events, 4.2 us)
Async XLA Ops:
  0.7 1.2 copy-start
  1.9 0.7 copy-start.2
  2.6 26.5 %copy-start.1 = (bf16[2,16,128,128]{3,2,1,0:T(8,128)(2,1)S(1)}, bf16[2,16,128,128]{3,2,1,0:T(8,128)(2,1)}, u32[]{:S(2)}) copy-start(bf16[2,16,128,128]{3,2,1,0:T(8,128)(2,1)} %ours.3) | copy-start | bytes 3145732
  3.2 10.3 %collective-permute-start = (bf16[2,8,128,128]{3,2,1,0:T(8,128)(2,1)S(1)}, bf16[2,8,128,128]{3,2,1,0:T(8,128)(2,1)S(1)}, u32[]{:S(2)}, u32[]{:S(2)}) collective-permute-start(bf16[2,8,128,128]{3,2,1,0:T(8,128)(2,1)S(1)} %get-tuple-element.22), channel_id=1, source_target_pairs={{0,8},{8,0},{16,24},{24,16},{32,40},{40,32},{48,56},{56,48},{64,72... | collective-permute-start | bytes 1572872 | tf_op jit(solution)/shard_map/ppermute | solution.py:302
  14.1 55.0 %copy-start.11 = (s32[128,128]{1,0:T(8,128)S(1)}, s32[128,128]{1,0:T(8,128)}, u32[]{:S(2)}) copy-start(s32[128,128]{1,0:T(8,128)} %param.11) | copy-start | bytes 196612
  14.1 55.0 %slice-start = ((s32[128,128]{1,0:T(8,128)}), s32[1,128]{1,0:T(1,128)S(1)}, s32[]{:S(2)}) async-start(s32[128,128]{1,0:T(8,128)} %param.11), calls=%async_computation.8 | async-start | bytes 1024 | tf_op jit(solution)/shard_map/jit(_roll_static)/slice | solution.py:336
  14.1 62.4 %copy-start.12 = (s32[128]{0:T(128)S(1)}, s32[128]{0:T(128)}, u32[]{:S(2)}) copy-start(s32[128]{0:T(128)} %constant.100) | copy-start | bytes 1540
  14.2 62.7 %copy-start.13 = (s32[128]{0:T(128)S(1)}, s32[128]{0:T(128)}, u32[]{:S(2)}) copy-start(s32[128]{0:T(128)} %constant.99) | copy-start | bytes 1540
  29.1 48.6 %copy-start.9 = (bf16[4,256,256]{2,1,0:T(8,128)(2,1)S(1)}, bf16[4,256,256]{2,1,0:T(8,128)(2,1)}, u32[]{:S(2)}) copy-start(bf16[4,256,256]{2,1,0:T(8,128)(2,1)} %constant.93.clone.tables) | copy-start | bytes 1572868
  29.1 32.0 %collective-permute-start.1 = (bf16[2,16,128,128]{3,2,1,0:T(8,128)(2,1)S(1)}, bf16[2,16,128,128]{3,2,1,0:T(8,128)(2,1)S(1)}, u32[]{:S(2)}, u32[]{:S(2)}) collective-permute-start(bf16[2,16,128,128]{3,2,1,0:T(8,128)(2,1)S(1)} %copy-done.1), channel_id=1, source_target_pairs={{0,16},{8,24},{16,0},{24,8},{32,48},{40,56},{48,32},{56,40},{64,80... | collective-permute-start | bytes 3145736 | tf_op jit(solution)/shard_map/ppermute | solution.py:302
  61.1 21.2 %copy-start.3 = (bf16[2,16,128,128]{3,2,1,0:T(8,128)(2,1)}, bf16[2,16,128,128]{3,2,1,0:T(8,128)(2,1)S(1)}, u32[]{:S(2)}) copy-start(bf16[2,16,128,128]{3,2,1,0:T(8,128)(2,1)S(1)} %collective-permute-done.1.theirs) | copy-start | bytes 3145732
  69.4 8.3 %collective-permute-start.2 = (bf16[4,2,128,128]{3,2,1,0:T(8,128)(2,1)S(1)}, bf16[4,2,128,128]{3,2,1,0:T(8,128)(2,1)S(1)}, u32[]{:S(2)}, u32[]{:S(2)}) collective-permute-start(bf16[4,2,128,128]{3,2,1,0:T(8,128)(2,1)S(1)} %all_to_all.42.own), channel_id=1, source_target_pairs={{0,8},{8,0},{16,24},{24,16},{32,40},{40,32},{48,56},{56,48},{64,72... | collective-permute-start | bytes 786440 | tf_op jit(solution)/shard_map/ppermute | solution.py:302
  77.7 4.7 %copy-start.6 = (bf16[4,2,128,128]{3,2,1,0:T(8,128)(2,1)}, bf16[4,2,128,128]{3,2,1,0:T(8,128)(2,1)S(1)}, u32[]{:S(2)}) copy-start(bf16[4,2,128,128]{3,2,1,0:T(8,128)(2,1)S(1)} %collective-permute-done.2.other) | copy-start | bytes 786436
  82.4 31.8 %copy-start.8 = (bf16[8,256,256]{2,1,0:T(8,128)(2,1)S(1)}, bf16[8,256,256]{2,1,0:T(8,128)(2,1)}, u32[]{:S(2)}) copy-start(bf16[8,256,256]{2,1,0:T(8,128)(2,1)} %constant.94.clone.tables) | copy-start | bytes 3145732
  118.5 31.6 %copy-start.4 = (bf16[2,16,128,128]{3,2,1,0:T(8,128)(2,1)S(1)}, bf16[2,16,128,128]{3,2,1,0:T(8,128)(2,1)}, u32[]{:S(2)}) copy-start(bf16[2,16,128,128]{3,2,1,0:T(8,128)(2,1)} %copy-done.3) | copy-start | bytes 3145732
  118.5 31.6 %copy-start.7 = (bf16[4,2,128,128]{3,2,1,0:T(8,128)(2,1)S(1)}, bf16[4,2,128,128]{3,2,1,0:T(8,128)(2,1)}, u32[]{:S(2)}) copy-start(bf16[4,2,128,128]{3,2,1,0:T(8,128)(2,1)} %copy-done.6) | copy-start | bytes 786436
  118.5 31.6 %copy-start.10 = (bf16[4,256,256]{2,1,0:T(8,128)(2,1)S(1)}, bf16[4,256,256]{2,1,0:T(8,128)(2,1)}, u32[]{:S(2)}) copy-start(bf16[4,256,256]{2,1,0:T(8,128)(2,1)} %constant.93.clone.tables) | copy-start | bytes 1572868
  152.7 3.9 %copy-start.5 = (bf16[2,16,128,128]{3,2,1,0:T(8,128)(2,1)}, bf16[2,16,128,128]{3,2,1,0:T(8,128)(2,1)S(1)}, u32[]{:S(2)}) copy-start(bf16[2,16,128,128]{3,2,1,0:T(8,128)(2,1)S(1)} %get-tuple-element.36) | copy-start | bytes 3145732
  152.7 3.9 %collective-permute-start.3 = (bf16[4,2,128,128]{3,2,1,0:T(8,128)(2,1)S(1)}, bf16[4,2,128,128]{3,2,1,0:T(8,128)(2,1)S(1)}, u32[]{:S(2)}, u32[]{:S(2)}) collective-permute-start(bf16[4,2,128,128]{3,2,1,0:T(8,128)(2,1)S(1)} %get-tuple-element.35), channel_id=1, source_target_pairs={{0,8},{8,0},{16,24},{24,16},{32,40},{40,32},{48,56},{56,48},{64,72... | collective-permute-start | bytes 786440 | tf_op jit(solution)/shard_map/ppermute | solution.py:302
  165.7 23.9 %collective-permute-start.4 = (bf16[2,16,128,128]{3,2,1,0:T(8,128)(2,1)}, bf16[2,16,128,128]{3,2,1,0:T(8,128)(2,1)S(1)}, u32[]{:S(2)}, u32[]{:S(2)}) collective-permute-start(bf16[2,16,128,128]{3,2,1,0:T(8,128)(2,1)} %copy-done.5), channel_id=1, source_target_pairs={{0,16},{8,24},{16,0},{24,8},{32,48},{40,56},{48,32},{56,40},{64,80... | collective-permute-start | bytes 3145736 | tf_op jit(solution)/shard_map/ppermute | solution.py:302
  207.9 5.7 %collective-permute-start.5 = (bf16[8,2,128,128]{3,2,1,0:T(8,128)(2,1)S(1)}, bf16[8,2,128,128]{3,2,1,0:T(8,128)(2,1)S(1)}, u32[]{:S(2)}, u32[]{:S(2)}) collective-permute-start(bf16[8,2,128,128]{3,2,1,0:T(8,128)(2,1)S(1)} %all_to_all.47.own), channel_id=1, source_target_pairs={{0,8},{8,0},{16,24},{24,16},{32,40},{40,32},{48,56},{56,48},{64,72... | collective-permute-start | bytes 1572872 | tf_op jit(solution)/shard_map/ppermute | solution.py:302

commit v9 on v8

--- a/solution.py
+++ b/solution.py
@@ -42,7 +42,8 @@
     for z in range(4)
     for xl in range(2)
 ]
-SLABS = [[band * 8 + (7 - g if band % 2 else g) for g in range(8)] for band in range(64)]
+MASKS = (0, 7, 4, 3)
+SLABS = [[band * 8 + (g ^ MASKS[band % 4]) for g in range(8)] for band in range(64)]
 LINE = [group[xl::2] for group in NEAR for xl in range(2)]
 VMEM = pl.BlockSpec(memory_space=pltpu.VMEM)
 SMEM = pl.BlockSpec(memory_space=pltpu.SMEM)
@@ -57,9 +58,11 @@
     high = matrix.astype(BF16)
     low = (matrix - high.astype(np.float32)).astype(BF16)
     plain = np.stack([high, low, high.T, low.T])
-    order = np.arange(2 * GRID).reshape(2, GRID // ROWS, ROWS)[:, ::-1].reshape(-1)
-    turned = np.stack([high[order], low[order], high.T[:, order], low.T[:, order]])
-    return plain, np.concatenate([plain, turned])
+    kinds = []
+    for mask in MASKS:
+        order = np.arange(2 * GRID).reshape(2, 8, ROWS)[:, np.arange(8) ^ mask].reshape(-1)
+        kinds += [high[order], low[order], high.T[:, order], low.T[:, order]]
+    return plain, np.stack(kinds)
 
 
 def dot(a, b):
@@ -145,9 +148,9 @@
     lax.fori_loop(0, n // ROWS, send, 0)
 
 
-def solve_kernel(core, spectrum, coulomb, tables, out, scratch):
+def solve_kernel(kind, spectrum, coulomb, tables, out, scratch):
     n = GRID
-    first = core[0] * 4
+    first = kind[0] * 4
     rest = spectrum[:, CHUNK:].reshape(n, n).astype(F32)
     lane = lax.broadcasted_iota(jnp.int32, (n, n), 1)
     dropped = coulomb[0, :1, :1] == 0.0
@@ -347,7 +350,9 @@
 
 def shards(orbitals, owners, cutoff):
     slab = lax.axis_index("ga")
-    first_row = (jnp.where(lax.axis_index("band") % 2 == 1, 7 - slab, slab) * ROWS).astype(jnp.int32)
+    kind = lax.axis_index("band") % 4
+    mask = jnp.where(kind % 2 == 1, 7, 0) ^ jnp.where(kind >= 2, 4, 0)
+    first_row = ((slab ^ mask) * ROWS).astype(jnp.int32)
     tables, both_tables = (jnp.asarray(table) for table in dft_tables())
     band = lax.axis_index("band")
     core = (band % 2).astype(jnp.int32).reshape(1)
@@ -374,7 +379,7 @@
             [pltpu.VMEM((ROWS * PAIR, GRID), F32)],
             flops,
             operands=3,
-        )(core, spectrum, coulomb, both_tables)
+        )(kind.astype(jnp.int32).reshape(1), spectrum, coulomb, both_tables)
     solved = exchange_slabs(solved)
     slab = (2, ROWS, GRID, GRID)
     half = (HALF // 2, 2, GRID, GRID)

time: 215 us -> 216 us (level)
  no operation moved by 1% of the time
where the time goes in v9:
time: 216 us; the launch traced here: 215 us
  blocking collectives  162 us (75%)
  starting transfers between devices  28.8 us (13%)
  Pallas kernels  15.1 us (7%)
  waiting for transfers between devices  3.87 us (2%)
  other arithmetic  2.63 us (1%)
  local copies, waits for them, and re-layouts  2.34 us (1%)
    all_to_all x6, blocking collectives, exchange_all(): return lax.all_to_all(x, 'band', 0, 0, axis_index_groups=groups, tiled=True)  98.3 us
    all_to_all x2, blocking collectives, exchange_slabs(): lax.all_to_all(x, ('band', 'ga'), 0, 0, axis_index_groups=SLABS, tiled=True)  63.3 us
    ppermute x6, starting transfers between devices, swap(): return lax.ppermute(x, 'band', [(i, i ^ bit) for i in range(64)])  28.8 us
    pallas_call x1, Pallas kernels, shards(): call(forward_kernel, jax.ShapeDtypeStruct((8, CHUNK + ROWS, GRID), BF16),...  4.66 us
  transfers between devices with their start and end apart: 6, of which 4 were waited for; matrix products, arithmetic and copies ran while one was open for 1% of the time, Pallas kernels for 0%

profile of v9, /device:TPU:1, one launch (start us, length us, event | category | flops | bytes accessed | tf_op | source)
XLA Modules:
  0.0 215.3 jit_solution(3472022289575292085)
XLA Ops:
  0.7 1.2 copy-done
  2.0 0.7 copy-done.2
  3.2 8.8 %collective-permute-start = (bf16[2,8,128,128]{3,2,1,0:T(8,128)(2,1)S(1)}, bf16[2,8,128,128]{3,2,1,0:T(8,128)(2,1)S(1)}, u32[]{:S(2)}, u32[]{:S(2)}) collective-permute-start(bf16[2,8,128,128]{3,2,1,0:T(8,128)(2,1)S(1)} %get-tuple-element.22), channel_id=1, source_target_pairs={{0,8},{8,0},{16,24},{24,16},{32,40},{40,32},{48,56},{56,48},{64,72... | collective-permute-start | bytes 1572872 | tf_op jit(solution)/shard_map/ppermute | solution.py:305
  12.0 1.5 collective-permute-done.received
  14.2 14.9 %all_to_all.40.pieces = bf16[8,2,128,128]{3,2,1,0:T(8,128)(2,1)S(1)} all-to-all(bf16[8,2,128,128]{3,2,1,0:T(8,128)(2,1)S(1)} %shard_map.105), channel_id=1, replica_groups={{0,16,32,48,64,80,96,112},{128,144,160,176,192,208,224,240},{256,272,28..., dimensions={0} | all-to-all | bytes 1048576 | tf_op jit(solution)/shard_map/all_to_all | solution.py:293
  29.1 3.4 %collective-permute-start.1 = (bf16[2,16,128,128]{3,2,1,0:T(8,128)(2,1)S(1)}, bf16[2,16,128,128]{3,2,1,0:T(8,128)(2,1)S(1)}, u32[]{:S(2)}, u32[]{:S(2)}) collective-permute-start(bf16[2,16,128,128]{3,2,1,0:T(8,128)(2,1)S(1)} %copy-done.1), channel_id=1, source_target_pairs={{0,16},{8,24},{16,0},{24,8},{32,48},{40,56},{48,32},{56,40},{64,80... | collective-permute-start | bytes 3145736 | tf_op jit(solution)/shard_map/ppermute | solution.py:305
  33.1 28.0 %all_to_all.41.pieces = bf16[4,2,128,128]{3,2,1,0:T(8,128)(2,1)S(1)} all-to-all(bf16[4,2,128,128]{3,2,1,0:T(8,128)(2,1)S(1)} %shard_map.106), channel_id=1, replica_groups={{0,128,384,256},{16,144,400,272},{32,160,416,288},{48,176,432,304},{64,..., dimensions={0} | all-to-all | bytes 524288 | tf_op jit(solution)/shard_map/all_to_all | solution.py:293
  61.8 7.3 %all_to_all.42.own = bf16[4,2,128,128]{3,2,1,0:T(8,128)(2,1)S(1)} all-to-all(bf16[4,2,128,128]{3,2,1,0:T(8,128)(2,1)S(1)} %shard_map.107), channel_id=1, replica_groups={{0,32,64,96},{16,48,80,112},{128,160,192,224},{144,176,208,240},{256,28..., dimensions={0} | all-to-all | bytes 524288 | tf_op jit(solution)/shard_map/all_to_all | solution.py:293
  69.5 7.1 %collective-permute-start.2 = (bf16[4,2,128,128]{3,2,1,0:T(8,128)(2,1)S(1)}, bf16[4,2,128,128]{3,2,1,0:T(8,128)(2,1)S(1)}, u32[]{:S(2)}, u32[]{:S(2)}) collective-permute-start(bf16[4,2,128,128]{3,2,1,0:T(8,128)(2,1)S(1)} %all_to_all.42.own), channel_id=1, source_target_pairs={{0,8},{8,0},{16,24},{24,16},{32,40},{40,32},{48,56},{56,48},{64,72... | collective-permute-start | bytes 786440 | tf_op jit(solution)/shard_map/ppermute | solution.py:305
  77.7 4.7 %forward_planes.1 = bf16[8,1040,128]{2,1,0:T(8,128)(2,1)S(1)} custom-call(s32[1]{0:T(128)} %bitcast.core, bf16[2,16,128,128]{3,2,1,0:T(8,128)(2,1)S(1)} %copy-done.1, bf16[2,16,128,128]{3,2,1,0:T(8,128)(2,1)S(1)} %collective-permute-done.1.theirs, bf16[4,2,128,128]{3,2,1,0:T(8,128)(2,1)S(1)} %all_to_all.42.own, ...), custom_call_target="tpu_custom_call" | custom-call | flops 3221225472 | bytes 5242880 | tf_op jit(solution)/shard_map/forward_planes/pallas_call | solution.py:367
  82.4 31.8 %all_to_all.43.spectrum = bf16[8,1040,128]{2,1,0:T(8,128)(2,1)S(1)} all-to-all(bf16[8,1040,128]{2,1,0:T(8,128)(2,1)S(1)} %forward_planes.1), channel_id=1, replica_groups={{0,1,2,3,4,5,6,7},{15,14,13,12,11,10,9,8},{20,21,22,23,16,17,18,19},{27..., dimensions={0} | all-to-all | bytes 4259840 | tf_op jit(solution)/shard_map/all_to_all | solution.py:301
  114.2 4.3 %coulomb_solve.1 = bf16[8,2,16,2,16,128]{5,4,3,2,1,0:T(8,128)(2,1)S(1)} custom-call(s32[1]{0:T(128)} %bitcast.1.kind, bf16[8,1040,128]{2,1,0:T(8,128)(2,1)S(1)} %all_to_all.43.spectrum, f32[16,128,128]{2,1,0:T(8,128)S(1)} %fusion.2.coulomb, bf16[16,256,256]{2,1,0:T(8,128)(2,1)S(1)} %copy-done.8), custom_call_target="tpu_custom_call" | custom-call | flops 3221225472 | bytes 5242880 | tf_op jit(solution)/shard_map/coulomb_solve/pallas_call | solution.py:376
  118.6 31.5 %all_to_all.44.solved = bf16[8,2,16,2,16,128]{5,4,3,2,1,0:T(8,128)(2,1)S(1)} all-to-all(bf16[8,2,16,2,16,128]{5,4,3,2,1,0:T(8,128)(2,1)S(1)} %coulomb_solve.1), channel_id=1, replica_groups={{0,1,2,3,4,5,6,7},{15,14,13,12,11,10,9,8},{20,21,22,23,16,17,18,19},{27..., dimensions={0} | all-to-all | bytes 4194304 | tf_op jit(solution)/shard_map/all_to_all | solution.py:301
  150.1 2.7 %backward_planes.1 = (f32[2,16,128,128]{3,2,1,0:T(8,128)S(1)}, bf16[2,16,128,128]{3,2,1,0:T(8,128)(2,1)S(1)}, f32[4,2,128,128]{3,2,1,0:T(8,128)S(1)}, bf16[4,2,128,128]{3,2,1,0:T(8,128)(2,1)S(1)}) custom-call(s32[1]{0:T(128)} %bitcast.core, bf16[8,2,16,2,16,128]{5,4,3,2,1,0:T(8,128)(2,1)S(1)} %all_to_all.44.solved, bf16[2,16,128,128]{3,2,1,0:T(8,128)(2,1)S(1)} %copy-done.1, ...), custom_call_target="tpu_custom_call" | custom-call | flops 3221225472 | bytes 5242880 | tf_op jit(solution)/shard_map/backward_planes/pallas_call | solution.py:387
  152.8 2.7 %collective-permute-start.3 = (bf16[4,2,128,128]{3,2,1,0:T(8,128)(2,1)S(1)}, bf16[4,2,128,128]{3,2,1,0:T(8,128)(2,1)S(1)}, u32[]{:S(2)}, u32[]{:S(2)}) collective-permute-start(bf16[4,2,128,128]{3,2,1,0:T(8,128)(2,1)S(1)} %get-tuple-element.35), channel_id=1, source_target_pairs={{0,8},{8,0},{16,24},{24,16},{32,40},{40,32},{48,56},{56,48},{64,72... | collective-permute-start | bytes 786440 | tf_op jit(solution)/shard_map/ppermute | solution.py:305
  155.5 1.1 collective-permute-done.3
  156.7 9.0 %all_to_all.45 = bf16[4,2,128,128]{3,2,1,0:T(8,128)(2,1)S(1)} all-to-all(bf16[4,2,128,128]{3,2,1,0:T(8,128)(2,1)S(1)} %add_convert_fusion), channel_id=1, replica_groups={{0,32,64,96},{16,48,80,112},{128,160,192,224},{144,176,208,240},{256,28..., dimensions={0} | all-to-all | bytes 524288 | tf_op jit(solution)/shard_map/all_to_all | solution.py:293
  165.7 2.6 %collective-permute-start.4 = (bf16[2,16,128,128]{3,2,1,0:T(8,128)(2,1)}, bf16[2,16,128,128]{3,2,1,0:T(8,128)(2,1)S(1)}, u32[]{:S(2)}, u32[]{:S(2)}) collective-permute-start(bf16[2,16,128,128]{3,2,1,0:T(8,128)(2,1)} %copy-done.5), channel_id=1, source_target_pairs={{0,16},{8,24},{16,0},{24,8},{32,48},{40,56},{48,32},{56,40},{64,80... | collective-permute-start | bytes 3145736 | tf_op jit(solution)/shard_map/ppermute | solution.py:305
  168.4 20.2 %all_to_all.46 = bf16[4,2,128,128]{3,2,1,0:T(8,128)(2,1)S(1)} all-to-all(bf16[4,2,128,128]{3,2,1,0:T(8,128)(2,1)S(1)} %broadcast_in_dim.9), channel_id=1, replica_groups={{0,128,384,256},{16,144,400,272},{32,160,416,288},{48,176,432,304},{64,..., dimensions={0} | all-to-all | bytes 524288 | tf_op jit(solution)/shard_map/all_to_all | solution.py:293
  188.7 1.0 collective-permute-done.4
  189.7 18.8 %all_to_all.47.own = bf16[8,2,128,128]{3,2,1,0:T(8,128)(2,1)S(1)} all-to-all(bf16[8,2,128,128]{3,2,1,0:T(8,128)(2,1)S(1)} %broadcast_in_dim.10), channel_id=1, replica_groups={{0,16,32,48,64,80,96,112},{128,144,160,176,192,208,224,240},{256,272,28..., dimensions={0} | all-to-all | bytes 1048576 | tf_op jit(solution)/shard_map/all_to_all | solution.py:293
  208.5 4.2 %collective-permute-start.5 = (bf16[8,2,128,128]{3,2,1,0:T(8,128)(2,1)S(1)}, bf16[8,2,128,128]{3,2,1,0:T(8,128)(2,1)S(1)}, u32[]{:S(2)}, u32[]{:S(2)}) collective-permute-start(bf16[8,2,128,128]{3,2,1,0:T(8,128)(2,1)S(1)} %all_to_all.47.own), channel_id=1, source_target_pairs={{0,8},{8,0},{16,24},{24,16},{32,40},{40,32},{48,56},{56,48},{64,72... | collective-permute-start | bytes 1572872 | tf_op jit(solution)/shard_map/ppermute | solution.py:305
  212.7 1.6 convert_add_fusion
  214.2 1.0 shard_map.108
  (50 shorter events, 4.2 us)
Async XLA Ops:
  0.7 1.2 copy-start
  2.0 0.7 copy-start.2
  2.6 26.5 %copy-start.1 = (bf16[2,16,128,128]{3,2,1,0:T(8,128)(2,1)S(1)}, bf16[2,16,128,128]{3,2,1,0:T(8,128)(2,1)}, u32[]{:S(2)}) copy-start(bf16[2,16,128,128]{3,2,1,0:T(8,128)(2,1)} %ours.3) | copy-start | bytes 3145732
  3.2 10.3 %collective-permute-start = (bf16[2,8,128,128]{3,2,1,0:T(8,128)(2,1)S(1)}, bf16[2,8,128,128]{3,2,1,0:T(8,128)(2,1)S(1)}, u32[]{:S(2)}, u32[]{:S(2)}) collective-permute-start(bf16[2,8,128,128]{3,2,1,0:T(8,128)(2,1)S(1)} %get-tuple-element.22), channel_id=1, source_target_pairs={{0,8},{8,0},{16,24},{24,16},{32,40},{40,32},{48,56},{56,48},{64,72... | collective-permute-start | bytes 1572872 | tf_op jit(solution)/shard_map/ppermute | solution.py:305
  14.2 55.0 %copy-start.11 = (s32[128,128]{1,0:T(8,128)S(1)}, s32[128,128]{1,0:T(8,128)}, u32[]{:S(2)}) copy-start(s32[128,128]{1,0:T(8,128)} %param.11) | copy-start | bytes 196612
  14.2 55.0 %slice-start = ((s32[128,128]{1,0:T(8,128)}), s32[1,128]{1,0:T(1,128)S(1)}, s32[]{:S(2)}) async-start(s32[128,128]{1,0:T(8,128)} %param.11), calls=%async_computation.8 | async-start | bytes 1024 | tf_op jit(solution)/shard_map/jit(_roll_static)/slice | solution.py:339
  14.2 62.4 %copy-start.12 = (s32[128]{0:T(128)S(1)}, s32[128]{0:T(128)}, u32[]{:S(2)}) copy-start(s32[128]{0:T(128)} %constant.106) | copy-start | bytes 1540
  14.2 62.7 %copy-start.13 = (s32[128]{0:T(128)S(1)}, s32[128]{0:T(128)}, u32[]{:S(2)}) copy-start(s32[128]{0:T(128)} %constant.105) | copy-start | bytes 1540
  29.1 48.6 %copy-start.9 = (bf16[4,256,256]{2,1,0:T(8,128)(2,1)S(1)}, bf16[4,256,256]{2,1,0:T(8,128)(2,1)}, u32[]{:S(2)}) copy-start(bf16[4,256,256]{2,1,0:T(8,128)(2,1)} %constant.99.clone.tables) | copy-start | bytes 1572868
  29.1 32.0 %collective-permute-start.1 = (bf16[2,16,128,128]{3,2,1,0:T(8,128)(2,1)S(1)}, bf16[2,16,128,128]{3,2,1,0:T(8,128)(2,1)S(1)}, u32[]{:S(2)}, u32[]{:S(2)}) collective-permute-start(bf16[2,16,128,128]{3,2,1,0:T(8,128)(2,1)S(1)} %copy-done.1), channel_id=1, source_target_pairs={{0,16},{8,24},{16,0},{24,8},{32,48},{40,56},{48,32},{56,40},{64,80... | collective-permute-start | bytes 3145736 | tf_op jit(solution)/shard_map/ppermute | solution.py:305
  61.2 21.2 %copy-start.3 = (bf16[2,16,128,128]{3,2,1,0:T(8,128)(2,1)}, bf16[2,16,128,128]{3,2,1,0:T(8,128)(2,1)S(1)}, u32[]{:S(2)}) copy-start(bf16[2,16,128,128]{3,2,1,0:T(8,128)(2,1)S(1)} %collective-permute-done.1.theirs) | copy-start | bytes 3145732
  69.5 8.3 %collective-permute-start.2 = (bf16[4,2,128,128]{3,2,1,0:T(8,128)(2,1)S(1)}, bf16[4,2,128,128]{3,2,1,0:T(8,128)(2,1)S(1)}, u32[]{:S(2)}, u32[]{:S(2)}) collective-permute-start(bf16[4,2,128,128]{3,2,1,0:T(8,128)(2,1)S(1)} %all_to_all.42.own), channel_id=1, source_target_pairs={{0,8},{8,0},{16,24},{24,16},{32,40},{40,32},{48,56},{56,48},{64,72... | collective-permute-start | bytes 786440 | tf_op jit(solution)/shard_map/ppermute | solution.py:305
  77.7 4.7 %copy-start.6 = (bf16[4,2,128,128]{3,2,1,0:T(8,128)(2,1)}, bf16[4,2,128,128]{3,2,1,0:T(8,128)(2,1)S(1)}, u32[]{:S(2)}) copy-start(bf16[4,2,128,128]{3,2,1,0:T(8,128)(2,1)S(1)} %collective-permute-done.2.other) | copy-start | bytes 786436
  82.4 31.8 %copy-start.8 = (bf16[16,256,256]{2,1,0:T(8,128)(2,1)S(1)}, bf16[16,256,256]{2,1,0:T(8,128)(2,1)}, u32[]{:S(2)}) copy-start(bf16[16,256,256]{2,1,0:T(8,128)(2,1)} %constant.100.clone.tables) | copy-start | bytes 6291460
  118.5 31.6 %copy-start.4 = (bf16[2,16,128,128]{3,2,1,0:T(8,128)(2,1)S(1)}, bf16[2,16,128,128]{3,2,1,0:T(8,128)(2,1)}, u32[]{:S(2)}) copy-start(bf16[2,16,128,128]{3,2,1,0:T(8,128)(2,1)} %copy-done.3) | copy-start | bytes 3145732
  118.5 31.6 %copy-start.7 = (bf16[4,2,128,128]{3,2,1,0:T(8,128)(2,1)S(1)}, bf16[4,2,128,128]{3,2,1,0:T(8,128)(2,1)}, u32[]{:S(2)}) copy-start(bf16[4,2,128,128]{3,2,1,0:T(8,128)(2,1)} %copy-done.6) | copy-start | bytes 786436
  118.6 31.5 %copy-start.10 = (bf16[4,256,256]{2,1,0:T(8,128)(2,1)S(1)}, bf16[4,256,256]{2,1,0:T(8,128)(2,1)}, u32[]{:S(2)}) copy-start(bf16[4,256,256]{2,1,0:T(8,128)(2,1)} %constant.99.clone.tables) | copy-start | bytes 1572868
  152.8 3.9 %copy-start.5 = (bf16[2,16,128,128]{3,2,1,0:T(8,128)(2,1)}, bf16[2,16,128,128]{3,2,1,0:T(8,128)(2,1)S(1)}, u32[]{:S(2)}) copy-start(bf16[2,16,128,128]{3,2,1,0:T(8,128)(2,1)S(1)} %get-tuple-element.36) | copy-start | bytes 3145732
  152.8 3.9 %collective-permute-start.3 = (bf16[4,2,128,128]{3,2,1,0:T(8,128)(2,1)S(1)}, bf16[4,2,128,128]{3,2,1,0:T(8,128)(2,1)S(1)}, u32[]{:S(2)}, u32[]{:S(2)}) collective-permute-start(bf16[4,2,128,128]{3,2,1,0:T(8,128)(2,1)S(1)} %get-tuple-element.35), channel_id=1, source_target_pairs={{0,8},{8,0},{16,24},{24,16},{32,40},{40,32},{48,56},{56,48},{64,72... | collective-permute-start | bytes 786440 | tf_op jit(solution)/shard_map/ppermute | solution.py:305
  165.7 23.9 %collective-permute-start.4 = (bf16[2,16,128,128]{3,2,1,0:T(8,128)(2,1)}, bf16[2,16,128,128]{3,2,1,0:T(8,128)(2,1)S(1)}, u32[]{:S(2)}, u32[]{:S(2)}) collective-permute-start(bf16[2,16,128,128]{3,2,1,0:T(8,128)(2,1)} %copy-done.5), channel_id=1, source_target_pairs={{0,16},{8,24},{16,0},{24,8},{32,48},{40,56},{48,32},{56,40},{64,80... | collective-permute-start | bytes 3145736 | tf_op jit(solution)/shard_map/ppermute | solution.py:305
  208.5 5.7 %collective-permute-start.5 = (bf16[8,2,128,128]{3,2,1,0:T(8,128)(2,1)S(1)}, bf16[8,2,128,128]{3,2,1,0:T(8,128)(2,1)S(1)}, u32[]{:S(2)}, u32[]{:S(2)}) collective-permute-start(bf16[8,2,128,128]{3,2,1,0:T(8,128)(2,1)S(1)} %all_to_all.47.own), channel_id=1, source_target_pairs={{0,8},{8,0},{16,24},{24,16},{32,40},{40,32},{48,56},{56,48},{64,72... | collective-permute-start | bytes 1572872 | tf_op jit(solution)/shard_map/ppermute | solution.py:305
